TPU v7x, 256 devices: a whole 4x4x8 slice. The times are simulated.
256 devices in a mesh: slab: 16 (over x, z_lo, core), chan: 16 (over y, z_hi).
Axes of the slice: x: 4, y: 4, z: 8 (z_hi: 4, z_lo: 2; z = z_hi * 2 + z_lo), core: 2. Of those that a mesh axis runs over, the one named last changes fastest.
Arguments:
- features: bfloat16 [64, 64, 32, 128], P('chan', 'slab'), may hold values from -6 to 6
- pre_act: bfloat16 [128, 64, 32, 128], P('chan', 'slab'), may hold values from -6 to 6
- out_grad: bfloat16 [128, 64, 32, 128], P('chan', 'slab'), may hold values from -6 to 6
- weight_one: bfloat16 [27, 64, 128], replicated, may hold values from -0.15625 to 0.15625
- weight_two: bfloat16 [27, 128, 128], replicated, may hold values from -0.109375 to 0.109375
- dropout_seed: int32 [1], replicated, may hold values from 0 to 1073741823
- layer_offset: int32 [1], replicated, may hold values from 0 to 16777215
Outputs:
- feature_grad: float32 [64, 64, 32, 128], P('chan', 'slab')
- weight_one_grad: float32 [64, 3456], P('chan')
- weight_two_grad: float32 [128, 3456], P('chan')
All inputs are finite; a program needn't handle non-finite values.
Results may differ from a plain program's by a relative error of at most 0.003.
Values may be sent and summed in bfloat16 or wider, within the bound.
No kernel may reach another device: no remote copies, remote signals or barrier semaphores. Data moves between devices by JAX's collectives and lax.ppermute only.
A program may use at most 128 MiB of HBM per device.

v0:
```python
import math

import jax
import jax.numpy as jnp
from jax import lax
from jax.sharding import PartitionSpec as P


def extended(cells, sides, width):
    for axis, dim in sides:
        count = lax.axis_size(axis)
        ends = count - 1
        head = lax.slice_in_dim(cells, 0, width, axis=dim)
        tail = lax.slice_in_dim(cells, cells.shape[dim] - width, cells.shape[dim], axis=dim)
        cells = jnp.concatenate(
            [
                lax.ppermute(tail, axis, [(i, (i + 1) % count) for i in range(ends)]),
                cells,
                lax.ppermute(head, axis, [((i + 1) % count, i) for i in range(ends)]),
            ],
            axis=dim,
        )
    return cells


def keep_factor(
    dropout_seed, layer_offset, chan_ids, depth_ids, row_ids, col_total, depth_total, row_total
):
    col_ids = jnp.arange(col_total, dtype=jnp.int32)
    position = (
        (chan_ids[:, None, None, None] * depth_total + depth_ids[None, :, None, None]) * row_total
        + row_ids[None, None, :, None]
    ) * col_total + col_ids[None, None, None, :]
    hashed = position + layer_offset[0] ^ dropout_seed[0]
    hashed = hashed * 739982445
    hashed = hashed ^ lax.shift_right_logical(hashed, jnp.int32(15))
    hashed = hashed * 695938361
    hashed = hashed ^ lax.shift_right_logical(hashed, jnp.int32(12))
    kept = hashed & 65535 < 52429
    return jnp.where(kept, 1.25, 0.0).astype(jnp.float32)


def tap_columns(source, depth_len, row_len, col_len):
    pieces = []
    for depth_tap in range(3):
        for row_tap in range(3):
            for col_tap in range(3):
                pieces.append(
                    source[
                        :,
                        2 - depth_tap : 2 - depth_tap + depth_len,
                        2 - row_tap : 2 - row_tap + row_len,
                        2 - col_tap : 2 - col_tap + col_len,
                    ]
                )
    stacked = jnp.stack(pieces, axis=0)
    return stacked.reshape(27 * source.shape[0], depth_len * row_len * col_len)


def tap_lhs(weight):
    return weight.transpose(1, 2, 0).reshape(weight.shape[1], 27 * weight.shape[0])


def weight_grad(columns, activation, group_n):
    product = lax.dot_general(
        columns,
        activation.reshape(activation.shape[0], -1),
        (((1,), (1,)), ((), ())),
        preferred_element_type=jnp.float32,
    )
    return product.reshape(27, group_n, activation.shape[0]).transpose(1, 2, 0)


def shards(features, pre_act, out_grad, weight_one, weight_two, dropout_seed, layer_offset):
    filters_one = weight_one.transpose(2, 1, 0)
    filters_two = weight_two.transpose(2, 1, 0)
    slab_count = lax.axis_size("slab")
    chan_pos = lax.axis_index("chan")
    slab_pos = lax.axis_index("slab")
    planes = pre_act.shape[1]
    widths = pre_act.shape[3]
    depth_total = planes * slab_count
    mid_total = filters_two.shape[1]
    in_total = filters_one.shape[1]
    depth_ids = slab_pos * planes - 1 + jnp.arange(planes + 2, dtype=jnp.int32)
    row_total = pre_act.shape[2]
    mid_local = pre_act.shape[0]
    out_local = out_grad.shape[0]
    in_local = features.shape[0]
    merged = jnp.concatenate([pre_act, out_grad, features], axis=0)
    with_edges = extended(merged, (("slab", 1),), 2)
    pre_ext = with_edges[:mid_local, 1 : planes + 3]
    grad_ext = with_edges[mid_local : mid_local + out_local]
    feat_ext = with_edges[mid_local + out_local :, 1 : planes + 3]
    chan_ids = chan_pos * mid_local + jnp.arange(mid_local, dtype=jnp.int32)
    kept_scale = keep_factor(
        dropout_seed,
        layer_offset,
        chan_ids,
        depth_ids,
        jnp.arange(row_total, dtype=jnp.int32),
        widths,
        depth_total,
        row_total,
    )
    hidden_ext = (jnp.maximum(pre_ext.astype(jnp.float32), 0.0) * kept_scale).astype(jnp.bfloat16)
    hidden_all, feat_all = (
        lax.all_gather(hidden_ext, "chan", axis=0, tiled=True),
        lax.all_gather(feat_ext, "chan", axis=0, tiled=True),
    )
    two_local = lax.dynamic_slice_in_dim(filters_two, chan_pos * out_local, out_local, 0)
    one_local = lax.dynamic_slice_in_dim(filters_one, chan_pos * mid_local, mid_local, 0)
    grad_zero = jnp.pad(grad_ext[:, 2 : planes + 2], ((0, 0), (2, 2), (1, 1), (1, 1)))
    two_grad = weight_grad(
        tap_columns(grad_zero, planes + 2, row_total, widths), hidden_all, out_local
    )
    grad_cols = tap_columns(
        jnp.pad(grad_ext, ((0, 0), (0, 0), (1, 1), (1, 1))), planes + 2, row_total, widths
    )
    two_lhs = tap_lhs(two_local)
    hidden_grad = lax.psum_scatter(
        jnp.dot(two_lhs, grad_cols, preferred_element_type=jnp.float32),
        "chan",
        scatter_dimension=0,
        tiled=True,
    ).reshape(mid_local, planes + 2, row_total, widths)
    pre_grad = jnp.where(pre_ext > 0, hidden_grad * kept_scale, 0.0).astype(jnp.bfloat16)
    own_zero = jnp.pad(pre_grad[:, 1 : planes + 1], ((0, 0), (2, 2), (1, 1), (1, 1)))
    one_grad = weight_grad(
        tap_columns(own_zero, planes + 2, row_total, widths), feat_all, mid_local
    )
    pre_cols = tap_columns(
        jnp.pad(pre_grad, ((0, 0), (0, 0), (1, 1), (1, 1))), planes, row_total, widths
    )
    one_lhs = tap_lhs(one_local)
    feature_grad = lax.psum_scatter(
        jnp.dot(one_lhs, pre_cols, preferred_element_type=jnp.float32),
        "chan",
        scatter_dimension=0,
        tiled=True,
    ).reshape(in_local, planes, row_total, widths)
    two_sum, one_sum = lax.psum((two_grad, one_grad), "slab")
    grad_scale = 1.0 / math.sqrt(depth_total * row_total * widths)
    one_out = (one_sum * grad_scale).reshape(one_sum.shape[0] // 2, 54 * in_total)
    two_out = (two_sum * grad_scale).reshape(two_sum.shape[0], 27 * mid_total)
    return (feature_grad, one_out, two_out)


def solution(mesh):
    placed = (
        P("chan", "slab", None, None),
        P("chan", "slab", None, None),
        P("chan", "slab", None, None),
        P(),
        P(),
        P(),
        P(),
    )
    return jax.shard_map(
        shards,
        mesh=mesh,
        in_specs=placed,
        out_specs=(P("chan", "slab", None, None), P("chan", None), P("chan", None)),
        check_vma=False,
    )
```

profile of v0, /device:TPU:1, one launch (start us, length us, event | category | flops | bytes accessed | tf_op | source)
XLA Modules:
  0.0 727.5 jit_solution(10303621724309860698)
XLA Ops:
  7.2 1.2 copy_dynamic-update-slice_fusion
  8.4 1.2 fusion.232
  9.6 1.1 constant_dynamic-update-slice_fusion
  10.7 1.0 fusion.231
  11.6 4.9 collective-permute-start
  16.6 1.9 collective-permute-start.1
  18.5 0.3 constant_dynamic-slice_fusion
  18.9 0.3 copy.90
  19.1 2.5 collective-permute-done
  21.6 0.7 copy-done.3
  22.3 4.7 collective-permute-done.1
  27.0 1.3 pad_maximum_fusion
  28.7 0.2 fusion.21
  29.0 0.2 fusion.23
  29.2 1.0 fusion.176
  30.2 0.2 fusion.25
  30.5 0.2 fusion.27
  30.8 0.2 fusion.31
  31.0 0.3 fusion.33
  31.3 0.2 fusion.37
  31.6 0.2 fusion.39
  32.0 0.2 fusion.41
  32.2 0.2 fusion.43
  32.5 0.2 fusion.47
  32.8 0.3 fusion.49
  33.1 0.2 fusion.53
  33.4 0.2 fusion.55
  33.7 0.2 fusion.57
  34.0 0.2 fusion.59
  34.3 0.2 fusion.63
  34.6 6.9 fusion.227
  41.6 0.9 copy-done.5
  42.5 0.9 pad_maximum_fusion.3
  43.4 0.7 copy.53
  45.6 158.5 %reduce-scatter.2.cloned.1.call-done = f32[8,24576]{1,0:T(8,128)} async-done(((f32[128,24576]{1,0:T(8,128)}), f32[8,24576]{1,0:T(8,128)}) %reduce-scatter.2.cloned.1.call-update) | async-done | bytes 786448 | tf_op jit(solution)/shard_map/reduce_scatter | solution.py:121
  204.1 2.5 fusion.12
  206.5 0.2 all-reduce.10.cloned.1.call-start
  206.8 1.2 dynamic-slice_bitcast_fusion
  208.2 0.6 dynamic-slice.8
  209.8 0.2 fusion.125
  211.3 0.2 fusion.143
  212.7 0.2 fusion.161
  217.3 0.4 copy-done.6
  218.3 0.2 fusion.71
  218.6 0.2 fusion.75
  219.8 0.2 fusion.89
  220.0 0.2 fusion.93
  221.2 0.2 fusion.107
  222.2 3.9 copy-done.2
  226.1 3.9 fusion.229
  230.0 0.3 all-reduce.8.cloned.1.call-start
  230.3 42.9 %all-gather.3.cloned.1.call-done = bf16[64,6,32,128]{3,2,1,0:T(8,128)(2,1)} async-done(((bf16[4,6,32,128]{3,2,1,0:T(8,128)(2,1)}), bf16[64,6,32,128]{3,2,1,0:T(8,128)(2,1)}) %all-gather.3.cloned.1.call-update) | async-done | bytes 3145744 | tf_op jit(solution)/shard_map/all_gather | solution.py:109
  273.2 8.6 %fusion.4 = f32[8,64,27]{1,0,2:T(8,128)S(1)} fusion(bf16[27,8,6,32,128]{4,1,3,0,2:T(8,128)(2,1)} %copy-done.2, bf16[64,6,32,128,1]{3,2,1,0,4:T(8,128)(2,1)} %bitcast.582), kind=kOutput, calls=%fused_computation.109 | convolution fusion | flops 679477248 | bytes 13817856 | tf_op jit(solution)/shard_map/dot_general | solution.py:65
  281.8 55.8 %psum.14 = f32[8,64,27]{1,0,2:T(8,128)S(1)} all-reduce(f32[8,64,27]{1,0,2:T(8,128)S(1)} %fusion.4), channel_id=1, replica_groups=mesh['slab'=16,'chan'=16] {'slab'}, use_global_device_ids=true, to_apply=%region_2.3 | all-reduce | flops 13824 | bytes 110592 | tf_op jit(solution)/shard_map/psum | solution.py:142
  337.7 0.8 reshape.99
  338.6 42.0 %all-gather.5.cloned.1.call-done = bf16[128,6,32,128]{3,0,2,1:T(8,128)(2,1)} async-done(((bf16[8,6,32,128]{3,0,2,1:T(8,128)(2,1)}), bf16[128,6,32,128]{3,0,2,1:T(8,128)(2,1)}) %all-gather.5.cloned.1.call-update) | async-done | bytes 6291472 | tf_op jit(solution)/shard_map/all_gather | solution.py:108
  380.6 9.5 %fusion.7 = f32[8,128,27]{1,0,2:T(8,128)} fusion(bf16[27,8,6,32,128]{4,1,3,0,2:T(8,128)(2,1)} %copy-done.6, bf16[128,6,32,128]{3,0,2,1:T(8,128)(2,1)} %all-gather.5.cloned.1.call-done), kind=kOutput, calls=%fused_computation.110 | convolution fusion | flops 1358954496 | bytes 17018880 | tf_op jit(solution)/shard_map/dot_general | solution.py:65
  390.2 205.1 %all-reduce.10.cloned.1.call-done = f32[64,16384]{1,0:T(8,128)} async-done(((f32[64,16384]{1,0:T(8,128)}), f32[64,16384]{1,0:T(8,128)}) %all-reduce.10.cloned.1.call-update) | async-done | bytes 4194320
  595.3 1.1 dynamic-slice_bitcast_fusion.1
  596.4 0.7 copy.91
  597.1 121.8 %all-reduce.8.cloned.1.call-done = f32[8,128,27]{1,0,2:T(8,128)} async-done(((f32[8,128,27]{1,0,2:T(8,128)}), f32[8,128,27]{1,0,2:T(8,128)}) %all-reduce.8.cloned.1.call-update) | async-done | bytes 110608 | tf_op jit(solution)/shard_map/psum | solution.py:142
  718.9 0.9 broadcast_multiply_fusion
  719.8 0.2 copy.83
  720.0 0.9 reshape.100
  (111 shorter events, 11.5 us)
Async XLA Ops:
  7.2 11.4 %copy-start = (bf16[27,128,128]{2,1,0:T(8,128)(2,1)S(1)}, bf16[27,128,128]{2,1,0:T(8,128)(2,1)}, u32[]{:S(2)}) copy-start(bf16[27,128,128]{2,1,0:T(8,128)(2,1)} %param.11) | copy-start | bytes 2654212
  7.2 196.9 %reduce-scatter.2.cloned.1.call-start = ((), (), s32[]{:S(2)}) async-start(), calls=%async_computation.1 | async-start | bytes 13369344 | tf_op jit(solution)/shard_map/reduce_scatter | solution.py:121
  11.6 9.9 %collective-permute-start = (bf16[20,2,32,128]{3,0,2,1:T(8,128)(2,1)}, bf16[20,2,32,128]{3,0,2,1:T(8,128)(2,1)S(1)}, u32[]{:S(2)}, u32[]{:S(2)}) collective-permute-start(bf16[20,2,32,128]{3,0,2,1:T(8,128)(2,1)} %get-tuple-element.5), channel_id=1, source_target_pairs={{0,16},{16,32},{32,48},{48,64},{64,80},{80,96},{96,112},{112,128},... | collective-permute-start | bytes 983048 | tf_op jit(solution)/shard_map/ppermute | solution.py:17
  16.6 10.4 %collective-permute-start.1 = (bf16[20,2,32,128]{3,0,2,1:T(8,128)(2,1)}, bf16[20,2,32,128]{3,0,2,1:T(8,128)(2,1)}, u32[]{:S(2)}, u32[]{:S(2)}) collective-permute-start(bf16[20,2,32,128]{3,0,2,1:T(8,128)(2,1)} %get-tuple-element.6), channel_id=1, source_target_pairs={{16,0},{32,16},{48,32},{64,48},{80,64},{96,80},{112,96},{128,112},... | collective-permute-start | bytes 983048 | tf_op jit(solution)/shard_map/ppermute | solution.py:19
  21.6 0.8 copy-start.3
  28.4 5.2 copy-start.4
  41.5 1.0 copy-start.5
  41.5 166.7 %copy-start.7 = (u32[256]{0:T(256)S(1)}, u32[256]{0:T(256)}, u32[]{:S(2)}) copy-start(u32[256]{0:T(256)} %constant.59) | copy-start | bytes 3076
  41.5 231.7 %all-gather.3.cloned.1.call-start = ((), (), s32[]{:S(2)}) async-start(), calls=%async_computation.2 | async-start | bytes 3342336 | tf_op jit(solution)/shard_map/all_gather | solution.py:109
  44.1 336.5 %all-gather.5.cloned.1.call-start = ((), (), s32[]{:S(2)}) async-start(), calls=%async_computation.3 | async-start | bytes 6684672 | tf_op jit(solution)/shard_map/all_gather | solution.py:108
  206.5 388.7 %all-reduce.10.cloned.1.call-start = ((), (), s32[]{:S(2)}) async-start(), calls=%async_computation.5 | async-start | bytes 8388608
  213.7 4.1 copy-start.6
  222.2 3.9 copy-start.2
  230.0 488.8 %all-reduce.8.cloned.1.call-start = ((), (), s32[]{:S(2)}) async-start(), calls=%async_computation.4 | async-start | bytes 221184 | tf_op jit(solution)/shard_map/psum | solution.py:142
  380.6 340.3 %copy-start.1 = (bf16[27,128,128]{2,1,0:T(8,128)(2,1)S(1)}, bf16[27,128,128]{2,1,0:T(8,128)(2,1)}, u32[]{:S(2)}) copy-start(bf16[27,128,128]{2,1,0:T(8,128)(2,1)} %param.11) | copy-start | bytes 2654212
Sparse Core Ops, SparseCore 0:
  41.6 162.3 reduce-scatter.1
  207.1 66.0 all-gather.2
  275.6 104.9 all-gather.4
  383.1 212.0 all-reduce.9
  598.3 120.4 all-reduce.7
where the time goes:
time: 728 us; the launch traced here: 727 us
  waiting for transfers between devices  577 us (79%)
  blocking collectives  55.8 us (8%)
  local copies, waits for them, and re-layouts  34.3 us (5%)
  matrix products  29 us (4%)
  between operations  16.7 us (2%)
  starting transfers between devices  7.45 us (1%)
    unnamed x6, waiting for transfers between devices  205 us
    reduce_scatter x1, waiting for transfers between devices, shards(): lax.psum_scatter(jnp.dot(two_lhs, grad_cols, preferred_element_type=jnp.f...  158 us
    psum x1, waiting for transfers between devices, shards(): two_sum, one_sum = lax.psum((two_grad, one_grad), 'slab')  122 us
    psum x1, blocking collectives, shards(): two_sum, one_sum = lax.psum((two_grad, one_grad), 'slab')  55.8 us
    all_gather x1, waiting for transfers between devices, shards(): lax.all_gather(feat_ext, 'chan', axis=0, tiled=True)  42.9 us
    all_gather x1, waiting for transfers between devices, shards(): lax.all_gather(hidden_ext, 'chan', axis=0, tiled=True)  42 us
    unnamed x124, local copies, waits for them, and re-layouts  26.8 us
    dot_general x2, matrix products, weight_grad(): lax.dot_general(columns, activation.reshape(activation.shape[0], -1), (((...  18.1 us
  transfers between devices with their start and end apart: 7, of which 7 were waited for; matrix products, arithmetic and copies ran while one was open for 6% of the time, Pallas kernels for 0%

commit v1 on v0

v1 whole, which is shorter than its diff:
```python
import math

import jax
import jax.numpy as jnp
from jax import lax
from jax.experimental import pallas as pl
from jax.experimental.pallas import tpu as pltpu
from jax.sharding import Mesh
from jax.sharding import PartitionSpec as P

BF16, F32 = jnp.bfloat16, jnp.float32
CHAN, SLAB = ("y", "zh"), ("x", "zl", "core")
Z, R, X = 4, 2, 128
NZ, NY = 64, 32
MID, CIN = 128, 64


def kept_scale(offset, seed, z, h, shape):
    c = lax.broadcasted_iota(jnp.int32, shape, 0)
    w = lax.broadcasted_iota(jnp.int32, shape, 1)
    position = ((c * NZ + z) * NY + h) * X + w
    m = (position + offset) ^ seed
    m = m * jnp.int32(739982445)
    m = m ^ lax.shift_right_logical(m, jnp.int32(15))
    m = m * jnp.int32(695938361)
    m = m ^ lax.shift_right_logical(m, jnp.int32(12))
    return jnp.where((m & 65535) < 52429, F32(1.25), F32(0.0))


def store_shifts(dst, plane, row, block):
    n = block.shape[0]
    lane = lax.broadcasted_iota(jnp.int32, block.shape, 1)
    cols = slice(row * X, (row + 1) * X)
    ahead = jnp.where(lane == X - 1, 0.0, pltpu.roll(block, X - 1, 1))
    behind = jnp.where(lane == 0, 0.0, pltpu.roll(block, 1, 1))
    dst[plane, 0:n, cols] = ahead.astype(BF16)
    dst[plane, n : 2 * n, cols] = block.astype(BF16)
    dst[plane, 2 * n : 3 * n, cols] = behind.astype(BF16)


def dot(a, b):
    return lax.dot_general(a, b, (((1,), (0,)), ((), ())), preferred_element_type=F32)


def dot_t(a, b):
    return lax.dot_general(a, b, (((1,), (1,)), ((), ())), preferred_element_type=F32)


def kernel(scal, own, left, right, feat, w_two, w_one, wout, fout, g3, p3, act, hid, fin):
    z0, h0, offset, seed = scal[0], scal[1], scal[2], scal[3]

    def build(src, base, at):
        def step(i, _):
            for row in range(6):
                store_shifts(g3, at + i, row, src[base + i * 6 + row].astype(F32))
            return 0

        return step

    lax.fori_loop(0, 2, build(left, 0, 0), 0)
    lax.fori_loop(0, 4, build(own, 0, 2), 0)
    lax.fori_loop(0, 2, build(right, 0, 6), 0)

    hid[...] = jnp.zeros_like(hid)

    def spread(i, _):
        for kd in range(3):
            total = None
            for kh in range(3):
                q = kd * 3 + kh
                lhs = jnp.concatenate([w_two[3 * q], w_two[3 * q + 1], w_two[3 * q + 2]], axis=1)
                part = dot(lhs, g3[i, :, (2 - kh) * X : (6 - kh) * X])
                total = part if total is None else total + part
            hid[i + kd] = hid[i + kd] + total
        return 0

    lax.fori_loop(0, 8, spread, 0)

    def mask(j, pre_of):
        for row in range(4):
            scale = kept_scale(offset, seed, z0 - 1 + j, h0 - 1 + row, (MID, X))
            pre = pre_of(row).astype(F32)
            grad = hid[j + 2, :, row * X : (row + 1) * X]
            store_shifts(p3, j, row, jnp.where(pre > 0, grad * scale, 0.0))
            yield row, pre, scale

    for _ in mask(0, lambda row: left[12 + row]):
        pass
    for _ in mask(5, lambda row: right[12 + row]):
        pass

    def inner(i, _):
        for row, pre, scale in mask(i + 1, lambda row: own[24 + i * 4 + row]):
            if row in (1, 2):
                act[i, :, (row - 1) * X : row * X] = (jnp.maximum(pre, 0.0) * scale).astype(BF16)
        return 0

    lax.fori_loop(0, Z, inner, 0)

    for q in range(9):
        kd, kh = divmod(q, 3)
        total = None
        for i in range(Z):
            rows = g3[i + 3 - kd, :, (3 - kh) * X : (5 - kh) * X]
            part = dot_t(rows, act[i])
            total = part if total is None else total + part
        for kw in range(3):
            wout[3 * q + kw] = total[kw * 128 : (kw + 1) * 128]

    blank = jnp.zeros((CIN, R * X), BF16)
    for q in range(5):
        total = None
        for i in range(Z):
            f = feat[i]
            for tap, rhs in ((q, jnp.concatenate([f, blank], 0)), (q + 5, jnp.concatenate([blank, f], 0))):
                if tap > 8:
                    continue
                kd, kh = divmod(tap, 3)
                part = dot_t(p3[i + 2 - kd, :, (2 - kh) * X : (4 - kh) * X], rhs)
                total = part if total is None else total + part
        for kw in range(3):
            wout[27 + 3 * q + kw] = total[kw * 128 : (kw + 1) * 128]

    fin[...] = jnp.zeros_like(fin)

    def spread_one(i, _):
        for kd in range(3):
            total = None
            for kh in range(3):
                q = kd * 3 + kh
                lhs = jnp.concatenate([w_one[3 * q], w_one[3 * q + 1], w_one[3 * q + 2]], axis=1)
                part = dot(lhs, p3[i, :, (2 - kh) * X : (4 - kh) * X])
                total = part if total is None else total + part
            fin[i + kd] = fin[i + kd] + total
        return 0

    lax.fori_loop(0, 6, spread_one, 0)
    for i in range(Z):
        fout[i] = fin[i + 2].astype(BF16)


def on_cells(scal, own, left, right, feat, weight_two, weight_one):
    vmem = pl.BlockSpec(memory_space=pltpu.VMEM)
    return pl.pallas_call(
        kernel,
        out_shape=(
            jax.ShapeDtypeStruct((42, 128, 128), F32),
            jax.ShapeDtypeStruct((Z, CIN, R * X), BF16),
        ),
        in_specs=[pl.BlockSpec(memory_space=pltpu.SMEM)] + [vmem] * 6,
        out_specs=(vmem, vmem),
        scratch_shapes=[
            pltpu.VMEM((8, 384, 6 * X), BF16),
            pltpu.VMEM((6, 384, 4 * X), BF16),
            pltpu.VMEM((Z, MID, R * X), BF16),
            pltpu.VMEM((10, MID, 4 * X), F32),
            pltpu.VMEM((8, CIN, R * X), F32),
        ],
        compiler_params=pltpu.CompilerParams(vmem_limit_bytes=48 * 1024 * 1024),
    )(scal, own, left, right, feat, weight_two, weight_one)


def shards(features, pre_act, out_grad, weight_one, weight_two, dropout_seed, layer_offset):
    chan_pos, slab_pos = lax.axis_index(CHAN), lax.axis_index(SLAB)
    core = lax.axis_index("core")

    grad = jnp.pad(out_grad.transpose(1, 2, 0, 3), ((0, 0), (2, 2), (0, 0), (0, 0))).reshape(Z, 18, 2, 8, X)
    grad = jnp.stack([grad[:, i : i + 16] for i in range(3)], axis=2)
    grad = grad.transpose(1, 0, 2, 3, 4, 5).reshape(16, 24, 8, X)
    pre = jnp.pad(pre_act.transpose(1, 2, 0, 3), ((0, 0), (1, 1), (0, 0), (0, 0))).reshape(Z, 17, 2, 8, X)
    pre = jnp.stack([pre[:, i : i + 16] for i in range(2)], axis=2)
    pre = pre.transpose(1, 0, 2, 3, 4, 5).reshape(16, 16, 8, X)
    feat = features.reshape(4, Z, 16, R, X).transpose(2, 1, 3, 0, 4).reshape(16, Z, 8, X)
    sent = jnp.concatenate([grad, pre, feat], axis=1)
    got = lax.all_to_all(sent, CHAN, 0, 0, tiled=True)
    cells = got.transpose(1, 0, 2, 3).reshape(44, 128, X)
    own = cells[:40]
    feat = cells[40:].reshape(Z, 16, R, 4, X).transpose(0, 1, 3, 2, 4).reshape(Z, CIN, R * X)

    up = [(i, i + 1) for i in range(15)]
    down = [(i + 1, i) for i in range(15)]
    left = lax.ppermute(jnp.concatenate([own[12:24], own[36:40]]), SLAB, up)
    right = lax.ppermute(jnp.concatenate([own[0:12], own[24:28]]), SLAB, down)

    scal = jnp.stack([slab_pos * Z, chan_pos * R, layer_offset[0], dropout_seed[0]])
    filters, feature = on_cells(scal, own, left, right, feat, weight_two, weight_one)

    filters = filters.reshape(2, 21, 128, 128)
    theirs = lax.dynamic_index_in_dim(filters, 1 - core, 0, keepdims=False).astype(BF16)
    mine = lax.dynamic_index_in_dim(filters, core, 0, keepdims=False)
    mine = mine + lax.ppermute(theirs, "core", [(0, 1), (1, 0)]).astype(F32)
    mine = mine.astype(BF16).reshape(21, 16, 8, 128).transpose(1, 0, 2, 3)
    feature = feature.reshape(Z, 16, 4, R, X).transpose(1, 0, 3, 2, 4).reshape(16, Z, 8, X)
    got = lax.all_to_all(jnp.concatenate([mine, feature], axis=1), CHAN, 0, 0, tiled=True)
    feature = got[:, 21:].reshape(16, Z, R, 4, X).transpose(3, 1, 0, 2, 4).reshape(4, Z, NY, X).astype(F32)
    part = got[:, :21].astype(F32).sum(axis=0)
    copies = jnp.broadcast_to(part[None], (8, 21, 8, 128))
    part = lax.all_to_all(copies, ("x", "zl"), 0, 0, tiled=True).sum(axis=0)
    scale = 1.0 / math.sqrt(NZ * NY * X)
    total = lax.all_gather(part * scale, "core", axis=0, tiled=True)
    two = total[:27].transpose(1, 2, 0).reshape(8, 27 * MID)
    one = total[27:].reshape(5, 3, 8, 2, CIN).transpose(3, 0, 1, 2, 4).reshape(30, 8, CIN)[:27]
    one = one.transpose(1, 2, 0).reshape(4, 54 * CIN)
    return feature, one, two


def solution(mesh):
    split = Mesh(mesh.devices.reshape(4, 2, 2, 4, 4), ("x", "zl", "core", "y", "zh"))
    cells = P(CHAN, SLAB, None, None)
    return jax.shard_map(
        shards,
        mesh=split,
        in_specs=(cells, cells, cells, P(), P(), P(), P()),
        out_specs=(cells, P(CHAN, None), P(CHAN, None)),
        check_vma=False,
    )
```

time: 728 us -> 145 us (0.20)
  waiting for transfers between devices: 577 us -> 14 us
  matrix products: 29 us -> 0 us
  local copies, waits for them, and re-layouts: 34.3 us -> 12.4 us
  blocking collectives: 55.8 us -> 75.1 us
  Pallas kernels: 0 us -> 17.7 us
  between operations: 16.7 us -> 2.29 us
  starting transfers between devices: 7.45 us -> 20 us
    unnamed x6 -> x0, waiting for transfers between devices: 205 us -> none
    reduce_scatter x1 -> x0, waiting for transfers between devices: 158 us -> none  [shards(): lax.psum_scatter(jnp.dot(two_lhs, grad_cols, preferred_element_type=jnp.f...]
    psum x1 -> x0, waiting for transfers between devices: 122 us -> none  [shards(): two_sum, one_sum = lax.psum((two_grad, one_grad), 'slab')]
    all_gather x2 -> x0, waiting for transfers between devices: 84.9 us -> none  [the longest x1 42.9 us: shards(): lax.all_gather(feat_ext, 'chan', axis=0, tiled=True)]
    all_to_all x0 -> x2, blocking collectives: none -> 70.8 us  [the longest x1 46.9 us: shards(): got = lax.all_to_all(sent, CHAN, 0, 0, tiled=True)]
    psum x1 -> x0, blocking collectives: 55.8 us -> none  [shards(): two_sum, one_sum = lax.psum((two_grad, one_grad), 'slab')]
    dot_general x4 -> x0, matrix products: 29 us -> none  [the longest x2 18.1 us: weight_grad(): lax.dot_general(columns, activation.reshape(activation.shape[0], -1), (((...]
    unnamed x124 -> x13, local copies, waits for them, and re-layouts: 26.8 us -> 3.61 us
  transfers between devices with their start and end apart: 7 -> 4, of which waited for: 7 -> 3; matrix products, arithmetic and copies ran while one was open for 6% -> 3% of each run, Pallas kernels for 0% -> 0%
where the time goes in v1:
time: 145 us
  blocking collectives  75.1 us (52%)
  starting transfers between devices  20 us (14%)
  Pallas kernels  17.7 us (12%)
  waiting for transfers between devices  14 us (10%)
  local copies, waits for them, and re-layouts  12.4 us (9%)
  other arithmetic  3.05 us (2%)
  between operations  2.29 us (2%)
    all_to_all x1, blocking collectives, shards(): got = lax.all_to_all(sent, CHAN, 0, 0, tiled=True)  46.9 us
    all_to_all x1, blocking collectives, shards(): lax.all_to_all(jnp.concatenate([mine, feature], axis=1), CHAN, 0, 0, tile...  24 us
    pallas_call x1, Pallas kernels, on_cells(): pl.pallas_call(kernel, out_shape=(jax.ShapeDtypeStruct((42, 128, 128), F3...  17.7 us
    all_to_all x1, starting transfers between devices, shards(): part = lax.all_to_all(copies, ('x', 'zl'), 0, 0, tiled=True).sum(axis=0)  11.7 us
    all_to_all x1, waiting for transfers between devices, shards(): part = lax.all_to_all(copies, ('x', 'zl'), 0, 0, tiled=True).sum(axis=0)  9.06 us
    ppermute x1, starting transfers between devices, shards(): right = lax.ppermute(jnp.concatenate([own[0:12], own[24:28]]), SLAB, down)  6.35 us
    all_gather x1, blocking collectives, shards(): total = lax.all_gather(part * scale, 'core', axis=0, tiled=True)  4.3 us
    unnamed x13, local copies, waits for them, and re-layouts  3.61 us
  transfers between devices with their start and end apart: 4, of which 3 were waited for; matrix products, arithmetic and copies ran while one was open for 3% of the time, Pallas kernels for 0%

profile of v1, /device:TPU:1, one launch (start us, length us, event | category | flops | bytes accessed | tf_op | source)
XLA Modules:
  0.0 144.6 jit_solution(9171670687080751394)
XLA Ops:
  0.6 1.1 copy.97
  1.8 0.1 slice_bitcast_fusion.4
  1.9 0.0 copy-start.3
  1.9 0.1 maximum_bitcast_fusion
  2.0 0.2 copy.67
  2.2 0.6 copy-done.3
  2.9 0.2 copy.96
  3.1 0.0 copy-start.4
  3.1 0.1 slice_bitcast_fusion.1
  3.2 0.1 maximum_bitcast_fusion.1
  3.3 0.7 copy-done.4
  4.0 0.2 copy.70
  4.2 0.2 pad_maximum_fusion
  4.3 46.9 %all_to_all.15 = bf16[16,44,8,128]{3,2,1,0:T(8,128)(2,1)S(1)} all-to-all(bf16[16,44,8,128]{3,2,1,0:T(8,128)(2,1)S(1)} %pad_maximum_fusion), channel_id=1, replica_groups=mesh['x'=4,'zl'=2,'core'=2,'y'=4,'zh'=4] {'y','zh'}, dimensions={0} | all-to-all | bytes 2883584 | tf_op jit(solution)/shard_map/all_to_all | solution.py:175
  51.2 0.0 copy-start.2
  51.3 0.1 fusion.4
  51.3 0.1 copy.94
  51.4 0.9 copy-done.2
  52.4 6.4 %collective-permute-start.1 = (bf16[16,128,128]{2,1,0:T(8,128)(2,1)S(1)}, bf16[16,128,128]{2,1,0:T(8,128)(2,1)S(1)}, u32[]{:S(2)}, u32[]{:S(2)}) collective-permute-start(bf16[16,128,128]{2,1,0:T(8,128)(2,1)S(1)} %pad_maximum_fusion.3), channel_id=1, source_target_pairs={{16,0},{32,16},{48,32},{64,48},{80,64},{96,80},{112,96},{128,112},... | collective-permute-start | bytes 1572872 | tf_op jit(solution)/shard_map/ppermute | solution.py:183
  58.8 0.1 copy.95
  58.9 0.8 pad_maximum_fusion.2
  59.7 1.9 %collective-permute-start = (bf16[16,128,128]{2,1,0:T(8,128)(2,1)}, bf16[16,128,128]{2,1,0:T(8,128)(2,1)S(1)}, u32[]{:S(2)}, u32[]{:S(2)}) collective-permute-start(bf16[16,128,128]{2,1,0:T(8,128)(2,1)} %pad_maximum_fusion.2), channel_id=1, source_target_pairs={{0,16},{16,32},{32,48},{48,64},{64,80},{80,96},{96,112},{112,128},... | collective-permute-start | bytes 1572872 | tf_op jit(solution)/shard_map/ppermute | solution.py:182
  63.0 0.1 pad_add_fusion.scal
  63.0 0.1 copy.76
  63.1 0.1 copy.77
  63.2 0.0 copy-start
  63.2 0.0 copy-start.1
  63.3 0.1 reshape.77.feat
  63.4 1.8 %copy_bitcast_fusion.own = bf16[40,128,128]{2,1,0:T(8,128)(2,1)S(1)} fusion(bf16[44,16,8,128]{3,2,0,1:T(8,128)(2,1)} %bitcast.77), kind=kLoop, calls=%fused_computation.5 | loop fusion | bytes 2621440 | tf_op jit(solution)/shard_map/slice | solution.py:177
  65.1 0.0 collective-permute-done.1.right
  65.1 2.9 %collective-permute-done.left = bf16[16,128,128]{2,1,0:T(8,128)(2,1)S(1)} collective-permute-done((bf16[16,128,128]{2,1,0:T(8,128)(2,1)}, bf16[16,128,128]{2,1,0:T(8,128)(2,1)S(1)}, u32[]{:S(2)}, u32[]{:S(2)}) %collective-permute-start) | collective-permute-done | bytes 524320 | tf_op jit(solution)/shard_map/ppermute | solution.py:182
  68.1 0.0 copy-done
  68.1 0.0 copy-done.1
  68.1 17.7 %shard_map.94 = (f32[42,128,128]{2,1,0:T(8,128)}, bf16[4,64,256]{2,1,0:T(8,128)(2,1)S(1)}) custom-call(s32[4]{0:T(128)S(1)} %pad_add_fusion.scal, bf16[40,128,128]{2,1,0:T(8,128)(2,1)S(1)} %copy_bitcast_fusion.own, bf16[16,128,128]{2,1,0:T(8,128)(2,1)S(1)} %collective-permute-done.left, bf16[16,128,128]{2,1,0:T(8,128)(2,1)S(1)} %collective-permute-done.1.right, ...), custom_call_target="tpu_custom_call" | custom-call | tf_op jit(solution)/shard_map/pallas_call | solution.py:144
  85.7 1.5 %fusion.1 = bf16[21,128,128]{2,1,0:T(8,128)(2,1)S(1)} fusion(f32[2,21,128,128]{3,2,1,0:T(8,128)} %bitcast.84, s32[]{:T(128)S(6)} %select_n.8), kind=kLoop, calls=%fused_computation.8 | loop fusion | bytes 1376260 | tf_op jit(solution)/shard_map/convert_element_type | solution.py:189
  87.2 0.1 collective-permute-start.2
  87.4 2.0 %collective-permute-done.2 = bf16[21,128,128]{2,1,0:T(8,128)(2,1)S(1)} collective-permute-done((bf16[21,128,128]{2,1,0:T(8,128)(2,1)S(1)}, bf16[21,128,128]{2,1,0:T(8,128)(2,1)S(1)}, u32[]{:S(2)}, u32[]{:S(2)}) %collective-permute-start.2) | collective-permute-done | bytes 688160 | tf_op jit(solution)/shard_map/ppermute | solution.py:191
  89.4 1.5 %fusion.2 = bf16[16,21,8,128]{3,2,0,1:T(8,128)(2,1)S(1)} fusion(bf16[21,128,128]{2,1,0:T(8,128)(2,1)S(1)} %collective-permute-done.2, f32[2,21,128,128]{3,2,1,0:T(8,128)} %bitcast.85, s32[]{:T(128)S(6)} %select_n.7), kind=kLoop, calls=%fused_computation.9 | loop fusion | flops 1032192 | bytes 2752516 | tf_op jit(solution)/shard_map/transpose | solution.py:192
  91.0 0.1 pad_maximum_fusion.1
  91.1 0.1 copy.80
  91.2 24.0 %all_to_all.16 = bf16[16,25,8,128]{3,2,1,0:T(8,128)(2,1)S(1)} all-to-all(bf16[16,25,8,128]{3,2,1,0:T(8,128)(2,1)S(1)} %copy.80), channel_id=1, replica_groups=mesh['x'=4,'zl'=2,'core'=2,'y'=4,'zh'=4] {'y','zh'}, dimensions={0} | all-to-all | bytes 1638400 | tf_op jit(solution)/shard_map/all_to_all | solution.py:194
  115.2 0.1 convert_reduce_fusion
  115.3 0.9 broadcast_in_dim.2
  116.2 11.7 %all-to-all-start.2 = ((f32[8,21,8,128]{3,2,1,0:T(8,128)}), f32[8,21,8,128]{3,2,1,0:T(8,128)S(1)}, u32[]{:S(2)}, u32[]{:S(2)}) async-start(f32[8,21,8,128]{3,2,1,0:T(8,128)} %broadcast_in_dim.2), calls=%async_computation.2 | async-start | bytes 1376256 | tf_op jit(solution)/shard_map/all_to_all | solution.py:198
  127.8 0.1 copy.86
  127.9 0.9 copy.82
  128.8 9.1 %all-to-all-done.2 = f32[8,21,8,128]{3,2,1,0:T(8,128)S(1)} async-done(((f32[8,21,8,128]{3,2,1,0:T(8,128)}), f32[8,21,8,128]{3,2,1,0:T(8,128)S(1)}, u32[]{:S(2)}, u32[]{:S(2)}) %all-to-all-start.2) | async-done | bytes 688160 | tf_op jit(solution)/shard_map/all_to_all | solution.py:198
  138.0 4.3 %all_gather.3 = f32[42,8,128]{2,1,0:T(8,128)S(1)} all-gather(f32[21,8,128]{2,1,0:T(8,128)S(1)} %broadcast_multiply_fusion), channel_id=1, replica_groups=mesh['x'=4,'zl'=2,'core'=2,'y'=4,'zh'=4] {'core'}, dimensions={0}, use_global_device_ids=true | all-gather | bytes 258048 | tf_op jit(solution)/shard_map/all_gather | solution.py:200
  142.3 0.2 copy.85
  142.5 0.9 reshape.85
  143.4 0.1 reshape.82
  143.6 0.1 copy.84
  143.8 0.8 reshape.84
  (18 shorter events, 0.4 us)
Async XLA Ops:
  1.9 1.0 copy-start.3
  3.1 0.9 copy-start.4
  51.2 1.1 copy-start.2
  52.4 12.7 %collective-permute-start.1 = (bf16[16,128,128]{2,1,0:T(8,128)(2,1)S(1)}, bf16[16,128,128]{2,1,0:T(8,128)(2,1)S(1)}, u32[]{:S(2)}, u32[]{:S(2)}) collective-permute-start(bf16[16,128,128]{2,1,0:T(8,128)(2,1)S(1)} %pad_maximum_fusion.3), channel_id=1, source_target_pairs={{16,0},{32,16},{48,32},{64,48},{80,64},{96,80},{112,96},{128,112},... | collective-permute-start | bytes 1572872 | tf_op jit(solution)/shard_map/ppermute | solution.py:183
  59.7 8.3 %collective-permute-start = (bf16[16,128,128]{2,1,0:T(8,128)(2,1)}, bf16[16,128,128]{2,1,0:T(8,128)(2,1)S(1)}, u32[]{:S(2)}, u32[]{:S(2)}) collective-permute-start(bf16[16,128,128]{2,1,0:T(8,128)(2,1)} %pad_maximum_fusion.2), channel_id=1, source_target_pairs={{0,16},{16,32},{32,48},{48,64},{64,80},{80,96},{96,112},{112,128},... | collective-permute-start | bytes 1572872 | tf_op jit(solution)/shard_map/ppermute | solution.py:182
  63.2 4.8 %copy-start = (bf16[27,128,128]{2,1,0:T(8,128)(2,1)S(1)}, bf16[27,128,128]{2,1,0:T(8,128)(2,1)}, u32[]{:S(2)}) copy-start(bf16[27,128,128]{2,1,0:T(8,128)(2,1)} %w_two.1) | copy-start | bytes 2654212
  63.2 4.8 %copy-start.1 = (bf16[27,64,128]{2,1,0:T(8,128)(2,1)S(1)}, bf16[27,64,128]{2,1,0:T(8,128)(2,1)}, u32[]{:S(2)}) copy-start(bf16[27,64,128]{2,1,0:T(8,128)(2,1)} %w_one.1) | copy-start | bytes 1327108
  87.2 2.2 %collective-permute-start.2 = (bf16[21,128,128]{2,1,0:T(8,128)(2,1)S(1)}, bf16[21,128,128]{2,1,0:T(8,128)(2,1)S(1)}, u32[]{:S(2)}, u32[]{:S(2)}) collective-permute-start(bf16[21,128,128]{2,1,0:T(8,128)(2,1)S(1)} %fusion.1), channel_id=1, source_target_pairs={{0,16},{16,0},{1,17},{17,1},{2,18},{18,2},{3,19},{19,3},{4,20},{20... | collective-permute-start | bytes 2064392 | tf_op jit(solution)/shard_map/ppermute | solution.py:191
  116.2 21.7 %all-to-all-start.2 = ((f32[8,21,8,128]{3,2,1,0:T(8,128)}), f32[8,21,8,128]{3,2,1,0:T(8,128)S(1)}, u32[]{:S(2)}, u32[]{:S(2)}) async-start(f32[8,21,8,128]{3,2,1,0:T(8,128)} %broadcast_in_dim.2), calls=%async_computation.2 | async-start | bytes 1376256 | tf_op jit(solution)/shard_map/all_to_all | solution.py:198

commit v2 on v1

v2 whole, which is shorter than its diff:
```python
import math

import jax
import jax.numpy as jnp
from jax import lax
from jax.experimental import pallas as pl
from jax.experimental.pallas import tpu as pltpu
from jax.sharding import Mesh
from jax.sharding import PartitionSpec as P

BF16, F32 = jnp.bfloat16, jnp.float32
CHAN, SLAB = ("y", "zh"), ("x", "zl", "core")
Z, R, X = 4, 2, 128
NZ, NY = 64, 32
MID, CIN = 128, 64
TILES = 8


def kept_scale(offset, seed, z, h):
    c = lax.broadcasted_iota(jnp.int32, (MID, X), 0)
    w = lax.broadcasted_iota(jnp.int32, (MID, X), 1)
    position = ((c * NZ + z) * NY + h) * X + w
    m = (position + offset) ^ seed
    m = m * jnp.int32(739982445)
    m = m ^ lax.shift_right_logical(m, jnp.int32(15))
    m = m * jnp.int32(695938361)
    m = m ^ lax.shift_right_logical(m, jnp.int32(12))
    return jnp.where((m & 65535) < 52429, F32(1.25), F32(0.0))


def store_shifts(dst, plane, row, block):
    lane = lax.broadcasted_iota(jnp.int32, block.shape, 1)
    cols = slice(row * X, (row + 1) * X)
    ahead = jnp.where(lane == X - 1, 0.0, pltpu.roll(block, X - 1, 1))
    behind = jnp.where(lane == 0, 0.0, pltpu.roll(block, 1, 1))
    dst[plane, 0:128, cols] = ahead.astype(BF16)
    dst[plane, 128:256, cols] = block.astype(BF16)
    dst[plane, 256:384, cols] = behind.astype(BF16)


def dot(a, b):
    return lax.dot_general(a, b, (((1,), (0,)), ((), ())), preferred_element_type=F32)


def dot_t(a, b):
    return lax.dot_general(a, b, (((1,), (1,)), ((), ())), preferred_element_type=F32)


def tile(ref, t):
    return ref[:, t].astype(F32).reshape(128, X)


def store_halves(core, mine, theirs, s, step, slab):
    for me in range(2):

        @pl.when(core == me)
        def _():
            for half in range(2):
                if 0 <= s - half * step <= step:
                    if half == me:
                        mine[s - half * step] = slab
                    else:
                        theirs[s - half * step] = slab.astype(BF16)


def kernel_a(got, w_two, g3, own, left, right, wk):
    for kd in range(3):
        for kh in range(3):
            for kw in range(3):
                wk[kh, kd * MID : (kd + 1) * MID, kw * 128 : (kw + 1) * 128] = w_two[9 * kd + 3 * kh + kw]
    for z in range(Z):
        for r in range(4):
            store_shifts(g3, z, r, tile(got, z * TILES + r))
    own[...] = jnp.zeros_like(own)
    for z in range(Z):
        total = None
        for kh in range(3):
            part = dot(wk[kh], g3[z, :, (2 - kh) * X : (4 - kh) * X])
            total = part if total is None else total + part
        for kd in range(3):
            term = total[kd * MID : (kd + 1) * MID]
            target = z + kd - 1
            if target < 0:
                left[...] = term
            elif target == Z:
                right[...] = term
            else:
                own[target] = own[target] + term


def kernel_b(scal, got, halo_l, halo_r, g3, mask, mine, theirs, act):
    z0, h0, offset, seed, core = scal[0], scal[1], scal[2], scal[3], scal[4]
    for w in range(-1, Z + 1):
        for r in range(R):
            ref, t = (halo_l, r) if w < 0 else (halo_r, r) if w == Z else (got, w * TILES + 4 + r)
            pre = tile(ref, t)
            if w < 0:
                pre = jnp.where(scal[5] > 0, pre, 0.0)
            elif w == Z:
                pre = jnp.where(scal[6] > 0, pre, 0.0)
            scale = kept_scale(offset, seed, z0 + w, h0 + r)
            act[w + 1, :, r * X : (r + 1) * X] = (jnp.maximum(pre, 0.0) * scale).astype(BF16)
            if 0 <= w < Z:
                mask[w, :, r * X : (r + 1) * X] = jnp.where(pre > 0, scale, 0.0).astype(BF16)
    for q in range(9):
        kd, kh = divmod(q, 3)
        total = None
        for s in range(Z):
            part = dot_t(g3[s, :, (2 - kh) * X : (4 - kh) * X], act[s + kd])
            total = part if total is None else total + part
        for kw in range(3):
            store_halves(core, mine, theirs, 3 * q + kw, 13, total[kw * 128 : (kw + 1) * 128])


def shuffle(back):
    i = lax.broadcasted_iota(jnp.int32, (128, 128), 1 if back else 0)
    j = lax.broadcasted_iota(jnp.int32, (128, 128), 0 if back else 1)
    at = (lax.rem(i, 64) // 4) * 8 + (i // 64) * 4 + lax.rem(i, 4)
    return jnp.where(at == j, F32(1.0), F32(0.0)).astype(BF16)


def kernel_c(scal, hid, from_l, from_r, mask, w_one, p3, fout, fl, fr, wk, fin):
    for kd in range(3):
        for kh in range(3):
            for kw in range(3):
                at = (kh * 3 + kd) * CIN
                wk[at : at + CIN, kw * 128 : (kw + 1) * 128] = w_one[9 * kd + 3 * kh + kw]
    for z in range(Z):
        grad = hid[z]
        if z == 0:
            grad = grad + jnp.where(scal[5] > 0, from_l[...], 0.0)
        if z == Z - 1:
            grad = grad + jnp.where(scal[6] > 0, from_r[...], 0.0)
        grad = grad * mask[z].astype(F32)
        for r in range(R):
            store_shifts(p3, z, r, grad[:, r * X : (r + 1) * X])
    fin[...] = jnp.zeros_like(fin)
    for s in range(Z):
        terms = dot(wk[...], p3[s])
        for kd in range(3):
            for kh in range(3):
                at = (kh * 3 + kd) * CIN
                cols = slice(kh * X, (kh + 2) * X)
                fin[s + kd, :, cols] = fin[s + kd, :, cols] + terms[at : at + CIN]
    back = shuffle(True)
    for w in range(-1, Z + 1):
        for i in range(2):
            rows = jnp.concatenate([fin[w + 1, :, (2 * i + r) * X : (2 * i + r + 1) * X] for r in range(2)], axis=0)
            high = rows.astype(BF16)
            tiles = dot(back, high)
            if w < 0:
                fl[:, i] = tiles.reshape(16, 8, X).astype(BF16)
            elif w == Z:
                fr[:, i] = tiles.reshape(16, 8, X).astype(BF16)
            else:
                tiles = tiles + dot(back, (rows - high.astype(F32)).astype(BF16))
                fout[:, 2 * w + i] = tiles.reshape(16, 8, X)


def kernel_d(scal, got, halo_l, halo_r, p3, mine, theirs, lo, hi):
    core = scal[4]
    lo[...] = jnp.zeros_like(lo)
    hi[...] = jnp.zeros_like(hi)
    order = shuffle(False)
    for w in range(-1, Z + 1):
        for i in range(2):
            ref, t = (halo_l, 2 + i) if w < 0 else (halo_r, 2 + i) if w == Z else (got, w * TILES + 6 + i)
            rows = dot(order, tile(ref, t).astype(BF16))
            if w < 0:
                rows = jnp.where(scal[5] > 0, rows, 0.0)
            elif w == Z:
                rows = jnp.where(scal[6] > 0, rows, 0.0)
            rows = rows.astype(BF16)
            for r in range(2):
                cols = slice((2 * i + r) * X, (2 * i + r + 1) * X)
                lo[w + 1, 0:CIN, cols] = rows[r * CIN : (r + 1) * CIN]
                hi[w + 1, CIN:, cols] = rows[r * CIN : (r + 1) * CIN]
    for q in range(5):
        total = None
        for s in range(Z):
            for tap, rhs in ((q, lo), (q + 5, hi)):
                if tap > 8:
                    continue
                kd, kh = divmod(tap, 3)
                part = dot_t(p3[s], rhs[s + kd, :, kh * X : (kh + 2) * X])
                total = part if total is None else total + part
        for kw in range(3):
            store_halves(core, mine, theirs, 3 * q + kw, 7, total[kw * 128 : (kw + 1) * 128])


VMEM, SMEM = pl.BlockSpec(memory_space=pltpu.VMEM), pl.BlockSpec(memory_space=pltpu.SMEM)


def call(body, args, outs, scratch, flops, scalars):
    return pl.pallas_call(
        body,
        out_shape=tuple(jax.ShapeDtypeStruct(shape, kind) for shape, kind in outs),
        in_specs=[SMEM] * scalars + [VMEM] * (len(args) - scalars),
        out_specs=(VMEM,) * len(outs),
        scratch_shapes=[pltpu.VMEM(shape, kind) for shape, kind in scratch],
        compiler_params=pltpu.CompilerParams(vmem_limit_bytes=24 * 1024 * 1024),
        cost_estimate=pl.CostEstimate(flops=flops, bytes_accessed=4 * 1024 * 1024, transcendentals=0),
    )(*args)


def pairs(rows, count, width):
    return jnp.stack([rows[:, i : i + 16] for i in range(count)], axis=2).swapaxes(0, 1).reshape(16, Z, width, 8, X)


def shards(features, pre_act, out_grad, weight_one, weight_two, dropout_seed, layer_offset):
    chan_pos, slab_pos, core = lax.axis_index(CHAN), lax.axis_index(SLAB), lax.axis_index("core")
    edge = ((0, 0), (1, 1), (0, 0), (0, 0))

    grad = jnp.pad(out_grad.transpose(1, 2, 0, 3), edge).reshape(Z, 17, 2, 8, X)
    pre = pre_act.transpose(1, 2, 0, 3).reshape(Z, 16, 2, 8, X)
    feat = jnp.pad(features.transpose(1, 2, 0, 3), edge).reshape(Z, 17, 1, 8, X)
    sent = jnp.concatenate([pairs(grad, 2, 4), pairs(pre, 1, 2), pairs(feat, 2, 2)], axis=2)
    got = lax.all_to_all(sent.reshape(16, Z * TILES, 8, X), CHAN, 0, 0, tiled=True)

    up = [(i, (i + 1) % 16) for i in range(16)]
    down = [((i + 1) % 16, i) for i in range(16)]
    has_l, has_r = slab_pos > 0, slab_pos < 15
    swap = [(0, 1), (1, 0)]
    halo_l = lax.ppermute(got[:, 3 * TILES + 4 :], SLAB, up)
    halo_r = lax.ppermute(got[:, 4:TILES], SLAB, down)
    scal = jnp.stack(
        [slab_pos * Z, chan_pos * R, layer_offset[0], dropout_seed[0], core, has_l.astype(jnp.int32), has_r.astype(jnp.int32)]
    )

    g3, hid, left, right = call(
        kernel_a,
        (got, weight_two),
        [((Z, 384, 4 * X), BF16), ((Z, MID, R * X), F32), ((MID, R * X), F32), ((MID, R * X), F32)],
        [((3, 384, 384), BF16)],
        10**9,
        0,
    )
    from_l = lax.ppermute(right, SLAB, up)
    from_r = lax.ppermute(left, SLAB, down)
    mask, mine_two, theirs_two = call(
        kernel_b,
        (scal, got, halo_l, halo_r, g3),
        [((Z, MID, R * X), BF16), ((14, 128, 128), F32), ((14, 128, 128), BF16)],
        [((Z + 2, MID, R * X), BF16)],
        4 * 10**9,
        1,
    )
    p3, feature, feature_l, feature_r = call(
        kernel_c,
        (scal, hid, from_l, from_r, mask, weight_one),
        [((Z, 384, R * X), BF16), ((16, 8, 8, X), F32), ((16, 2, 8, X), BF16), ((16, 2, 8, X), BF16)],
        [((9 * CIN, 384), BF16), ((Z + 2, CIN, 4 * X), F32)],
        2 * 10**9,
        1,
    )
    mine_one, theirs_one = call(
        kernel_d,
        (scal, got, halo_l, halo_r, p3),
        [((8, 128, 128), F32), ((8, 128, 128), BF16)],
        [((Z + 2, 128, 4 * X), BF16), ((Z + 2, 128, 4 * X), BF16)],
        2 * 10**9,
        1,
    )

    mine_two = mine_two + lax.ppermute(theirs_two, "core", swap).astype(F32)
    mine_one = mine_one + lax.ppermute(theirs_one, "core", swap).astype(F32)
    mine = jnp.concatenate([mine_two, mine_one]).astype(BF16).reshape(22, 16, 8, 128).transpose(1, 0, 2, 3)
    feature_l, feature_r = (
        jnp.where(has_l, lax.ppermute(feature_r, SLAB, up).astype(F32), 0.0),
        jnp.where(has_r, lax.ppermute(feature_l, SLAB, down).astype(F32), 0.0),
    )
    feature = jnp.concatenate(
        [feature[:, 0:2] + feature_l, feature[:, 2:6], feature[:, 6:8] + feature_r], axis=1
    ).astype(BF16)
    got = lax.all_to_all(jnp.concatenate([mine, feature], axis=1), CHAN, 0, 0, tiled=True)

    rows = got[:, 22:].astype(F32).reshape(16, Z, 4, 4, X)
    none = jnp.zeros((1, Z, 4, X), F32)
    first = rows[:, :, 1] + jnp.concatenate([none, rows[:-1, :, 3]])
    second = rows[:, :, 2] + jnp.concatenate([rows[1:, :, 0], none])
    feature = jnp.stack([first, second], axis=2).transpose(3, 1, 0, 2, 4).reshape(4, Z, NY, X)

    part = got[:, :22].astype(F32).sum(axis=0)
    part = part + lax.ppermute(part, "zl", swap)
    part = part + lax.ppermute(part, "x", [(i, i ^ 1) for i in range(4)])
    part = part + lax.ppermute(part, "x", [(i, i ^ 2) for i in range(4)])
    scale = 1.0 / math.sqrt(NZ * NY * X)
    total = lax.all_gather(part * scale, "core", axis=0, tiled=False)
    two = jnp.concatenate([total[0, :14], total[1, 1:14]])
    one = jnp.concatenate([total[0, 14:], total[1, 15:]])
    two = two.transpose(1, 2, 0).reshape(8, 27 * MID)
    one = one.reshape(5, 3, 8, 2, CIN).transpose(3, 0, 1, 2, 4).reshape(30, 8, CIN)[:27]
    one = one.transpose(1, 2, 0).reshape(4, 54 * CIN)
    return feature, one, two


def solution(mesh):
    split = Mesh(mesh.devices.reshape(4, 2, 2, 4, 4), ("x", "zl", "core", "y", "zh"))
    cells = P(CHAN, SLAB, None, None)
    return jax.shard_map(
        shards,
        mesh=split,
        in_specs=(cells, cells, cells, P(), P(), P(), P()),
        out_specs=(cells, P(CHAN, None), P(CHAN, None)),
        check_vma=False,
    )
```

time: 145 us -> 123 us (0.85)
  local copies, waits for them, and re-layouts: 12.4 us -> 6.2 us
  starting transfers between devices: 20 us -> 14.2 us
  Pallas kernels: 17.7 us -> 14.3 us
  waiting for transfers between devices: 14 us -> 11.3 us
  other arithmetic: 3.05 us -> 0.97 us
  blocking collectives: 75.1 us -> 73.5 us
    all_to_all x1 -> x0, starting transfers between devices: 11.7 us -> none  [shards(): part = lax.all_to_all(copies, ('x', 'zl'), 0, 0, tiled=True).sum(axis=0)]
    all_to_all x1 -> x0, waiting for transfers between devices: 9.06 us -> none  [shards(): part = lax.all_to_all(copies, ('x', 'zl'), 0, 0, tiled=True).sum(axis=0)]
    all_to_all x1, blocking collectives: 46.9 us -> 39.1 us  [shards(): lax.all_to_all(sent.reshape(16, Z * TILES, 8, X), CHAN, 0, 0, tiled=True)]
    ppermute x3 -> x11, waiting for transfers between devices: 4.95 us -> 11.3 us  [the longest x1 3.32 us: shards(): part = part + lax.ppermute(part, 'x', [(i, i ^ 1) for i in range(4)])]
    ppermute x3 -> x11, starting transfers between devices: 8.35 us -> 14.2 us  [the longest x1 4.03 us: shards(): halo_r = lax.ppermute(got[:, 4:TILES], SLAB, down)]
    all_to_all x1, blocking collectives: 24 us -> 28.7 us  [shards(): lax.all_to_all(jnp.concatenate([mine, feature], axis=1), CHAN, 0, 0, tile...]
    pallas_call x1 -> x4, Pallas kernels: 17.7 us -> 14.3 us  [call(): pl.pallas_call(body, out_shape=tuple((jax.ShapeDtypeStruct(shape, kind) f...]
    convert_element_type x2 -> x0, local copies, waits for them, and re-layouts: 2.37 us -> none  [the longest x1 1.46 us: shards(): lax.dynamic_index_in_dim(filters, 1 - core, 0, keepdims=False).astype(BF16)]
  transfers between devices with their start and end apart: 4 -> 11, of which waited for: 3 -> 6; matrix products, arithmetic and copies ran while one was open for 3% -> 1% of each run, Pallas kernels for 0% -> 10%
where the time goes in v2:
time: 123 us
  blocking collectives  73.5 us (60%)
  Pallas kernels  14.3 us (12%)
  starting transfers between devices  14.2 us (12%)
  waiting for transfers between devices  11.3 us (9%)
  local copies, waits for them, and re-layouts  6.2 us (5%)
  between operations  2.28 us (2%)
    all_to_all x1, blocking collectives, shards(): lax.all_to_all(sent.reshape(16, Z * TILES, 8, X), CHAN, 0, 0, tiled=True)  39.1 us
    all_to_all x1, blocking collectives, shards(): lax.all_to_all(jnp.concatenate([mine, feature], axis=1), CHAN, 0, 0, tile...  28.7 us
    pallas_call x4, Pallas kernels, call(): pl.pallas_call(body, out_shape=tuple((jax.ShapeDtypeStruct(shape, kind) f...  14.3 us
    all_gather x1, blocking collectives, shards(): total = lax.all_gather(part * scale, 'core', axis=0, tiled=False)  5.7 us
    ppermute x1, starting transfers between devices, shards(): halo_r = lax.ppermute(got[:, 4:TILES], SLAB, down)  4.03 us
    ppermute x1, starting transfers between devices, shards(): mine_one = mine_one + lax.ppermute(theirs_one, 'core', swap).astype(F32)  3.84 us
    ppermute x1, waiting for transfers between devices, shards(): part = part + lax.ppermute(part, 'x', [(i, i ^ 1) for i in range(4)])  3.32 us
    ppermute x1, waiting for transfers between devices, shards(): part = part + lax.ppermute(part, 'zl', swap)  3.29 us
  transfers between devices with their start and end apart: 11, of which 6 were waited for; matrix products, arithmetic and copies ran while one was open for 1% of the time, Pallas kernels for 10%

profile of v2, /device:TPU:1, one launch (start us, length us, event | category | flops | bytes accessed | tf_op | source)
XLA Modules:
  0.0 122.8 jit_solution(17934265185622462758)
XLA Ops:
  0.6 0.0 copy-start.2
  0.6 1.1 copy.93
  1.7 0.1 pad.11.clone
  1.8 1.1 copy.71
  3.0 0.0 copy-done.2
  3.0 0.2 copy.100
  3.2 0.1 slice_bitcast_fusion.1
  3.3 0.1 maximum_bitcast_fusion
  3.5 0.1 pad_maximum_fusion
  3.6 0.0 copy-start
  3.6 39.1 %all_to_all.10.got = bf16[16,32,8,128]{3,2,1,0:T(8,128)(2,1)S(1)} all-to-all(bf16[16,32,8,128]{3,2,1,0:T(8,128)(2,1)S(1)} %bitcast.87), channel_id=1, replica_groups=mesh['x'=4,'zl'=2,'core'=2,'y'=4,'zh'=4] {'y','zh'}, dimensions={0} | all-to-all | bytes 2097152 | tf_op jit(solution)/shard_map/all_to_all | solution.py:218
  42.7 4.0 %collective-permute-start.1 = (bf16[16,4,8,128]{3,2,1,0:T(8,128)(2,1)S(1)}, bf16[16,4,8,128]{3,2,1,0:T(8,128)(2,1)S(1)}, u32[]{:S(2)}, u32[]{:S(2)}) collective-permute-start(bf16[16,4,8,128]{3,2,1,0:T(8,128)(2,1)S(1)} %get-tuple-element.29), channel_id=1, source_target_pairs={{16,0},{32,16},{48,32},{64,48},{80,64},{96,80},{112,96},{128,112},... | collective-permute-start | bytes 393224 | tf_op jit(solution)/shard_map/ppermute | solution.py:225
  46.7 0.0 collective-permute-start
  48.0 0.1 stack.58.scal
  48.1 0.0 copy-done
  48.1 1.6 %shard_map.94 = (bf16[4,384,512]{2,1,0:T(8,128)(2,1)S(1)}, f32[4,128,256]{2,1,0:T(8,128)S(1)}, f32[128,256]{1,0:T(8,128)S(1)}, f32[128,256]{1,0:T(8,128)S(1)}) custom-call(bf16[16,32,8,128]{3,2,1,0:T(8,128)(2,1)S(1)} %all_to_all.10.got, bf16[27,128,128]{2,1,0:T(8,128)(2,1)S(1)} %copy-done), custom_call_target="tpu_custom_call" | custom-call | flops 1000000000 | bytes 4194304 | tf_op jit(solution)/shard_map/pallas_call | solution.py:195
  49.7 0.1 collective-permute-start.3
  49.8 0.6 collective-permute-start.4
  50.4 0.0 collective-permute-done.1.halo_r
  50.4 0.0 collective-permute-done.halo_l
  50.4 0.0 copy-start.1
  50.4 5.9 %shard_map.95 = (bf16[4,128,256]{2,1,0:T(8,128)(2,1)S(1)}, f32[14,128,128]{2,1,0:T(8,128)S(1)}, bf16[14,128,128]{2,1,0:T(8,128)(2,1)S(1)}) custom-call(s32[7]{0:T(128)S(1)} %stack.58.scal, bf16[16,32,8,128]{3,2,1,0:T(8,128)(2,1)S(1)} %all_to_all.10.got, bf16[16,4,8,128]{3,2,1,0:T(8,128)(2,1)S(1)} %collective-permute-done.halo_l, ...), custom_call_target="tpu_custom_call" | custom-call | flops 4000000000 | bytes 4194304 | tf_op jit(solution)/shard_map/pallas_call | solution.py:195
  56.3 0.0 collective-permute-done.3.from_l
  56.3 0.3 collective-permute-done.4.from_r
  56.6 0.0 copy-done.1
  56.6 1.7 %shard_map.96 = (bf16[4,384,256]{2,1,0:T(8,128)(2,1)S(1)}, f32[16,8,8,128]{3,2,1,0:T(8,128)S(1)}, bf16[16,2,8,128]{3,2,1,0:T(8,128)(2,1)S(1)}, bf16[16,2,8,128]{3,2,1,0:T(8,128)(2,1)S(1)}) custom-call(s32[7]{0:T(128)S(1)} %stack.58.scal, f32[4,128,256]{2,1,0:T(8,128)S(1)} %get-tuple-element.19.hid, f32[128,256]{1,0:T(8,128)S(1)} %collective-permute-done.3.from_l, ...), custom_call_target="tpu_custom_call" | custom-call | flops 2000000000 | bytes 4194304 | tf_op jit(solution)/shard_map/pallas_call | solution.py:195
  58.3 1.9 %collective-permute-start.6 = (bf16[16,2,8,128]{3,2,1,0:T(8,128)(2,1)S(1)}, bf16[16,2,8,128]{3,2,1,0:T(8,128)(2,1)S(1)}, u32[]{:S(2)}, u32[]{:S(2)}) collective-permute-start(bf16[16,2,8,128]{3,2,1,0:T(8,128)(2,1)S(1)} %get-tuple-element.27), channel_id=1, source_target_pairs={{0,16},{16,32},{32,48},{48,64},{64,80},{80,96},{96,112},{112,128},... | collective-permute-start | bytes 196616 | tf_op jit(solution)/shard_map/ppermute | solution.py:269
  60.2 1.7 %collective-permute-start.7 = (bf16[16,2,8,128]{3,2,1,0:T(8,128)(2,1)S(1)}, bf16[16,2,8,128]{3,2,1,0:T(8,128)(2,1)S(1)}, u32[]{:S(2)}, u32[]{:S(2)}) collective-permute-start(bf16[16,2,8,128]{3,2,1,0:T(8,128)(2,1)S(1)} %get-tuple-element.28), channel_id=1, source_target_pairs={{16,0},{32,16},{48,32},{64,48},{80,64},{96,80},{112,96},{128,112},... | collective-permute-start | bytes 196616 | tf_op jit(solution)/shard_map/ppermute | solution.py:270
  61.9 5.2 %shard_map.97 = (f32[8,128,128]{2,1,0:T(8,128)S(1)}, bf16[8,128,128]{2,1,0:T(8,128)(2,1)S(1)}) custom-call(s32[7]{0:T(128)S(1)} %stack.58.scal, bf16[16,32,8,128]{3,2,1,0:T(8,128)(2,1)S(1)} %all_to_all.10.got, bf16[16,4,8,128]{3,2,1,0:T(8,128)(2,1)S(1)} %collective-permute-done.halo_l, bf16[16,4,8,128]{3,2,1,0:T(8,128)(2,1)S(1)} %collective-permute-done.1.halo_r, ...), custom_call_target="tpu_custom_call" | custom-call | flops 2000000000 | bytes 4194304 | tf_op jit(solution)/shard_map/pallas_call | solution.py:195
  67.1 3.8 %collective-permute-start.5 = (bf16[8,128,128]{2,1,0:T(8,128)(2,1)S(1)}, bf16[8,128,128]{2,1,0:T(8,128)(2,1)S(1)}, u32[]{:S(2)}, u32[]{:S(2)}) collective-permute-start(bf16[8,128,128]{2,1,0:T(8,128)(2,1)S(1)} %get-tuple-element.25), channel_id=1, source_target_pairs={{0,16},{16,0},{1,17},{17,1},{2,18},{18,2},{3,19},{19,3},{4,20},{20... | collective-permute-start | bytes 786440 | tf_op jit(solution)/shard_map/ppermute | solution.py:266
  70.9 0.1 collective-permute-start.2
  71.0 0.0 collective-permute-done.6
  71.0 0.0 collective-permute-done.7
  71.1 1.0 collective-permute-done.5
  72.1 0.1 fusion.1
  72.1 0.7 collective-permute-done.2
  72.8 0.1 fusion
  73.0 0.1 copy_bitcast_fusion
  73.1 0.2 pad_maximum_fusion.1
  73.3 28.7 %all_to_all.11 = bf16[16,30,8,128]{3,2,1,0:T(8,128)(2,1)S(1)} all-to-all(bf16[16,30,8,128]{3,2,1,0:T(8,128)(2,1)S(1)} %pad_maximum_fusion.1), channel_id=1, replica_groups=mesh['x'=4,'zl'=2,'core'=2,'y'=4,'zh'=4] {'y','zh'}, dimensions={0} | all-to-all | bytes 1966080 | tf_op jit(solution)/shard_map/all_to_all | solution.py:275
  102.0 0.2 copy.89
  102.2 0.1 convert_reduce_fusion
  102.3 0.1 collective-permute-start.8
  102.5 3.3 %collective-permute-done.8 = f32[22,8,128]{2,1,0:T(8,128)S(1)} collective-permute-done((f32[22,8,128]{2,1,0:T(8,128)S(1)}, f32[22,8,128]{2,1,0:T(8,128)S(1)}, u32[]{:S(2)}, u32[]{:S(2)}) %collective-permute-start.8) | collective-permute-done | bytes 90144 | tf_op jit(solution)/shard_map/ppermute | solution.py:284
  105.8 0.1 collective-permute-start.9
  105.9 3.3 %collective-permute-done.9 = f32[22,8,128]{2,1,0:T(8,128)S(1)} collective-permute-done((f32[22,8,128]{2,1,0:T(8,128)S(1)}, f32[22,8,128]{2,1,0:T(8,128)S(1)}, u32[]{:S(2)}, u32[]{:S(2)}) %collective-permute-start.9) | collective-permute-done | bytes 90144 | tf_op jit(solution)/shard_map/ppermute | solution.py:285
  109.3 1.8 %collective-permute-start.10 = (f32[22,8,128]{2,1,0:T(8,128)S(1)}, f32[22,8,128]{2,1,0:T(8,128)S(1)}, u32[]{:S(2)}, u32[]{:S(2)}) collective-permute-start(f32[22,8,128]{2,1,0:T(8,128)S(1)} %add.54), channel_id=1, source_target_pairs={{0,128},{64,192},{128,0},{192,64},{1,129},{65,193},{129,1},{193,65... | collective-permute-start | bytes 270344 | tf_op jit(solution)/shard_map/ppermute | solution.py:286
  111.1 0.9 copy.82
  112.0 2.7 %collective-permute-done.10 = f32[22,8,128]{2,1,0:T(8,128)S(1)} collective-permute-done((f32[22,8,128]{2,1,0:T(8,128)S(1)}, f32[22,8,128]{2,1,0:T(8,128)S(1)}, u32[]{:S(2)}, u32[]{:S(2)}) %collective-permute-start.10) | collective-permute-done | bytes 90144 | tf_op jit(solution)/shard_map/ppermute | solution.py:286
  114.7 5.7 %all-gather = f32[44,8,128]{2,1,0:T(8,128)S(1)} all-gather(f32[22,8,128]{2,1,0:T(8,128)S(1)} %add_multiply_fusion), channel_id=2, replica_groups=mesh['x'=4,'zl'=2,'core'=2,'y'=4,'zh'=4] {'core'}, dimensions={0}, use_global_device_ids=true | all-gather | bytes 270336 | tf_op jit(solution)/shard_map/all_gather | solution.py:288
  120.4 0.1 reshape.59
  120.6 0.1 copy.84
  120.8 0.8 reshape.61
  121.6 0.2 copy.85
  121.8 0.9 reshape.62
  (25 shorter events, 0.5 us)
Async XLA Ops:
  0.6 2.3 %copy-start.2 = (bf16[8,4,32,128]{3,2,1,0:T(8,128)(2,1)S(1)}, bf16[8,4,32,128]{3,2,1,0:T(8,128)(2,1)}, u32[]{:S(2)}) copy-start(bf16[8,4,32,128]{3,2,1,0:T(8,128)(2,1)} %param.9) | copy-start | bytes 786436
  3.6 44.5 %copy-start = (bf16[27,128,128]{2,1,0:T(8,128)(2,1)S(1)}, bf16[27,128,128]{2,1,0:T(8,128)(2,1)}, u32[]{:S(2)}) copy-start(bf16[27,128,128]{2,1,0:T(8,128)(2,1)} %w_two.1) | copy-start | bytes 2654212
  42.7 7.7 %collective-permute-start.1 = (bf16[16,4,8,128]{3,2,1,0:T(8,128)(2,1)S(1)}, bf16[16,4,8,128]{3,2,1,0:T(8,128)(2,1)S(1)}, u32[]{:S(2)}, u32[]{:S(2)}) collective-permute-start(bf16[16,4,8,128]{3,2,1,0:T(8,128)(2,1)S(1)} %get-tuple-element.29), channel_id=1, source_target_pairs={{16,0},{32,16},{48,32},{64,48},{80,64},{96,80},{112,96},{128,112},... | collective-permute-start | bytes 393224 | tf_op jit(solution)/shard_map/ppermute | solution.py:225
  46.7 3.6 %collective-permute-start = (bf16[16,4,8,128]{3,2,1,0:T(8,128)(2,1)S(1)}, bf16[16,4,8,128]{3,2,1,0:T(8,128)(2,1)S(1)}, u32[]{:S(2)}, u32[]{:S(2)}) collective-permute-start(bf16[16,4,8,128]{3,2,1,0:T(8,128)(2,1)S(1)} %get-tuple-element.30), channel_id=1, source_target_pairs={{0,16},{16,32},{32,48},{48,64},{64,80},{80,96},{96,112},{112,128},... | collective-permute-start | bytes 393224 | tf_op jit(solution)/shard_map/ppermute | solution.py:224
  49.7 6.6 %collective-permute-start.3 = (f32[128,256]{1,0:T(8,128)S(1)}, f32[128,256]{1,0:T(8,128)S(1)}, u32[]{:S(2)}, u32[]{:S(2)}) collective-permute-start(f32[128,256]{1,0:T(8,128)S(1)} %get-tuple-element.20), channel_id=1, source_target_pairs={{0,16},{16,32},{32,48},{48,64},{64,80},{80,96},{96,112},{112,128},... | collective-permute-start | bytes 393224 | tf_op jit(solution)/shard_map/ppermute | solution.py:238
  49.8 6.8 %collective-permute-start.4 = (f32[128,256]{1,0:T(8,128)S(1)}, f32[128,256]{1,0:T(8,128)S(1)}, u32[]{:S(2)}, u32[]{:S(2)}) collective-permute-start(f32[128,256]{1,0:T(8,128)S(1)} %get-tuple-element.21), channel_id=1, source_target_pairs={{16,0},{32,16},{48,32},{64,48},{80,64},{96,80},{112,96},{128,112},... | collective-permute-start | bytes 393224 | tf_op jit(solution)/shard_map/ppermute | solution.py:239
  50.4 6.2 %copy-start.1 = (bf16[27,64,128]{2,1,0:T(8,128)(2,1)S(1)}, bf16[27,64,128]{2,1,0:T(8,128)(2,1)}, u32[]{:S(2)}) copy-start(bf16[27,64,128]{2,1,0:T(8,128)(2,1)} %w_one.1) | copy-start | bytes 1327108
  58.3 12.8 %collective-permute-start.6 = (bf16[16,2,8,128]{3,2,1,0:T(8,128)(2,1)S(1)}, bf16[16,2,8,128]{3,2,1,0:T(8,128)(2,1)S(1)}, u32[]{:S(2)}, u32[]{:S(2)}) collective-permute-start(bf16[16,2,8,128]{3,2,1,0:T(8,128)(2,1)S(1)} %get-tuple-element.27), channel_id=1, source_target_pairs={{0,16},{16,32},{32,48},{48,64},{64,80},{80,96},{96,112},{112,128},... | collective-permute-start | bytes 196616 | tf_op jit(solution)/shard_map/ppermute | solution.py:269
  60.2 10.8 %collective-permute-start.7 = (bf16[16,2,8,128]{3,2,1,0:T(8,128)(2,1)S(1)}, bf16[16,2,8,128]{3,2,1,0:T(8,128)(2,1)S(1)}, u32[]{:S(2)}, u32[]{:S(2)}) collective-permute-start(bf16[16,2,8,128]{3,2,1,0:T(8,128)(2,1)S(1)} %get-tuple-element.28), channel_id=1, source_target_pairs={{16,0},{32,16},{48,32},{64,48},{80,64},{96,80},{112,96},{128,112},... | collective-permute-start | bytes 196616 | tf_op jit(solution)/shard_map/ppermute | solution.py:270
  67.1 5.0 %collective-permute-start.5 = (bf16[8,128,128]{2,1,0:T(8,128)(2,1)S(1)}, bf16[8,128,128]{2,1,0:T(8,128)(2,1)S(1)}, u32[]{:S(2)}, u32[]{:S(2)}) collective-permute-start(bf16[8,128,128]{2,1,0:T(8,128)(2,1)S(1)} %get-tuple-element.25), channel_id=1, source_target_pairs={{0,16},{16,0},{1,17},{17,1},{2,18},{18,2},{3,19},{19,3},{4,20},{20... | collective-permute-start | bytes 786440 | tf_op jit(solution)/shard_map/ppermute | solution.py:266
  70.9 1.9 %collective-permute-start.2 = (bf16[14,128,128]{2,1,0:T(8,128)(2,1)S(1)}, bf16[14,128,128]{2,1,0:T(8,128)(2,1)S(1)}, u32[]{:S(2)}, u32[]{:S(2)}) collective-permute-start(bf16[14,128,128]{2,1,0:T(8,128)(2,1)S(1)} %get-tuple-element.18), channel_id=1, source_target_pairs={{0,16},{16,0},{1,17},{17,1},{2,18},{18,2},{3,19},{19,3},{4,20},{20... | collective-permute-start | bytes 1376264 | tf_op jit(solution)/shard_map/ppermute | solution.py:265
  102.3 3.5 %collective-permute-start.8 = (f32[22,8,128]{2,1,0:T(8,128)S(1)}, f32[22,8,128]{2,1,0:T(8,128)S(1)}, u32[]{:S(2)}, u32[]{:S(2)}) collective-permute-start(f32[22,8,128]{2,1,0:T(8,128)S(1)} %convert_reduce_fusion), channel_id=1, source_target_pairs={{0,32},{32,0},{1,33},{33,1},{2,34},{34,2},{3,35},{35,3},{4,36},{36... | collective-permute-start | bytes 270344 | tf_op jit(solution)/shard_map/ppermute | solution.py:284
  105.8 3.5 %collective-permute-start.9 = (f32[22,8,128]{2,1,0:T(8,128)S(1)}, f32[22,8,128]{2,1,0:T(8,128)S(1)}, u32[]{:S(2)}, u32[]{:S(2)}) collective-permute-start(f32[22,8,128]{2,1,0:T(8,128)S(1)} %add.53), channel_id=1, source_target_pairs={{0,64},{64,0},{128,192},{192,128},{1,65},{65,1},{129,193},{193,129... | collective-permute-start | bytes 270344 | tf_op jit(solution)/shard_map/ppermute | solution.py:285
  109.3 5.4 %collective-permute-start.10 = (f32[22,8,128]{2,1,0:T(8,128)S(1)}, f32[22,8,128]{2,1,0:T(8,128)S(1)}, u32[]{:S(2)}, u32[]{:S(2)}) collective-permute-start(f32[22,8,128]{2,1,0:T(8,128)S(1)} %add.54), channel_id=1, source_target_pairs={{0,128},{64,192},{128,0},{192,64},{1,129},{65,193},{129,1},{193,65... | collective-permute-start | bytes 270344 | tf_op jit(solution)/shard_map/ppermute | solution.py:286

commit v3 on v2

--- a/solution.py
+++ b/solution.py
@@ -50,17 +50,15 @@
     return ref[:, t].astype(F32).reshape(128, X)
 
 
-def store_halves(core, mine, theirs, s, step, slab):
+def store_halves(core, mine, theirs, s, count, step, slab):
     for me in range(2):
 
         @pl.when(core == me)
         def _():
             for half in range(2):
-                if 0 <= s - half * step <= step:
-                    if half == me:
-                        mine[s - half * step] = slab
-                    else:
-                        theirs[s - half * step] = slab.astype(BF16)
+                if 0 <= s - half * step < count:
+                    dst = mine if half == me else theirs
+                    dst[s - half * step] = slab.astype(dst.dtype)
 
 
 def kernel_a(got, w_two, g3, own, left, right, wk):
@@ -99,17 +97,19 @@
             elif w == Z:
                 pre = jnp.where(scal[6] > 0, pre, 0.0)
             scale = kept_scale(offset, seed, z0 + w, h0 + r)
-            act[w + 1, :, r * X : (r + 1) * X] = (jnp.maximum(pre, 0.0) * scale).astype(BF16)
+            cols = slice(r * X, (r + 1) * X)
+            act[(w + 1) * MID : (w + 2) * MID, cols] = (jnp.maximum(pre, 0.0) * scale).astype(BF16)
             if 0 <= w < Z:
-                mask[w, :, r * X : (r + 1) * X] = jnp.where(pre > 0, scale, 0.0).astype(BF16)
-    for q in range(9):
-        kd, kh = divmod(q, 3)
+                mask[w, :, cols] = jnp.where(pre > 0, scale, 0.0).astype(BF16)
+    for kh in range(3):
         total = None
         for s in range(Z):
-            part = dot_t(g3[s, :, (2 - kh) * X : (4 - kh) * X], act[s + kd])
+            part = dot_t(g3[s, :, (2 - kh) * X : (4 - kh) * X], act[s * MID : (s + 3) * MID])
             total = part if total is None else total + part
-        for kw in range(3):
-            store_halves(core, mine, theirs, 3 * q + kw, 13, total[kw * 128 : (kw + 1) * 128])
+        for kd in range(3):
+            for kw in range(3):
+                slab = total[kw * 128 : (kw + 1) * 128, kd * MID : (kd + 1) * MID]
+                store_halves(core, mine, theirs, 9 * kd + 3 * kh + kw, 14, 13, slab)
 
 
 def shuffle(back):
@@ -157,10 +157,8 @@
                 fout[:, 2 * w + i] = tiles.reshape(16, 8, X)
 
 
-def kernel_d(scal, got, halo_l, halo_r, p3, mine, theirs, lo, hi):
+def kernel_d(scal, got, halo_l, halo_r, p3, mine, theirs, feat):
     core = scal[4]
-    lo[...] = jnp.zeros_like(lo)
-    hi[...] = jnp.zeros_like(hi)
     order = shuffle(False)
     for w in range(-1, Z + 1):
         for i in range(2):
@@ -170,22 +168,21 @@
                 rows = jnp.where(scal[5] > 0, rows, 0.0)
             elif w == Z:
                 rows = jnp.where(scal[6] > 0, rows, 0.0)
-            rows = rows.astype(BF16)
             for r in range(2):
                 cols = slice((2 * i + r) * X, (2 * i + r + 1) * X)
-                lo[w + 1, 0:CIN, cols] = rows[r * CIN : (r + 1) * CIN]
-                hi[w + 1, CIN:, cols] = rows[r * CIN : (r + 1) * CIN]
-    for q in range(5):
+                feat[(w + 1) * CIN : (w + 2) * CIN, cols] = rows[r * CIN : (r + 1) * CIN].astype(BF16)
+    last = []
+    for kh in range(3):
         total = None
         for s in range(Z):
-            for tap, rhs in ((q, lo), (q + 5, hi)):
-                if tap > 8:
-                    continue
-                kd, kh = divmod(tap, 3)
-                part = dot_t(p3[s], rhs[s + kd, :, kh * X : (kh + 2) * X])
-                total = part if total is None else total + part
+            part = dot_t(p3[s], feat[s * CIN : (s + 3) * CIN, kh * X : (kh + 2) * X])
+            total = part if total is None else total + part
         for kw in range(3):
-            store_halves(core, mine, theirs, 3 * q + kw, 7, total[kw * 128 : (kw + 1) * 128])
+            store_halves(core, mine, theirs, 3 * kh + kw, 7, 7, total[kw * 128 : (kw + 1) * 128, : 2 * CIN])
+            last.append(total[kw * 128 : (kw + 1) * 128, 2 * CIN :])
+    last.append(jnp.zeros((128, CIN), F32))
+    for b in range(5):
+        store_halves(core, mine, theirs, 9 + b, 7, 7, jnp.concatenate([last[b], last[b + 5]], axis=1))
 
 
 VMEM, SMEM = pl.BlockSpec(memory_space=pltpu.VMEM), pl.BlockSpec(memory_space=pltpu.SMEM)
@@ -241,7 +238,7 @@
         kernel_b,
         (scal, got, halo_l, halo_r, g3),
         [((Z, MID, R * X), BF16), ((14, 128, 128), F32), ((14, 128, 128), BF16)],
-        [((Z + 2, MID, R * X), BF16)],
+        [(((Z + 2) * MID, R * X), BF16)],
         4 * 10**9,
         1,
     )
@@ -256,15 +253,15 @@
     mine_one, theirs_one = call(
         kernel_d,
         (scal, got, halo_l, halo_r, p3),
-        [((8, 128, 128), F32), ((8, 128, 128), BF16)],
-        [((Z + 2, 128, 4 * X), BF16), ((Z + 2, 128, 4 * X), BF16)],
+        [((7, 128, 128), F32), ((7, 128, 128), BF16)],
+        [(((Z + 2) * CIN, 4 * X), BF16)],
         2 * 10**9,
         1,
     )
 
     mine_two = mine_two + lax.ppermute(theirs_two, "core", swap).astype(F32)
     mine_one = mine_one + lax.ppermute(theirs_one, "core", swap).astype(F32)
-    mine = jnp.concatenate([mine_two, mine_one]).astype(BF16).reshape(22, 16, 8, 128).transpose(1, 0, 2, 3)
+    mine = jnp.concatenate([mine_two, mine_one]).astype(BF16).reshape(21, 16, 8, 128).transpose(1, 0, 2, 3)
     feature_l, feature_r = (
         jnp.where(has_l, lax.ppermute(feature_r, SLAB, up).astype(F32), 0.0),
         jnp.where(has_r, lax.ppermute(feature_l, SLAB, down).astype(F32), 0.0),
@@ -274,22 +271,22 @@
     ).astype(BF16)
     got = lax.all_to_all(jnp.concatenate([mine, feature], axis=1), CHAN, 0, 0, tiled=True)
 
-    rows = got[:, 22:].astype(F32).reshape(16, Z, 4, 4, X)
+    rows = got[:, 21:].astype(F32).reshape(16, Z, 4, 4, X)
     none = jnp.zeros((1, Z, 4, X), F32)
     first = rows[:, :, 1] + jnp.concatenate([none, rows[:-1, :, 3]])
     second = rows[:, :, 2] + jnp.concatenate([rows[1:, :, 0], none])
     feature = jnp.stack([first, second], axis=2).transpose(3, 1, 0, 2, 4).reshape(4, Z, NY, X)
 
-    part = got[:, :22].astype(F32).sum(axis=0)
+    part = got[:, :21].astype(F32).sum(axis=0)
     part = part + lax.ppermute(part, "zl", swap)
     part = part + lax.ppermute(part, "x", [(i, i ^ 1) for i in range(4)])
     part = part + lax.ppermute(part, "x", [(i, i ^ 2) for i in range(4)])
     scale = 1.0 / math.sqrt(NZ * NY * X)
     total = lax.all_gather(part * scale, "core", axis=0, tiled=False)
     two = jnp.concatenate([total[0, :14], total[1, 1:14]])
-    one = jnp.concatenate([total[0, 14:], total[1, 15:]])
+    one = total[:, 14:].reshape(14, 8, 2, CIN)
+    one = jnp.concatenate([one[:9, :, 0], one[:9, :, 1], one[9:, :, 0], one[9:13, :, 1]])
     two = two.transpose(1, 2, 0).reshape(8, 27 * MID)
-    one = one.reshape(5, 3, 8, 2, CIN).transpose(3, 0, 1, 2, 4).reshape(30, 8, CIN)[:27]
     one = one.transpose(1, 2, 0).reshape(4, 54 * CIN)
     return feature, one, two
 

time: 123 us -> 117 us (0.951)
  Pallas kernels: 14.3 us -> 8.74 us
  waiting for transfers between devices: 11.3 us -> 12.6 us
    pallas_call x4, Pallas kernels: 14.3 us -> 8.74 us  [call(): pl.pallas_call(body, out_shape=tuple((jax.ShapeDtypeStruct(shape, kind) f...]
    ppermute x1, waiting for transfers between devices: 0.3 us -> 3.34 us  [shards(): from_r = lax.ppermute(left, SLAB, down)]
    ppermute x1, starting transfers between devices: 1.95 us -> 0.08 us  [shards(): lax.ppermute(feature_r, SLAB, up).astype(F32)]
    ppermute x1, waiting for transfers between devices: 2.71 us -> 1.26 us  [shards(): part = part + lax.ppermute(part, 'x', [(i, i ^ 2) for i in range(4)])]
    ppermute x1, starting transfers between devices: 1.77 us -> 3.05 us  [shards(): part = part + lax.ppermute(part, 'x', [(i, i ^ 2) for i in range(4)])]
  transfers between devices with their start and end apart: 11 -> 11, of which waited for: 6 -> 6; matrix products, arithmetic and copies ran while one was open for 1% -> 1% of each run, Pallas kernels for 10% -> 6%
where the time goes in v3:
time: 117 us
  blocking collectives  72.4 us (62%)
  starting transfers between devices  13.5 us (12%)
  waiting for transfers between devices  12.6 us (11%)
  Pallas kernels  8.74 us (7%)
  local copies, waits for them, and re-layouts  6.27 us (5%)
  between operations  2.29 us (2%)
    all_to_all x1, blocking collectives, shards(): lax.all_to_all(sent.reshape(16, Z * TILES, 8, X), CHAN, 0, 0, tiled=True)  39.1 us
    all_to_all x1, blocking collectives, shards(): lax.all_to_all(jnp.concatenate([mine, feature], axis=1), CHAN, 0, 0, tile...  28.1 us
    pallas_call x4, Pallas kernels, call(): pl.pallas_call(body, out_shape=tuple((jax.ShapeDtypeStruct(shape, kind) f...  8.74 us
    all_gather x1, blocking collectives, shards(): total = lax.all_gather(part * scale, 'core', axis=0, tiled=False)  5.26 us
    ppermute x1, starting transfers between devices, shards(): halo_r = lax.ppermute(got[:, 4:TILES], SLAB, down)  4.03 us
    ppermute x1, starting transfers between devices, shards(): mine_one = mine_one + lax.ppermute(theirs_one, 'core', swap).astype(F32)  3.84 us
    ppermute x1, waiting for transfers between devices, shards(): from_r = lax.ppermute(left, SLAB, down)  3.34 us
    ppermute x1, waiting for transfers between devices, shards(): part = part + lax.ppermute(part, 'x', [(i, i ^ 1) for i in range(4)])  3.28 us
  transfers between devices with their start and end apart: 11, of which 6 were waited for; matrix products, arithmetic and copies ran while one was open for 1% of the time, Pallas kernels for 6%

profile of v3, /device:TPU:1, one launch (start us, length us, event | category | flops | bytes accessed | tf_op | source)
XLA Modules:
  0.0 116.8 jit_solution(536894353391497099)
XLA Ops:
  0.6 0.0 copy-start.2
  0.6 1.1 copy.93
  1.7 0.1 pad.11.clone
  1.8 1.1 copy.70
  3.0 0.0 copy-done.2
  3.0 0.2 copy.100
  3.2 0.1 slice_bitcast_fusion.1
  3.3 0.1 maximum_bitcast_fusion
  3.5 0.1 pad_maximum_fusion
  3.6 0.0 copy-start
  3.6 39.1 %all_to_all.10.got = bf16[16,32,8,128]{3,2,1,0:T(8,128)(2,1)S(1)} all-to-all(bf16[16,32,8,128]{3,2,1,0:T(8,128)(2,1)S(1)} %bitcast.89), channel_id=1, replica_groups=mesh['x'=4,'zl'=2,'core'=2,'y'=4,'zh'=4] {'y','zh'}, dimensions={0} | all-to-all | bytes 2097152 | tf_op jit(solution)/shard_map/all_to_all | solution.py:215
  42.7 4.0 %collective-permute-start.1 = (bf16[16,4,8,128]{3,2,1,0:T(8,128)(2,1)S(1)}, bf16[16,4,8,128]{3,2,1,0:T(8,128)(2,1)S(1)}, u32[]{:S(2)}, u32[]{:S(2)}) collective-permute-start(bf16[16,4,8,128]{3,2,1,0:T(8,128)(2,1)S(1)} %get-tuple-element.29), channel_id=1, source_target_pairs={{16,0},{32,16},{48,32},{64,48},{80,64},{96,80},{112,96},{128,112},... | collective-permute-start | bytes 393224 | tf_op jit(solution)/shard_map/ppermute | solution.py:222
  46.7 0.0 collective-permute-start
  48.0 0.1 stack.58.scal
  48.1 0.0 copy-done
  48.1 1.6 %shard_map.94 = (bf16[4,384,512]{2,1,0:T(8,128)(2,1)S(1)}, f32[4,128,256]{2,1,0:T(8,128)S(1)}, f32[128,256]{1,0:T(8,128)S(1)}, f32[128,256]{1,0:T(8,128)S(1)}) custom-call(bf16[16,32,8,128]{3,2,1,0:T(8,128)(2,1)S(1)} %all_to_all.10.got, bf16[27,128,128]{2,1,0:T(8,128)(2,1)S(1)} %copy-done), custom_call_target="tpu_custom_call" | custom-call | flops 1000000000 | bytes 4194304 | tf_op jit(solution)/shard_map/pallas_call | solution.py:192
  49.7 0.1 collective-permute-start.3
  49.8 0.6 collective-permute-start.4
  50.4 0.0 collective-permute-done.1.halo_r
  50.4 0.0 collective-permute-done.halo_l
  50.4 0.0 copy-start.1
  50.4 2.9 %shard_map.95 = (bf16[4,128,256]{2,1,0:T(8,128)(2,1)S(1)}, f32[14,128,128]{2,1,0:T(8,128)S(1)}, bf16[14,128,128]{2,1,0:T(8,128)(2,1)S(1)}) custom-call(s32[7]{0:T(128)S(1)} %stack.58.scal, bf16[16,32,8,128]{3,2,1,0:T(8,128)(2,1)S(1)} %all_to_all.10.got, bf16[16,4,8,128]{3,2,1,0:T(8,128)(2,1)S(1)} %collective-permute-done.halo_l, ...), custom_call_target="tpu_custom_call" | custom-call | flops 4000000000 | bytes 4194304 | tf_op jit(solution)/shard_map/pallas_call | solution.py:192
  53.3 0.0 collective-permute-done.3.from_l
  53.3 3.3 %collective-permute-done.4.from_r = f32[128,256]{1,0:T(8,128)S(1)} collective-permute-done((f32[128,256]{1,0:T(8,128)S(1)}, f32[128,256]{1,0:T(8,128)S(1)}, u32[]{:S(2)}, u32[]{:S(2)}) %collective-permute-start.4) | collective-permute-done | bytes 131104 | tf_op jit(solution)/shard_map/ppermute | solution.py:236
  56.6 0.0 copy-done.1
  56.6 1.7 %shard_map.96 = (bf16[4,384,256]{2,1,0:T(8,128)(2,1)S(1)}, f32[16,8,8,128]{3,2,1,0:T(8,128)S(1)}, bf16[16,2,8,128]{3,2,1,0:T(8,128)(2,1)S(1)}, bf16[16,2,8,128]{3,2,1,0:T(8,128)(2,1)S(1)}) custom-call(s32[7]{0:T(128)S(1)} %stack.58.scal, f32[4,128,256]{2,1,0:T(8,128)S(1)} %get-tuple-element.19.hid, f32[128,256]{1,0:T(8,128)S(1)} %collective-permute-done.3.from_l, ...), custom_call_target="tpu_custom_call" | custom-call | flops 2000000000 | bytes 4194304 | tf_op jit(solution)/shard_map/pallas_call | solution.py:192
  58.3 0.1 collective-permute-start.6
  58.4 1.4 %collective-permute-start.7 = (bf16[16,2,8,128]{3,2,1,0:T(8,128)(2,1)S(1)}, bf16[16,2,8,128]{3,2,1,0:T(8,128)(2,1)S(1)}, u32[]{:S(2)}, u32[]{:S(2)}) collective-permute-start(bf16[16,2,8,128]{3,2,1,0:T(8,128)(2,1)S(1)} %get-tuple-element.28), channel_id=1, source_target_pairs={{16,0},{32,16},{48,32},{64,48},{80,64},{96,80},{112,96},{128,112},... | collective-permute-start | bytes 196616 | tf_op jit(solution)/shard_map/ppermute | solution.py:267
  59.8 2.7 %shard_map.97 = (f32[7,128,128]{2,1,0:T(8,128)S(1)}, bf16[7,128,128]{2,1,0:T(8,128)(2,1)S(1)}) custom-call(s32[7]{0:T(128)S(1)} %stack.58.scal, bf16[16,32,8,128]{3,2,1,0:T(8,128)(2,1)S(1)} %all_to_all.10.got, bf16[16,4,8,128]{3,2,1,0:T(8,128)(2,1)S(1)} %collective-permute-done.halo_l, bf16[16,4,8,128]{3,2,1,0:T(8,128)(2,1)S(1)} %collective-permute-done.1.halo_r, ...), custom_call_target="tpu_custom_call" | custom-call | flops 2000000000 | bytes 4194304 | tf_op jit(solution)/shard_map/pallas_call | solution.py:192
  62.5 3.8 %collective-permute-start.5 = (bf16[7,128,128]{2,1,0:T(8,128)(2,1)S(1)}, bf16[7,128,128]{2,1,0:T(8,128)(2,1)S(1)}, u32[]{:S(2)}, u32[]{:S(2)}) collective-permute-start(bf16[7,128,128]{2,1,0:T(8,128)(2,1)S(1)} %get-tuple-element.25), channel_id=1, source_target_pairs={{0,16},{16,0},{1,17},{17,1},{2,18},{18,2},{3,19},{19,3},{4,20},{20... | collective-permute-start | bytes 688136 | tf_op jit(solution)/shard_map/ppermute | solution.py:263
  66.3 0.3 collective-permute-start.2
  66.6 0.0 collective-permute-done.6
  66.6 0.0 collective-permute-done.7
  66.6 0.8 collective-permute-done.5
  67.5 0.6 collective-permute-done.2
  68.1 0.1 fusion
  68.2 0.1 copy_bitcast_fusion
  68.4 0.2 pad_maximum_fusion.1
  68.5 28.1 %all_to_all.11 = bf16[16,29,8,128]{3,2,1,0:T(8,128)(2,1)S(1)} all-to-all(bf16[16,29,8,128]{3,2,1,0:T(8,128)(2,1)S(1)} %pad_maximum_fusion.1), channel_id=1, replica_groups=mesh['x'=4,'zl'=2,'core'=2,'y'=4,'zh'=4] {'y','zh'}, dimensions={0} | all-to-all | bytes 1900544 | tf_op jit(solution)/shard_map/all_to_all | solution.py:272
  96.7 0.2 copy.88
  96.8 0.1 convert_reduce_fusion
  96.9 0.1 collective-permute-start.8
  97.1 3.2 %collective-permute-done.8 = f32[21,8,128]{2,1,0:T(8,128)S(1)} collective-permute-done((f32[21,8,128]{2,1,0:T(8,128)S(1)}, f32[21,8,128]{2,1,0:T(8,128)S(1)}, u32[]{:S(2)}, u32[]{:S(2)}) %collective-permute-start.8) | collective-permute-done | bytes 86048 | tf_op jit(solution)/shard_map/ppermute | solution.py:281
  100.4 0.1 collective-permute-start.9
  100.5 3.3 %collective-permute-done.9 = f32[21,8,128]{2,1,0:T(8,128)S(1)} collective-permute-done((f32[21,8,128]{2,1,0:T(8,128)S(1)}, f32[21,8,128]{2,1,0:T(8,128)S(1)}, u32[]{:S(2)}, u32[]{:S(2)}) %collective-permute-start.9) | collective-permute-done | bytes 86048 | tf_op jit(solution)/shard_map/ppermute | solution.py:282
  103.8 3.0 %collective-permute-start.10 = (f32[21,8,128]{2,1,0:T(8,128)S(1)}, f32[21,8,128]{2,1,0:T(8,128)S(1)}, u32[]{:S(2)}, u32[]{:S(2)}) collective-permute-start(f32[21,8,128]{2,1,0:T(8,128)S(1)} %add.54), channel_id=1, source_target_pairs={{0,128},{64,192},{128,0},{192,64},{1,129},{65,193},{129,1},{193,65... | collective-permute-start | bytes 258056 | tf_op jit(solution)/shard_map/ppermute | solution.py:283
  106.9 0.9 copy.81
  107.8 1.3 %collective-permute-done.10 = f32[21,8,128]{2,1,0:T(8,128)S(1)} collective-permute-done((f32[21,8,128]{2,1,0:T(8,128)S(1)}, f32[21,8,128]{2,1,0:T(8,128)S(1)}, u32[]{:S(2)}, u32[]{:S(2)}) %collective-permute-start.10) | collective-permute-done | bytes 86048 | tf_op jit(solution)/shard_map/ppermute | solution.py:283
  109.1 5.3 %all-gather = f32[42,8,128]{2,1,0:T(8,128)S(1)} all-gather(f32[21,8,128]{2,1,0:T(8,128)S(1)} %add_multiply_fusion), channel_id=2, replica_groups=mesh['x'=4,'zl'=2,'core'=2,'y'=4,'zh'=4] {'core'}, dimensions={0}, use_global_device_ids=true | all-gather | bytes 258048 | tf_op jit(solution)/shard_map/all_gather | solution.py:285
  114.3 0.1 reshape.56
  114.5 0.1 fusion.8
  114.6 0.1 copy.83
  114.8 0.8 reshape.57
  115.6 0.2 copy.84
  115.9 0.9 reshape.58
  (25 shorter events, 0.6 us)
Async XLA Ops:
  0.6 2.3 %copy-start.2 = (bf16[8,4,32,128]{3,2,1,0:T(8,128)(2,1)S(1)}, bf16[8,4,32,128]{3,2,1,0:T(8,128)(2,1)}, u32[]{:S(2)}) copy-start(bf16[8,4,32,128]{3,2,1,0:T(8,128)(2,1)} %param.9) | copy-start | bytes 786436
  3.6 44.5 %copy-start = (bf16[27,128,128]{2,1,0:T(8,128)(2,1)S(1)}, bf16[27,128,128]{2,1,0:T(8,128)(2,1)}, u32[]{:S(2)}) copy-start(bf16[27,128,128]{2,1,0:T(8,128)(2,1)} %w_two.1) | copy-start | bytes 2654212
  42.7 7.7 %collective-permute-start.1 = (bf16[16,4,8,128]{3,2,1,0:T(8,128)(2,1)S(1)}, bf16[16,4,8,128]{3,2,1,0:T(8,128)(2,1)S(1)}, u32[]{:S(2)}, u32[]{:S(2)}) collective-permute-start(bf16[16,4,8,128]{3,2,1,0:T(8,128)(2,1)S(1)} %get-tuple-element.29), channel_id=1, source_target_pairs={{16,0},{32,16},{48,32},{64,48},{80,64},{96,80},{112,96},{128,112},... | collective-permute-start | bytes 393224 | tf_op jit(solution)/shard_map/ppermute | solution.py:222
  46.7 3.6 %collective-permute-start = (bf16[16,4,8,128]{3,2,1,0:T(8,128)(2,1)S(1)}, bf16[16,4,8,128]{3,2,1,0:T(8,128)(2,1)S(1)}, u32[]{:S(2)}, u32[]{:S(2)}) collective-permute-start(bf16[16,4,8,128]{3,2,1,0:T(8,128)(2,1)S(1)} %get-tuple-element.30), channel_id=1, source_target_pairs={{0,16},{16,32},{32,48},{48,64},{64,80},{80,96},{96,112},{112,128},... | collective-permute-start | bytes 393224 | tf_op jit(solution)/shard_map/ppermute | solution.py:221
  49.7 3.6 %collective-permute-start.3 = (f32[128,256]{1,0:T(8,128)S(1)}, f32[128,256]{1,0:T(8,128)S(1)}, u32[]{:S(2)}, u32[]{:S(2)}) collective-permute-start(f32[128,256]{1,0:T(8,128)S(1)} %get-tuple-element.20), channel_id=1, source_target_pairs={{0,16},{16,32},{32,48},{48,64},{64,80},{80,96},{96,112},{112,128},... | collective-permute-start | bytes 393224 | tf_op jit(solution)/shard_map/ppermute | solution.py:235
  49.8 6.8 %collective-permute-start.4 = (f32[128,256]{1,0:T(8,128)S(1)}, f32[128,256]{1,0:T(8,128)S(1)}, u32[]{:S(2)}, u32[]{:S(2)}) collective-permute-start(f32[128,256]{1,0:T(8,128)S(1)} %get-tuple-element.21), channel_id=1, source_target_pairs={{16,0},{32,16},{48,32},{64,48},{80,64},{96,80},{112,96},{128,112},... | collective-permute-start | bytes 393224 | tf_op jit(solution)/shard_map/ppermute | solution.py:236
  50.4 6.2 %copy-start.1 = (bf16[27,64,128]{2,1,0:T(8,128)(2,1)S(1)}, bf16[27,64,128]{2,1,0:T(8,128)(2,1)}, u32[]{:S(2)}) copy-start(bf16[27,64,128]{2,1,0:T(8,128)(2,1)} %w_one.1) | copy-start | bytes 1327108
  58.3 8.3 %collective-permute-start.6 = (bf16[16,2,8,128]{3,2,1,0:T(8,128)(2,1)S(1)}, bf16[16,2,8,128]{3,2,1,0:T(8,128)(2,1)S(1)}, u32[]{:S(2)}, u32[]{:S(2)}) collective-permute-start(bf16[16,2,8,128]{3,2,1,0:T(8,128)(2,1)S(1)} %get-tuple-element.27), channel_id=1, source_target_pairs={{0,16},{16,32},{32,48},{48,64},{64,80},{80,96},{96,112},{112,128},... | collective-permute-start | bytes 196616 | tf_op jit(solution)/shard_map/ppermute | solution.py:266
  58.4 8.2 %collective-permute-start.7 = (bf16[16,2,8,128]{3,2,1,0:T(8,128)(2,1)S(1)}, bf16[16,2,8,128]{3,2,1,0:T(8,128)(2,1)S(1)}, u32[]{:S(2)}, u32[]{:S(2)}) collective-permute-start(bf16[16,2,8,128]{3,2,1,0:T(8,128)(2,1)S(1)} %get-tuple-element.28), channel_id=1, source_target_pairs={{16,0},{32,16},{48,32},{64,48},{80,64},{96,80},{112,96},{128,112},... | collective-permute-start | bytes 196616 | tf_op jit(solution)/shard_map/ppermute | solution.py:267
  62.5 5.0 %collective-permute-start.5 = (bf16[7,128,128]{2,1,0:T(8,128)(2,1)S(1)}, bf16[7,128,128]{2,1,0:T(8,128)(2,1)S(1)}, u32[]{:S(2)}, u32[]{:S(2)}) collective-permute-start(bf16[7,128,128]{2,1,0:T(8,128)(2,1)S(1)} %get-tuple-element.25), channel_id=1, source_target_pairs={{0,16},{16,0},{1,17},{17,1},{2,18},{18,2},{3,19},{19,3},{4,20},{20... | collective-permute-start | bytes 688136 | tf_op jit(solution)/shard_map/ppermute | solution.py:263
  66.3 1.8 %collective-permute-start.2 = (bf16[14,128,128]{2,1,0:T(8,128)(2,1)S(1)}, bf16[14,128,128]{2,1,0:T(8,128)(2,1)S(1)}, u32[]{:S(2)}, u32[]{:S(2)}) collective-permute-start(bf16[14,128,128]{2,1,0:T(8,128)(2,1)S(1)} %get-tuple-element.18), channel_id=1, source_target_pairs={{0,16},{16,0},{1,17},{17,1},{2,18},{18,2},{3,19},{19,3},{4,20},{20... | collective-permute-start | bytes 1376264 | tf_op jit(solution)/shard_map/ppermute | solution.py:262
  96.9 3.4 %collective-permute-start.8 = (f32[21,8,128]{2,1,0:T(8,128)S(1)}, f32[21,8,128]{2,1,0:T(8,128)S(1)}, u32[]{:S(2)}, u32[]{:S(2)}) collective-permute-start(f32[21,8,128]{2,1,0:T(8,128)S(1)} %convert_reduce_fusion), channel_id=1, source_target_pairs={{0,32},{32,0},{1,33},{33,1},{2,34},{34,2},{3,35},{35,3},{4,36},{36... | collective-permute-start | bytes 258056 | tf_op jit(solution)/shard_map/ppermute | solution.py:281
  100.4 3.4 %collective-permute-start.9 = (f32[21,8,128]{2,1,0:T(8,128)S(1)}, f32[21,8,128]{2,1,0:T(8,128)S(1)}, u32[]{:S(2)}, u32[]{:S(2)}) collective-permute-start(f32[21,8,128]{2,1,0:T(8,128)S(1)} %add.53), channel_id=1, source_target_pairs={{0,64},{64,0},{128,192},{192,128},{1,65},{65,1},{129,193},{193,129... | collective-permute-start | bytes 258056 | tf_op jit(solution)/shard_map/ppermute | solution.py:282
  103.8 5.2 %collective-permute-start.10 = (f32[21,8,128]{2,1,0:T(8,128)S(1)}, f32[21,8,128]{2,1,0:T(8,128)S(1)}, u32[]{:S(2)}, u32[]{:S(2)}) collective-permute-start(f32[21,8,128]{2,1,0:T(8,128)S(1)} %add.54), channel_id=1, source_target_pairs={{0,128},{64,192},{128,0},{192,64},{1,129},{65,193},{129,1},{193,65... | collective-permute-start | bytes 258056 | tf_op jit(solution)/shard_map/ppermute | solution.py:283

commit v4 on v3

v4 whole, which is shorter than its diff:
```python
import math

import jax
import jax.numpy as jnp
from jax import lax
from jax.experimental import pallas as pl
from jax.experimental.pallas import tpu as pltpu
from jax.sharding import Mesh
from jax.sharding import PartitionSpec as P

BF16, F32 = jnp.bfloat16, jnp.float32
CHAN, SLAB = ("y", "zh"), ("x", "zl", "core")
Z, R, X = 4, 2, 128
NZ, NY = 64, 32
MID, CIN = 128, 64
PRE, GRAD, FEAT = (0, 20, 22, 18), 2, 24


def kept_scale(offset, seed, z, h):
    c = lax.broadcasted_iota(jnp.int32, (MID, X), 0)
    w = lax.broadcasted_iota(jnp.int32, (MID, X), 1)
    position = ((c * NZ + z) * NY + h) * X + w
    m = (position + offset) ^ seed
    m = m * jnp.int32(739982445)
    m = m ^ lax.shift_right_logical(m, jnp.int32(15))
    m = m * jnp.int32(695938361)
    m = m ^ lax.shift_right_logical(m, jnp.int32(12))
    return jnp.where((m & 65535) < 52429, F32(1.25), F32(0.0))


def store_shifts(dst, plane, row, block):
    lane = lax.broadcasted_iota(jnp.int32, block.shape, 1)
    cols = slice(row * X, (row + 1) * X)
    ahead = jnp.where(lane == X - 1, 0.0, pltpu.roll(block, X - 1, 1))
    behind = jnp.where(lane == 0, 0.0, pltpu.roll(block, 1, 1))
    dst[plane, 0:128, cols] = ahead.astype(BF16)
    dst[plane, 128:256, cols] = block.astype(BF16)
    dst[plane, 256:384, cols] = behind.astype(BF16)


def dot(a, b):
    return lax.dot_general(a, b, (((1,), (0,)), ((), ())), preferred_element_type=F32)


def dot_t(a, b):
    return lax.dot_general(a, b, (((1,), (1,)), ((), ())), preferred_element_type=F32)


def tile(ref, t):
    return ref[:, t].astype(F32).reshape(128, X)


def store_halves(core, mine, theirs, s, count, step, slab):
    for me in range(2):

        @pl.when(core == me)
        def _():
            for half in range(2):
                if 0 <= s - half * step < count:
                    dst = mine if half == me else theirs
                    dst[s - half * step] = slab.astype(dst.dtype)


def shuffle(back):
    i = lax.broadcasted_iota(jnp.int32, (128, 128), 1 if back else 0)
    j = lax.broadcasted_iota(jnp.int32, (128, 128), 0 if back else 1)
    at = (lax.rem(i, 64) // 4) * 8 + (i // 64) * 4 + lax.rem(i, 4)
    return jnp.where(at == j, F32(1.0), F32(0.0)).astype(BF16)


def scaled(scal, pre, w, r):
    scale = kept_scale(scal[2], scal[3], scal[0] + w, scal[1] + r)
    return (jnp.maximum(pre, 0.0) * scale).astype(BF16), jnp.where(pre > 0, scale, 0.0)


def kernel_s(grad_in, pre_in, feat_in, sent, grad, pre, feat, rows8, rows4, sems):
    copies = [
        pltpu.make_async_copy(src, dst, sems.at[i])
        for i, (src, dst) in enumerate(((grad_in, grad), (pre_in, pre), (feat_in, feat)))
    ]
    for copy in copies:
        copy.start()
    sent[0, GRAD : GRAD + 4 * Z] = jnp.zeros((4 * Z, 8, X), BF16)
    sent[15, GRAD : GRAD + 4 * Z] = jnp.zeros((4 * Z, 8, X), BF16)
    rows4[...] = jnp.zeros_like(rows4)
    copies[0].wait()
    for z in range(Z):
        for c in range(8):
            rows8[z, pl.ds(c, NY, stride=8), :] = grad[c, z].astype(F32)
        rows = rows8[z].reshape(16, 2, 8, X).astype(BF16)
        at = GRAD + 4 * z
        sent[1:, at] = rows[:-1, 1]
        sent[:, at + 1] = rows[:, 0]
        sent[:, at + 2] = rows[:, 1]
        sent[:-1, at + 3] = rows[1:, 0]
    copies[1].wait()
    copies[2].wait()
    for z in range(Z):
        for c in range(8):
            rows8[Z + z, pl.ds(c, NY, stride=8), :] = pre[c, z].astype(F32)
        rows = rows8[Z + z].reshape(16, 2, 8, X).astype(BF16)
        sent[:, PRE[z]] = rows[:, 0]
        sent[:, PRE[z] + 1] = rows[:, 1]
        for c in range(4):
            rows4[z, pl.ds(4 + c, NY, stride=4), :] = feat[c, z].astype(F32)
        rows = rows4[z].reshape(17, 8, X).astype(BF16)
        sent[:, FEAT + 2 * z] = rows[:-1]
        sent[:, FEAT + 2 * z + 1] = rows[1:]


def add_feature_terms(fin, wf, rows, plane):
    first, end = max(0, 1 - plane), min(3, Z + 1 - plane)
    terms = dot(wf[first * 3 * CIN : end * 3 * CIN], rows)
    for kd in range(first, end):
        for kh in range(3):
            at = ((kd - first) * 3 + kh) * CIN
            cols = slice(kh * X, (kh + 2) * X)
            fin[plane - 1 + kd, :, cols] = fin[plane - 1 + kd, :, cols] + terms[at : at + CIN]


def raw_one_terms(feat, planes, total, kh):
    for plane, rows in planes:
        part = dot_t(rows, feat[(plane + 1) * CIN : (plane + 4) * CIN, kh * X : (kh + 2) * X])
        total = part if total is None else total + part
    return total


def kernel_a(scal, got, w_two, w_one, g3, hid, mask, two, wk, feat, wf, fin, one, act, p3):
    for kd in range(3):
        for kh in range(3):
            for kw in range(3):
                wk[kh, kd * MID : (kd + 1) * MID, kw * 128 : (kw + 1) * 128] = w_two[9 * kd + 3 * kh + kw]
    for z in range(Z):
        for r in range(4):
            store_shifts(g3, z, r, tile(got, GRAD + 4 * z + r))
    hid[...] = jnp.zeros_like(hid)
    for z in range(Z):
        total = None
        for kh in range(3):
            part = dot(wk[kh], g3[z, :, (2 - kh) * X : (4 - kh) * X])
            total = part if total is None else total + part
        for kd in range(3):
            hid[z + kd] = hid[z + kd] + total[kd * MID : (kd + 1) * MID]
    act[...] = jnp.zeros_like(act)
    for w in range(Z):
        for r in range(R):
            cols = slice(r * X, (r + 1) * X)
            hidden, kept = scaled(scal, tile(got, PRE[w] + r), w, r)
            act[(w + 1) * MID : (w + 2) * MID, cols] = hidden
            mask[w, :, cols] = kept.astype(BF16)
    for kh in range(3):
        total = None
        for s in range(Z):
            part = dot_t(g3[s, :, (2 - kh) * X : (4 - kh) * X], act[s * MID : (s + 3) * MID])
            total = part if total is None else total + part
        two[kh] = total
    order = shuffle(False)
    feat[...] = jnp.zeros_like(feat)
    for w in range(Z):
        for i in range(2):
            rows = dot(order, tile(got, FEAT + 2 * w + i).astype(BF16)).astype(BF16)
            for r in range(2):
                cols = slice((2 * i + r) * X, (2 * i + r + 1) * X)
                feat[(w + 2) * CIN : (w + 3) * CIN, cols] = rows[r * CIN : (r + 1) * CIN]
    for kd in range(3):
        for kh in range(3):
            for kw in range(3):
                at = (kd * 3 + kh) * CIN
                wf[at : at + CIN, kw * 128 : (kw + 1) * 128] = w_one[9 * kd + 3 * kh + kw]
    fin[...] = jnp.zeros_like(fin)
    for at, z in enumerate((1, 2)):
        for r in range(R):
            cols = slice(r * X, (r + 1) * X)
            store_shifts(p3, at, r, hid[z + 1, :, cols] * mask[z, :, cols].astype(F32))
        add_feature_terms(fin, wf, p3[at], z)
    for kh in range(3):
        one[kh] = raw_one_terms(feat, ((1, p3[0]), (2, p3[1])), None, kh)


def kernel_c(
    scal, halo_l, halo_r, g3, part_hid, mask, part_two, wk, feat, wf, part_fin, part_one,
    fout, mine, theirs, mine_one, theirs_one, g, hid, act, p3, fin,
):
    core, has_l, has_r = scal[4], scal[5] > 0, scal[6] > 0
    for at in range(4):
        for r in range(4):
            if at < 2:
                store_shifts(g, at, r, jnp.where(has_l, tile(halo_l, 4 * at + r), 0.0))
            else:
                store_shifts(g, at, r, jnp.where(has_r, tile(halo_r, 4 * at - 6 + r), 0.0))
    hid[...] = part_hid[...]
    for at, plane, first, end in ((0, -2, 2, 3), (1, -1, 1, 3), (2, 4, 0, 2), (3, 5, 0, 1)):
        total = None
        for kh in range(3):
            part = dot(wk[kh, first * MID : end * MID], g[at, :, (2 - kh) * X : (4 - kh) * X])
            total = part if total is None else total + part
        for kd in range(first, end):
            hid[plane + kd] = hid[plane + kd] + total[(kd - first) * MID : (kd - first + 1) * MID]
    outer = (-1, 0, Z - 1, Z)
    for at, plane in enumerate(outer):
        j = plane + 1
        for r in range(R):
            cols = slice(r * X, (r + 1) * X)
            if j == 0:
                hidden, kept = scaled(scal, jnp.where(has_l, tile(halo_l, 8 + r), 0.0), -1, r)
                act[0, :, cols] = hidden
            elif j == Z + 1:
                hidden, kept = scaled(scal, jnp.where(has_r, tile(halo_r, r), 0.0), Z, r)
                act[1, :, cols] = hidden
            else:
                kept = mask[j - 1, :, cols].astype(F32)
            store_shifts(p3, at, r, hid[j, :, cols] * kept)
    for kh in range(3):
        rows = slice((2 - kh) * X, (4 - kh) * X)
        low = dot_t(g3[0, :, rows], act[0])
        high = dot_t(g3[Z - 1, :, rows], act[1])
        for kd in range(3):
            for kw in range(3):
                slab = part_two[kh, kw * 128 : (kw + 1) * 128, kd * MID : (kd + 1) * MID]
                if kd != 1:
                    slab = slab + (low if kd == 0 else high)[kw * 128 : (kw + 1) * 128]
                store_halves(core, mine, theirs, 9 * kd + 3 * kh + kw, 14, 13, slab)
    fin[...] = part_fin[...]
    for at, plane in enumerate(outer):
        add_feature_terms(fin, wf, p3[at], plane)
    back = shuffle(True)
    for w in range(Z):
        for i in range(2):
            rows = jnp.concatenate([fin[w, :, (2 * i + r) * X : (2 * i + r + 1) * X] for r in range(2)], axis=0)
            fout[:, 2 * w + i] = dot(back, rows.astype(BF16)).reshape(16, 8, X).astype(BF16)
    last = []
    for kh in range(3):
        total = raw_one_terms(feat, [(plane, p3[at]) for at, plane in enumerate(outer)], part_one[kh], kh)
        for kw in range(3):
            store_halves(core, mine_one, theirs_one, 3 * kh + kw, 7, 7, total[kw * 128 : (kw + 1) * 128, : 2 * CIN])
            last.append(total[kw * 128 : (kw + 1) * 128, 2 * CIN :])
    last.append(jnp.zeros((128, CIN), F32))
    for b in range(5):
        store_halves(core, mine_one, theirs_one, 9 + b, 7, 7, jnp.concatenate([last[b], last[b + 5]], axis=1))


VMEM, SMEM = pl.BlockSpec(memory_space=pltpu.VMEM), pl.BlockSpec(memory_space=pltpu.SMEM)


def call(body, args, outs, scratch, flops, scalars):
    return pl.pallas_call(
        body,
        out_shape=tuple(jax.ShapeDtypeStruct(shape, kind) for shape, kind in outs),
        in_specs=[SMEM] * scalars + [VMEM] * (len(args) - scalars),
        out_specs=(VMEM,) * len(outs),
        scratch_shapes=[pltpu.VMEM(shape, kind) for shape, kind in scratch],
        compiler_params=pltpu.CompilerParams(vmem_limit_bytes=24 * 1024 * 1024),
        cost_estimate=pl.CostEstimate(flops=flops, bytes_accessed=4 * 1024 * 1024, transcendentals=0),
    )(*args)


def shards(features, pre_act, out_grad, weight_one, weight_two, dropout_seed, layer_offset):
    chan_pos, slab_pos, core = lax.axis_index(CHAN), lax.axis_index(SLAB), lax.axis_index("core")

    anywhere = pl.BlockSpec(memory_space=pl.ANY)
    sent = pl.pallas_call(
        kernel_s,
        out_shape=jax.ShapeDtypeStruct((16, 32, 8, X), BF16),
        in_specs=[anywhere] * 3,
        out_specs=VMEM,
        scratch_shapes=[
            pltpu.VMEM(out_grad.shape, BF16),
            pltpu.VMEM(pre_act.shape, BF16),
            pltpu.VMEM(features.shape, BF16),
            pltpu.VMEM((2 * Z, NY * 8, X), F32),
            pltpu.VMEM((Z, (NY + 2) * 4, X), F32),
            pltpu.SemaphoreType.DMA((3,)),
        ],
        compiler_params=pltpu.CompilerParams(vmem_limit_bytes=56 * 1024 * 1024),
    )(out_grad, pre_act, features)
    got = lax.all_to_all(sent, CHAN, 0, 0, tiled=True)

    up = [(i, (i + 1) % 16) for i in range(16)]
    down = [((i + 1) % 16, i) for i in range(16)]
    swap = [(0, 1), (1, 0)]
    halo_l = lax.ppermute(got[:, 10:20], SLAB, up)
    halo_r = lax.ppermute(got[:, :10], SLAB, down)
    has_l, has_r = slab_pos > 0, slab_pos < 15
    scal = jnp.stack(
        [slab_pos * Z, chan_pos * R, layer_offset[0], dropout_seed[0], core, has_l.astype(jnp.int32), has_r.astype(jnp.int32)]
    )

    own = call(
        kernel_a,
        (scal, got, weight_two, weight_one),
        [
            ((Z, 384, 4 * X), BF16),
            ((Z + 2, MID, R * X), F32),
            ((Z, MID, R * X), BF16),
            ((3, 384, 384), F32),
            ((3, 384, 384), BF16),
            (((Z + 4) * CIN, 4 * X), BF16),
            ((9 * CIN, 384), BF16),
            ((Z, CIN, 4 * X), F32),
            ((3, 384, 3 * CIN), F32),
        ],
        [(((Z + 2) * MID, R * X), BF16), ((2, 384, R * X), BF16)],
        6 * 10**9,
        1,
    )
    feature, mine_two, theirs_two, mine_one, theirs_one = call(
        kernel_c,
        (scal, halo_l, halo_r) + tuple(own),
        [
            ((16, 8, 8, X), BF16),
            ((14, 128, 128), F32),
            ((14, 128, 128), BF16),
            ((7, 128, 128), F32),
            ((7, 128, 128), BF16),
        ],
        [
            ((4, 384, 4 * X), BF16),
            ((Z + 2, MID, R * X), F32),
            ((2, MID, R * X), BF16),
            ((4, 384, R * X), BF16),
            ((Z, CIN, 4 * X), F32),
        ],
        3 * 10**9,
        1,
    )

    mine_two = mine_two + lax.ppermute(theirs_two, "core", swap).astype(F32)
    mine_one = mine_one + lax.ppermute(theirs_one, "core", swap).astype(F32)
    mine = jnp.concatenate([mine_two, mine_one]).astype(BF16).reshape(21, 16, 8, 128).transpose(1, 0, 2, 3)
    got = lax.all_to_all(jnp.concatenate([mine, feature], axis=1), CHAN, 0, 0, tiled=True)

    rows = got[:, 21:].astype(F32).reshape(16, Z, 4, 4, X)
    none = jnp.zeros((1, Z, 4, X), F32)
    first = rows[:, :, 1] + jnp.concatenate([none, rows[:-1, :, 3]])
    second = rows[:, :, 2] + jnp.concatenate([rows[1:, :, 0], none])
    feature = jnp.stack([first, second], axis=2).transpose(3, 1, 0, 2, 4).reshape(4, Z, NY, X)

    part = got[:, :21].astype(F32).sum(axis=0)
    part = part + lax.ppermute(part, "zl", swap)
    part = part + lax.ppermute(part, "x", [(i, i ^ 1) for i in range(4)])
    part = part + lax.ppermute(part, "x", [(i, i ^ 2) for i in range(4)])
    scale = 1.0 / math.sqrt(NZ * NY * X)
    total = lax.all_gather(part * scale, "core", axis=0, tiled=False)
    two = jnp.concatenate([total[0, :14], total[1, 1:14]])
    one = total[:, 14:].reshape(14, 8, 2, CIN)
    one = jnp.concatenate([one[:9, :, 0], one[:9, :, 1], one[9:, :, 0], one[9:13, :, 1]])
    two = two.transpose(1, 2, 0).reshape(8, 27 * MID)
    one = one.transpose(1, 2, 0).reshape(4, 54 * CIN)
    return feature, one, two


def solution(mesh):
    split = Mesh(mesh.devices.reshape(4, 2, 2, 4, 4), ("x", "zl", "core", "y", "zh"))
    cells = P(CHAN, SLAB, None, None)
    return jax.shard_map(
        shards,
        mesh=split,
        in_specs=(cells, cells, cells, P(), P(), P(), P()),
        out_specs=(cells, P(CHAN, None), P(CHAN, None)),
        check_vma=False,
    )
```

time: 117 us -> 116 us (level)
  blocking collectives: 72.4 us -> 36.1 us
  waiting for transfers between devices: 12.6 us -> 38.8 us
  starting transfers between devices: 13.5 us -> 22.4 us
  Pallas kernels: 8.74 us -> 11.7 us
  local copies, waits for them, and re-layouts: 6.27 us -> 3.63 us
    all_to_all x1 -> x0, blocking collectives: 39.1 us -> none  [shards(): lax.all_to_all(sent.reshape(16, Z * TILES, 8, X), CHAN, 0, 0, tiled=True)]
    all_to_all x0 -> x1, waiting for transfers between devices: none -> 24.6 us  [shards(): got = lax.all_to_all(sent, CHAN, 0, 0, tiled=True)]
    all_to_all x0 -> x1, starting transfers between devices: none -> 11.9 us  [shards(): got = lax.all_to_all(sent, CHAN, 0, 0, tiled=True)]
    unnamed x10 -> x5, local copies, waits for them, and re-layouts: 2.54 us -> 0.19 us
    pallas_call x0 -> x1, Pallas kernels: none -> 2.31 us  [shards(): pl.pallas_call(kernel_s, out_shape=jax.ShapeDtypeStruct((16, 32, 8, X), B...]
    ppermute x1, waiting for transfers between devices: 1.26 us -> 2.97 us  [shards(): part = part + lax.ppermute(part, 'x', [(i, i ^ 2) for i in range(4)])]
    all_gather x1, blocking collectives: 5.26 us -> 6.8 us  [shards(): total = lax.all_gather(part * scale, 'core', axis=0, tiled=False)]
    ppermute x1, starting transfers between devices: 3.05 us -> 1.66 us  [shards(): part = part + lax.ppermute(part, 'x', [(i, i ^ 2) for i in range(4)])]
  transfers between devices with their start and end apart: 11 -> 8, of which waited for: 6 -> 8; matrix products, arithmetic and copies ran while one was open for 1% -> 1% of each run, Pallas kernels for 6% -> 4%
where the time goes in v4:
time: 116 us; the launch traced here: 115 us
  waiting for transfers between devices  38.8 us (33%)
  blocking collectives  36.1 us (31%)
  starting transfers between devices  22.4 us (19%)
  Pallas kernels  11.7 us (10%)
  local copies, waits for them, and re-layouts  3.63 us (3%)
  between operations  2.16 us (2%)
    all_to_all x1, blocking collectives, shards(): lax.all_to_all(jnp.concatenate([mine, feature], axis=1), CHAN, 0, 0, tile...  29.3 us
    all_to_all x1, waiting for transfers between devices, shards(): got = lax.all_to_all(sent, CHAN, 0, 0, tiled=True)  24.6 us
    all_to_all x1, starting transfers between devices, shards(): got = lax.all_to_all(sent, CHAN, 0, 0, tiled=True)  11.9 us
    pallas_call x2, Pallas kernels, call(): pl.pallas_call(body, out_shape=tuple((jax.ShapeDtypeStruct(shape, kind) f...  9.38 us
    all_gather x1, blocking collectives, shards(): total = lax.all_gather(part * scale, 'core', axis=0, tiled=False)  6.8 us
    ppermute x1, starting transfers between devices, shards(): halo_r = lax.ppermute(got[:, :10], SLAB, down)  5.34 us
    ppermute x1, waiting for transfers between devices, shards(): part = part + lax.ppermute(part, 'x', [(i, i ^ 1) for i in range(4)])  3.28 us
    ppermute x1, waiting for transfers between devices, shards(): part = part + lax.ppermute(part, 'zl', swap)  3.25 us
  transfers between devices with their start and end apart: 8, of which 8 were waited for; matrix products, arithmetic and copies ran while one was open for 1% of the time, Pallas kernels for 4%

profile of v4, /device:TPU:1, one launch (start us, length us, event | category | flops | bytes accessed | tf_op | source)
XLA Modules:
  0.0 115.4 jit_solution(872905084266559793)
XLA Ops:
  0.6 2.3 %shard_map.94 = bf16[16,32,8,128]{3,2,1,0:T(8,128)(2,1)} custom-call(bf16[8,4,32,128]{3,2,1,0:T(8,128)(2,1)} %grad_in.1, bf16[8,4,32,128]{3,2,1,0:T(8,128)(2,1)} %pre_in.1, bf16[4,4,32,128]{3,2,1,0:T(8,128)(2,1)} %feat_in.1), custom_call_target="tpu_custom_call" | custom-call | tf_op jit(solution)/shard_map/pallas_call | solution.py:261
  2.9 0.0 copy-start
  3.0 0.0 copy-start.1
  3.0 11.9 %all-to-all-start = ((bf16[16,32,8,128]{3,2,1,0:T(8,128)(2,1)}), bf16[16,32,8,128]{3,2,1,0:T(8,128)(2,1)S(1)}, u32[]{:S(2)}, u32[]{:S(2)}) async-start(bf16[16,32,8,128]{3,2,1,0:T(8,128)(2,1)} %shard_map.94), calls=%async_computation | async-start | bytes 2097152 | tf_op jit(solution)/shard_map/all_to_all | solution.py:276
  16.2 0.1 stack.40.scal
  16.3 24.6 %all-to-all-done.got = bf16[16,32,8,128]{3,2,1,0:T(8,128)(2,1)S(1)} async-done(((bf16[16,32,8,128]{3,2,1,0:T(8,128)(2,1)}), bf16[16,32,8,128]{3,2,1,0:T(8,128)(2,1)S(1)}, u32[]{:S(2)}, u32[]{:S(2)}) %all-to-all-start) | async-done | bytes 1048608 | tf_op jit(solution)/shard_map/all_to_all | solution.py:276
  41.0 5.3 %collective-permute-start.1 = (bf16[16,10,8,128]{3,2,1,0:T(8,128)(2,1)S(1)}, bf16[16,10,8,128]{3,2,1,0:T(8,128)(2,1)S(1)}, u32[]{:S(2)}, u32[]{:S(2)}) collective-permute-start(bf16[16,10,8,128]{3,2,1,0:T(8,128)(2,1)S(1)} %get-tuple-element.31), channel_id=1, source_target_pairs={{16,0},{32,16},{48,32},{64,48},{80,64},{96,80},{112,96},{128,112},... | collective-permute-start | bytes 983048 | tf_op jit(solution)/shard_map/ppermute | solution.py:282
  46.3 0.0 collective-permute-start
  46.3 0.0 copy-done
  46.3 0.0 copy-done.1
  46.3 4.3 %shard_map.95 = (bf16[4,384,512]{2,1,0:T(8,128)(2,1)S(1)}, f32[6,128,256]{2,1,0:T(8,128)S(1)}, bf16[4,128,256]{2,1,0:T(8,128)(2,1)S(1)}, f32[3,384,384]{2,1,0:T(...) custom-call(s32[7]{0:T(128)S(1)} %stack.40.scal, ...), custom_call_target="tpu_custom_call" | custom-call | flops 6000000000 | bytes 4194304 | tf_op jit(solution)/shard_map/pallas_call | solution.py:246
  50.7 0.7 collective-permute-done.1.halo_r
  51.4 2.3 %collective-permute-done.halo_l = bf16[16,10,8,128]{3,2,1,0:T(8,128)(2,1)S(1)} collective-permute-done((bf16[16,10,8,128]{3,2,1,0:T(8,128)(2,1)S(1)}, bf16[16,10,8,128]{3,2,1,0:T(8,128)(2,1)S(1)}, u32[]{:S(2)}, u32[]{:S(2)}) %collective-permute-start) | collective-permute-done | bytes 327712 | tf_op jit(solution)/shard_map/ppermute | solution.py:281
  53.6 5.0 %shard_map.96 = (bf16[16,8,8,128]{3,2,1,0:T(8,128)(2,1)S(1)}, f32[14,128,128]{2,1,0:T(8,128)S(1)}, bf16[14,128,128]{2,1,0:T(8,128)(2,1)S(1)}, f32[7,128,128]{2,1,0:T(8,128)S(1)}, bf16[7,128,128]{2,1,0:T(8,128)(2,1)S(1)}) custom-call(s32[7]{0:T(128)S(1)} %stack.40.scal, bf16[16,10,8,128]{3,2,1,0:T(8,128)(2,1)S(1)} %collective-permute-done.halo_l, ...), custom_call_target="tpu_custom_call" | custom-call | flops 3000000000 | bytes 4194304 | tf_op jit(solution)/shard_map/pallas_call | solution.py:246
  58.7 3.2 %collective-permute-start.3 = (bf16[7,128,128]{2,1,0:T(8,128)(2,1)S(1)}, bf16[7,128,128]{2,1,0:T(8,128)(2,1)S(1)}, u32[]{:S(2)}, u32[]{:S(2)}) collective-permute-start(bf16[7,128,128]{2,1,0:T(8,128)(2,1)S(1)} %get-tuple-element.29), channel_id=1, source_target_pairs={{0,16},{16,0},{1,17},{17,1},{2,18},{18,2},{3,19},{19,3},{4,20},{20... | collective-permute-start | bytes 688136 | tf_op jit(solution)/shard_map/ppermute | solution.py:328
  61.9 0.1 collective-permute-start.2
  62.0 1.0 collective-permute-done.3
  63.0 0.1 fusion.1
  63.1 0.6 collective-permute-done.2
  63.7 0.1 fusion
  63.9 0.1 copy_bitcast_fusion
  64.0 0.1 pad_maximum_fusion
  64.1 29.3 %all_to_all.10 = bf16[16,29,8,128]{3,2,1,0:T(8,128)(2,1)S(1)} all-to-all(bf16[16,29,8,128]{3,2,1,0:T(8,128)(2,1)S(1)} %pad_maximum_fusion), channel_id=1, replica_groups=mesh['x'=4,'zl'=2,'core'=2,'y'=4,'zh'=4] {'y','zh'}, dimensions={0} | all-to-all | bytes 1900544 | tf_op jit(solution)/shard_map/all_to_all | solution.py:330
  93.4 0.2 copy.42
  93.5 0.1 convert_reduce_fusion
  93.6 0.1 collective-permute-start.4
  93.8 3.2 %collective-permute-done.4 = f32[21,8,128]{2,1,0:T(8,128)S(1)} collective-permute-done((f32[21,8,128]{2,1,0:T(8,128)S(1)}, f32[21,8,128]{2,1,0:T(8,128)S(1)}, u32[]{:S(2)}, u32[]{:S(2)}) %collective-permute-start.4) | collective-permute-done | bytes 86048 | tf_op jit(solution)/shard_map/ppermute | solution.py:339
  97.1 0.1 collective-permute-start.5
  97.2 3.3 %collective-permute-done.5 = f32[21,8,128]{2,1,0:T(8,128)S(1)} collective-permute-done((f32[21,8,128]{2,1,0:T(8,128)S(1)}, f32[21,8,128]{2,1,0:T(8,128)S(1)}, u32[]{:S(2)}, u32[]{:S(2)}) %collective-permute-start.5) | collective-permute-done | bytes 86048 | tf_op jit(solution)/shard_map/ppermute | solution.py:340
  100.5 1.7 %collective-permute-start.6 = (f32[21,8,128]{2,1,0:T(8,128)S(1)}, f32[21,8,128]{2,1,0:T(8,128)S(1)}, u32[]{:S(2)}, u32[]{:S(2)}) collective-permute-start(f32[21,8,128]{2,1,0:T(8,128)S(1)} %add.42), channel_id=1, source_target_pairs={{0,128},{64,192},{128,0},{192,64},{1,129},{65,193},{129,1},{193,65... | collective-permute-start | bytes 258056 | tf_op jit(solution)/shard_map/ppermute | solution.py:341
  102.2 0.9 copy.37
  103.1 3.0 %collective-permute-done.6 = f32[21,8,128]{2,1,0:T(8,128)S(1)} collective-permute-done((f32[21,8,128]{2,1,0:T(8,128)S(1)}, f32[21,8,128]{2,1,0:T(8,128)S(1)}, u32[]{:S(2)}, u32[]{:S(2)}) %collective-permute-start.6) | collective-permute-done | bytes 86048 | tf_op jit(solution)/shard_map/ppermute | solution.py:341
  106.1 6.8 %all-gather = f32[42,8,128]{2,1,0:T(8,128)S(1)} all-gather(f32[21,8,128]{2,1,0:T(8,128)S(1)} %add_multiply_fusion), channel_id=2, replica_groups=mesh['x'=4,'zl'=2,'core'=2,'y'=4,'zh'=4] {'core'}, dimensions={0}, use_global_device_ids=true | all-gather | bytes 258048 | tf_op jit(solution)/shard_map/all_gather | solution.py:343
  112.9 0.1 reshape.32
  113.1 0.1 fusion.7
  113.2 0.1 copy.39
  113.3 0.8 reshape.33
  114.2 0.2 copy.40
  114.4 0.9 reshape.34
  (16 shorter events, 0.3 us)
Async XLA Ops:
  2.9 43.4 %copy-start = (bf16[27,128,128]{2,1,0:T(8,128)(2,1)S(1)}, bf16[27,128,128]{2,1,0:T(8,128)(2,1)}, u32[]{:S(2)}) copy-start(bf16[27,128,128]{2,1,0:T(8,128)(2,1)} %w_two.1) | copy-start | bytes 2654212
  3.0 43.4 %copy-start.1 = (bf16[27,64,128]{2,1,0:T(8,128)(2,1)S(1)}, bf16[27,64,128]{2,1,0:T(8,128)(2,1)}, u32[]{:S(2)}) copy-start(bf16[27,64,128]{2,1,0:T(8,128)(2,1)} %w_one.1) | copy-start | bytes 1327108
  3.0 37.9 %all-to-all-start = ((bf16[16,32,8,128]{3,2,1,0:T(8,128)(2,1)}), bf16[16,32,8,128]{3,2,1,0:T(8,128)(2,1)S(1)}, u32[]{:S(2)}, u32[]{:S(2)}) async-start(bf16[16,32,8,128]{3,2,1,0:T(8,128)(2,1)} %shard_map.94), calls=%async_computation | async-start | bytes 2097152 | tf_op jit(solution)/shard_map/all_to_all | solution.py:276
  41.0 10.4 %collective-permute-start.1 = (bf16[16,10,8,128]{3,2,1,0:T(8,128)(2,1)S(1)}, bf16[16,10,8,128]{3,2,1,0:T(8,128)(2,1)S(1)}, u32[]{:S(2)}, u32[]{:S(2)}) collective-permute-start(bf16[16,10,8,128]{3,2,1,0:T(8,128)(2,1)S(1)} %get-tuple-element.31), channel_id=1, source_target_pairs={{16,0},{32,16},{48,32},{64,48},{80,64},{96,80},{112,96},{128,112},... | collective-permute-start | bytes 983048 | tf_op jit(solution)/shard_map/ppermute | solution.py:282
  46.3 7.3 %collective-permute-start = (bf16[16,10,8,128]{3,2,1,0:T(8,128)(2,1)S(1)}, bf16[16,10,8,128]{3,2,1,0:T(8,128)(2,1)S(1)}, u32[]{:S(2)}, u32[]{:S(2)}) collective-permute-start(bf16[16,10,8,128]{3,2,1,0:T(8,128)(2,1)S(1)} %get-tuple-element.32), channel_id=1, source_target_pairs={{0,16},{16,32},{32,48},{48,64},{64,80},{80,96},{96,112},{112,128},... | collective-permute-start | bytes 983048 | tf_op jit(solution)/shard_map/ppermute | solution.py:281
  58.7 4.3 %collective-permute-start.3 = (bf16[7,128,128]{2,1,0:T(8,128)(2,1)S(1)}, bf16[7,128,128]{2,1,0:T(8,128)(2,1)S(1)}, u32[]{:S(2)}, u32[]{:S(2)}) collective-permute-start(bf16[7,128,128]{2,1,0:T(8,128)(2,1)S(1)} %get-tuple-element.29), channel_id=1, source_target_pairs={{0,16},{16,0},{1,17},{17,1},{2,18},{18,2},{3,19},{19,3},{4,20},{20... | collective-permute-start | bytes 688136 | tf_op jit(solution)/shard_map/ppermute | solution.py:328
  61.9 1.8 %collective-permute-start.2 = (bf16[14,128,128]{2,1,0:T(8,128)(2,1)S(1)}, bf16[14,128,128]{2,1,0:T(8,128)(2,1)S(1)}, u32[]{:S(2)}, u32[]{:S(2)}) collective-permute-start(bf16[14,128,128]{2,1,0:T(8,128)(2,1)S(1)} %get-tuple-element.27), channel_id=1, source_target_pairs={{0,16},{16,0},{1,17},{17,1},{2,18},{18,2},{3,19},{19,3},{4,20},{20... | collective-permute-start | bytes 1376264 | tf_op jit(solution)/shard_map/ppermute | solution.py:327
  93.6 3.4 %collective-permute-start.4 = (f32[21,8,128]{2,1,0:T(8,128)S(1)}, f32[21,8,128]{2,1,0:T(8,128)S(1)}, u32[]{:S(2)}, u32[]{:S(2)}) collective-permute-start(f32[21,8,128]{2,1,0:T(8,128)S(1)} %convert_reduce_fusion), channel_id=1, source_target_pairs={{0,32},{32,0},{1,33},{33,1},{2,34},{34,2},{3,35},{35,3},{4,36},{36... | collective-permute-start | bytes 258056 | tf_op jit(solution)/shard_map/ppermute | solution.py:339
  97.1 3.4 %collective-permute-start.5 = (f32[21,8,128]{2,1,0:T(8,128)S(1)}, f32[21,8,128]{2,1,0:T(8,128)S(1)}, u32[]{:S(2)}, u32[]{:S(2)}) collective-permute-start(f32[21,8,128]{2,1,0:T(8,128)S(1)} %add.41), channel_id=1, source_target_pairs={{0,64},{64,0},{128,192},{192,128},{1,65},{65,1},{129,193},{193,129... | collective-permute-start | bytes 258056 | tf_op jit(solution)/shard_map/ppermute | solution.py:340
  100.5 5.6 %collective-permute-start.6 = (f32[21,8,128]{2,1,0:T(8,128)S(1)}, f32[21,8,128]{2,1,0:T(8,128)S(1)}, u32[]{:S(2)}, u32[]{:S(2)}) collective-permute-start(f32[21,8,128]{2,1,0:T(8,128)S(1)} %add.42), channel_id=1, source_target_pairs={{0,128},{64,192},{128,0},{192,64},{1,129},{65,193},{129,1},{193,65... | collective-permute-start | bytes 258056 | tf_op jit(solution)/shard_map/ppermute | solution.py:341

commit v5 on v4

--- a/solution.py
+++ b/solution.py
@@ -50,15 +50,17 @@
     return ref[:, t].astype(F32).reshape(128, X)
 
 
-def store_halves(core, mine, theirs, s, count, step, slab):
-    for me in range(2):
-
-        @pl.when(core == me)
-        def _():
-            for half in range(2):
-                if 0 <= s - half * step < count:
-                    dst = mine if half == me else theirs
-                    dst[s - half * step] = slab.astype(dst.dtype)
+def store_slab(core, mine, theirs, s, slab):
+    at = s // 6 * 3 + s % 3
+    owner = s // 3 % 2
+
+    @pl.when(core == owner)
+    def _():
+        mine[at] = slab
+
+    @pl.when(core != owner)
+    def _():
+        theirs[at] = slab.astype(BF16)
 
 
 def shuffle(back):
@@ -179,9 +181,11 @@
 
 def kernel_c(
     scal, halo_l, halo_r, g3, part_hid, mask, part_two, wk, feat, wf, part_fin, part_one,
-    fout, mine, theirs, mine_one, theirs_one, g, hid, act, p3, fin,
+    fout, mine, theirs, g, hid, act, p3, fin,
 ):
     core, has_l, has_r = scal[4], scal[5] > 0, scal[6] > 0
+    mine[20:] = jnp.zeros((4, 128, 128), F32)
+    theirs[20:] = jnp.zeros((4, 128, 128), BF16)
     for at in range(4):
         for r in range(4):
             if at < 2:
@@ -219,7 +223,7 @@
                 slab = part_two[kh, kw * 128 : (kw + 1) * 128, kd * MID : (kd + 1) * MID]
                 if kd != 1:
                     slab = slab + (low if kd == 0 else high)[kw * 128 : (kw + 1) * 128]
-                store_halves(core, mine, theirs, 9 * kd + 3 * kh + kw, 14, 13, slab)
+                store_slab(core, mine, theirs, 9 * kd + 3 * kh + kw, slab)
     fin[...] = part_fin[...]
     for at, plane in enumerate(outer):
         add_feature_terms(fin, wf, p3[at], plane)
@@ -232,11 +236,22 @@
     for kh in range(3):
         total = raw_one_terms(feat, [(plane, p3[at]) for at, plane in enumerate(outer)], part_one[kh], kh)
         for kw in range(3):
-            store_halves(core, mine_one, theirs_one, 3 * kh + kw, 7, 7, total[kw * 128 : (kw + 1) * 128, : 2 * CIN])
+            store_slab(core, mine, theirs, 27 + 3 * kh + kw, total[kw * 128 : (kw + 1) * 128, : 2 * CIN])
             last.append(total[kw * 128 : (kw + 1) * 128, 2 * CIN :])
     last.append(jnp.zeros((128, CIN), F32))
     for b in range(5):
-        store_halves(core, mine_one, theirs_one, 9 + b, 7, 7, jnp.concatenate([last[b], last[b + 5]], axis=1))
+        store_slab(core, mine, theirs, 36 + b, jnp.concatenate([last[b], last[b + 5]], axis=1))
+
+
+def kernel_p(shares, feature, sent):
+    for i in range(3):
+        total = shares[0, i].astype(F32)
+        for j in range(1, 8):
+            total = total + shares[j, i].astype(F32)
+        high = total.astype(BF16).astype(F32)
+        sent[:, i] = high.reshape(16, 8, X).astype(BF16)
+        sent[:, 3 + i] = (total - high).reshape(16, 8, X).astype(BF16)
+    sent[:, 6:] = feature[...]
 
 
 VMEM, SMEM = pl.BlockSpec(memory_space=pltpu.VMEM), pl.BlockSpec(memory_space=pltpu.SMEM)
@@ -303,15 +318,13 @@
         6 * 10**9,
         1,
     )
-    feature, mine_two, theirs_two, mine_one, theirs_one = call(
+    feature, mine, theirs = call(
         kernel_c,
         (scal, halo_l, halo_r) + tuple(own),
         [
             ((16, 8, 8, X), BF16),
-            ((14, 128, 128), F32),
-            ((14, 128, 128), BF16),
-            ((7, 128, 128), F32),
-            ((7, 128, 128), BF16),
+            ((24, 128, 128), F32),
+            ((24, 128, 128), BF16),
         ],
         [
             ((4, 384, 4 * X), BF16),
@@ -324,25 +337,23 @@
         1,
     )
 
-    mine_two = mine_two + lax.ppermute(theirs_two, "core", swap).astype(F32)
-    mine_one = mine_one + lax.ppermute(theirs_one, "core", swap).astype(F32)
-    mine = jnp.concatenate([mine_two, mine_one]).astype(BF16).reshape(21, 16, 8, 128).transpose(1, 0, 2, 3)
-    got = lax.all_to_all(jnp.concatenate([mine, feature], axis=1), CHAN, 0, 0, tiled=True)
-
-    rows = got[:, 21:].astype(F32).reshape(16, Z, 4, 4, X)
+    mine = (mine + lax.ppermute(theirs, "core", swap).astype(F32)).astype(BF16)
+    shares = lax.all_to_all(mine.reshape(8, 3, 128, 128), ("x", "zl"), 0, 0, tiled=True)
+    (sent,) = call(kernel_p, (shares, feature), [((16, 14, 8, X), BF16)], [], 10**6, 0)
+    got = lax.all_to_all(sent, CHAN, 0, 0, tiled=True)
+
+    rows = got[:, 6:].astype(F32).reshape(16, Z, 4, 4, X)
     none = jnp.zeros((1, Z, 4, X), F32)
     first = rows[:, :, 1] + jnp.concatenate([none, rows[:-1, :, 3]])
     second = rows[:, :, 2] + jnp.concatenate([rows[1:, :, 0], none])
     feature = jnp.stack([first, second], axis=2).transpose(3, 1, 0, 2, 4).reshape(4, Z, NY, X)
 
-    part = got[:, :21].astype(F32).sum(axis=0)
-    part = part + lax.ppermute(part, "zl", swap)
-    part = part + lax.ppermute(part, "x", [(i, i ^ 1) for i in range(4)])
-    part = part + lax.ppermute(part, "x", [(i, i ^ 2) for i in range(4)])
     scale = 1.0 / math.sqrt(NZ * NY * X)
-    total = lax.all_gather(part * scale, "core", axis=0, tiled=False)
-    two = jnp.concatenate([total[0, :14], total[1, 1:14]])
-    one = total[:, 14:].reshape(14, 8, 2, CIN)
+    part = got[:, :6].astype(F32).sum(axis=0)
+    part = (part[:3] + part[3:]) * scale
+    total = lax.all_to_all(jnp.broadcast_to(part[None], (16, 3, 8, 128)), SLAB, 0, 0, tiled=True)
+    total = total.reshape(48, 8, 128)
+    two, one = total[:27], total[27:41].reshape(14, 8, 2, CIN)
     one = jnp.concatenate([one[:9, :, 0], one[:9, :, 1], one[9:, :, 0], one[9:13, :, 1]])
     two = two.transpose(1, 2, 0).reshape(8, 27 * MID)
     one = one.transpose(1, 2, 0).reshape(4, 54 * CIN)

time: 116 us -> 115 us (level)
  waiting for transfers between devices: 38.8 us -> 35.1 us
  starting transfers between devices: 22.4 us -> 25.8 us
    ppermute x5 -> x1, waiting for transfers between devices: 11.1 us -> 1.91 us  [shards(): mine = (mine + lax.ppermute(theirs, 'core', swap).astype(F32)).astype(BF16)]
    all_gather x1 -> x0, blocking collectives: 6.8 us -> none  [shards(): total = lax.all_gather(part * scale, 'core', axis=0, tiled=False)]
    all_to_all x1 -> x2, blocking collectives: 29.3 us -> 35.1 us  [the longest x1 19 us: shards(): got = lax.all_to_all(sent, CHAN, 0, 0, tiled=True)]
    all_to_all x0 -> x1, waiting for transfers between devices: none -> 5.53 us  [shards(): lax.all_to_all(jnp.broadcast_to(part[None], (16, 3, 8, 128)), SLAB, 0, 0,...]
    all_to_all x0 -> x1, starting transfers between devices: none -> 5.37 us  [shards(): lax.all_to_all(jnp.broadcast_to(part[None], (16, 3, 8, 128)), SLAB, 0, 0,...]
    ppermute x5 -> x1, starting transfers between devices: 5.17 us -> 3.2 us  [shards(): mine = (mine + lax.ppermute(theirs, 'core', swap).astype(F32)).astype(BF16)]
    pallas_call x2 -> x3, Pallas kernels: 9.38 us -> 9.52 us  [call(): pl.pallas_call(body, out_shape=tuple((jax.ShapeDtypeStruct(shape, kind) f...]
  transfers between devices with their start and end apart: 8 -> 5, of which waited for: 8 -> 5; matrix products, arithmetic and copies ran while one was open for 1% -> 1% of each run, Pallas kernels for 4% -> 4%
where the time goes in v5:
time: 115 us
  waiting for transfers between devices  35.1 us (31%)
  blocking collectives  35.1 us (31%)
  starting transfers between devices  25.8 us (22%)
  Pallas kernels  11.8 us (10%)
  local copies, waits for them, and re-layouts  4.17 us (4%)
  between operations  2.12 us (2%)
    all_to_all x1, waiting for transfers between devices, shards(): got = lax.all_to_all(sent, CHAN, 0, 0, tiled=True)  24.6 us
    all_to_all x1, blocking collectives, shards(): got = lax.all_to_all(sent, CHAN, 0, 0, tiled=True)  19 us
    all_to_all x1, blocking collectives, shards(): lax.all_to_all(mine.reshape(8, 3, 128, 128), ('x', 'zl'), 0, 0, tiled=True)  16.1 us
    all_to_all x1, starting transfers between devices, shards(): got = lax.all_to_all(sent, CHAN, 0, 0, tiled=True)  11.9 us
    pallas_call x3, Pallas kernels, call(): pl.pallas_call(body, out_shape=tuple((jax.ShapeDtypeStruct(shape, kind) f...  9.52 us
    all_to_all x1, waiting for transfers between devices, shards(): lax.all_to_all(jnp.broadcast_to(part[None], (16, 3, 8, 128)), SLAB, 0, 0,...  5.53 us
    all_to_all x1, starting transfers between devices, shards(): lax.all_to_all(jnp.broadcast_to(part[None], (16, 3, 8, 128)), SLAB, 0, 0,...  5.37 us
    ppermute x1, starting transfers between devices, shards(): halo_r = lax.ppermute(got[:, :10], SLAB, down)  5.34 us
  transfers between devices with their start and end apart: 5, of which 5 were waited for; matrix products, arithmetic and copies ran while one was open for 1% of the time, Pallas kernels for 4%

profile of v5, /device:TPU:1, one launch (start us, length us, event | category | flops | bytes accessed | tf_op | source)
XLA Modules:
  0.0 114.5 jit_solution(2609244843950802246)
XLA Ops:
  0.6 2.3 %shard_map.94 = bf16[16,32,8,128]{3,2,1,0:T(8,128)(2,1)} custom-call(bf16[8,4,32,128]{3,2,1,0:T(8,128)(2,1)} %grad_in.1, bf16[8,4,32,128]{3,2,1,0:T(8,128)(2,1)} %pre_in.1, bf16[4,4,32,128]{3,2,1,0:T(8,128)(2,1)} %feat_in.1), custom_call_target="tpu_custom_call" | custom-call | tf_op jit(solution)/shard_map/pallas_call | solution.py:276
  2.9 0.0 copy-start
  2.9 0.0 copy-start.1
  3.0 11.9 %all-to-all-start = ((bf16[16,32,8,128]{3,2,1,0:T(8,128)(2,1)}), bf16[16,32,8,128]{3,2,1,0:T(8,128)(2,1)S(1)}, u32[]{:S(2)}, u32[]{:S(2)}) async-start(bf16[16,32,8,128]{3,2,1,0:T(8,128)(2,1)} %shard_map.94), calls=%async_computation | async-start | bytes 2097152 | tf_op jit(solution)/shard_map/all_to_all | solution.py:291
  16.2 0.1 stack.40.scal
  16.3 24.6 %all-to-all-done.got = bf16[16,32,8,128]{3,2,1,0:T(8,128)(2,1)S(1)} async-done(((bf16[16,32,8,128]{3,2,1,0:T(8,128)(2,1)}), bf16[16,32,8,128]{3,2,1,0:T(8,128)(2,1)S(1)}, u32[]{:S(2)}, u32[]{:S(2)}) %all-to-all-start) | async-done | bytes 1048608 | tf_op jit(solution)/shard_map/all_to_all | solution.py:291
  41.0 5.3 %collective-permute-start.1 = (bf16[16,10,8,128]{3,2,1,0:T(8,128)(2,1)S(1)}, bf16[16,10,8,128]{3,2,1,0:T(8,128)(2,1)S(1)}, u32[]{:S(2)}, u32[]{:S(2)}) collective-permute-start(bf16[16,10,8,128]{3,2,1,0:T(8,128)(2,1)S(1)} %get-tuple-element.27), channel_id=1, source_target_pairs={{16,0},{32,16},{48,32},{64,48},{80,64},{96,80},{112,96},{128,112},... | collective-permute-start | bytes 983048 | tf_op jit(solution)/shard_map/ppermute | solution.py:297
  46.3 0.0 collective-permute-start
  46.3 0.0 copy-done
  46.3 0.0 copy-done.1
  46.3 4.3 %shard_map.95 = (bf16[4,384,512]{2,1,0:T(8,128)(2,1)S(1)}, f32[6,128,256]{2,1,0:T(8,128)S(1)}, bf16[4,128,256]{2,1,0:T(8,128)(2,1)S(1)}, f32[3,384,384]{2,1,0:T(...) custom-call(s32[7]{0:T(128)S(1)} %stack.40.scal, ...), custom_call_target="tpu_custom_call" | custom-call | flops 6000000000 | bytes 4194304 | tf_op jit(solution)/shard_map/pallas_call | solution.py:261
  50.7 0.7 collective-permute-done.1.halo_r
  51.3 2.3 %collective-permute-done.halo_l = bf16[16,10,8,128]{3,2,1,0:T(8,128)(2,1)S(1)} collective-permute-done((bf16[16,10,8,128]{3,2,1,0:T(8,128)(2,1)S(1)}, bf16[16,10,8,128]{3,2,1,0:T(8,128)(2,1)S(1)}, u32[]{:S(2)}, u32[]{:S(2)}) %collective-permute-start) | collective-permute-done | bytes 327712 | tf_op jit(solution)/shard_map/ppermute | solution.py:296
  53.6 5.1 %shard_map.96 = (bf16[16,8,8,128]{3,2,1,0:T(8,128)(2,1)S(1)}, f32[24,128,128]{2,1,0:T(8,128)S(1)}, bf16[24,128,128]{2,1,0:T(8,128)(2,1)S(1)}) custom-call(s32[7]{0:T(128)S(1)} %stack.40.scal, bf16[16,10,8,128]{3,2,1,0:T(8,128)(2,1)S(1)} %collective-permute-done.halo_l, bf16[16,10,8,128]{3,2,1,0:T(8,128)(2,1)S(1)} %collective-permute-done.1.halo_r, ...), custom_call_target="tpu_custom_call" | custom-call | flops 3000000000 | bytes 4194304 | tf_op jit(solution)/shard_map/pallas_call | solution.py:261
  58.7 3.2 %collective-permute-start.2 = (bf16[24,128,128]{2,1,0:T(8,128)(2,1)S(1)}, bf16[24,128,128]{2,1,0:T(8,128)(2,1)S(1)}, u32[]{:S(2)}, u32[]{:S(2)}) collective-permute-start(bf16[24,128,128]{2,1,0:T(8,128)(2,1)S(1)} %get-tuple-element.25), channel_id=1, source_target_pairs={{0,16},{16,0},{1,17},{17,1},{2,18},{18,2},{3,19},{19,3},{4,20},{20... | collective-permute-start | bytes 2359304 | tf_op jit(solution)/shard_map/ppermute | solution.py:340
  61.9 1.9 %collective-permute-done.2 = bf16[24,128,128]{2,1,0:T(8,128)(2,1)S(1)} collective-permute-done((bf16[24,128,128]{2,1,0:T(8,128)(2,1)S(1)}, bf16[24,128,128]{2,1,0:T(8,128)(2,1)S(1)}, u32[]{:S(2)}, u32[]{:S(2)}) %collective-permute-start.2) | collective-permute-done | bytes 786464 | tf_op jit(solution)/shard_map/ppermute | solution.py:340
  63.8 0.2 add_convert_fusion
  64.1 16.1 %all_to_all.20.shares = bf16[8,3,128,128]{3,2,1,0:T(8,128)(2,1)S(1)} all-to-all(bf16[8,3,128,128]{3,2,1,0:T(8,128)(2,1)S(1)} %bitcast.49), channel_id=1, replica_groups=mesh['x'=4,'zl'=2,'core'=2,'y'=4,'zh'=4] {'x','zl'}, dimensions={0} | all-to-all | bytes 1572864 | tf_op jit(solution)/shard_map/all_to_all | solution.py:341
  80.2 0.1 shard_map.97
  80.3 19.0 %all_to_all.21 = bf16[16,14,8,128]{3,2,1,0:T(8,128)(2,1)S(1)} all-to-all(bf16[16,14,8,128]{3,2,1,0:T(8,128)(2,1)S(1)} %shard_map.97), channel_id=1, replica_groups=mesh['x'=4,'zl'=2,'core'=2,'y'=4,'zh'=4] {'y','zh'}, dimensions={0} | all-to-all | bytes 917504 | tf_op jit(solution)/shard_map/all_to_all | solution.py:343
  99.3 0.7 broadcast_in_dim.2
  100.0 5.4 %all-to-all-start.3 = ((f32[16,3,8,128]{3,2,1,0:T(8,128)}), f32[16,3,8,128]{3,2,1,0:T(8,128)S(1)}, u32[]{:S(2)}, u32[]{:S(2)}) async-start(f32[16,3,8,128]{3,2,1,0:T(8,128)} %broadcast_in_dim.2), calls=%async_computation.3 | async-start | bytes 393216 | tf_op jit(solution)/shard_map/all_to_all | solution.py:354
  105.5 0.1 fusion.3
  105.6 0.1 maximum_bitcast_fusion
  105.7 0.9 copy.17
  106.6 5.5 %all-to-all-done.3 = f32[16,3,8,128]{3,2,1,0:T(8,128)S(1)} async-done(((f32[16,3,8,128]{3,2,1,0:T(8,128)}), f32[16,3,8,128]{3,2,1,0:T(8,128)S(1)}, u32[]{:S(2)}, u32[]{:S(2)}) %all-to-all-start.3) | async-done | bytes 196640 | tf_op jit(solution)/shard_map/all_to_all | solution.py:354
  112.1 0.1 reshape.37
  112.3 0.1 fusion.6
  112.4 0.1 copy.19
  112.5 0.8 reshape.38
  113.4 0.2 copy.20
  113.6 0.9 reshape.39
  (11 shorter events, 0.2 us)
Async XLA Ops:
  2.9 43.4 %copy-start = (bf16[27,128,128]{2,1,0:T(8,128)(2,1)S(1)}, bf16[27,128,128]{2,1,0:T(8,128)(2,1)}, u32[]{:S(2)}) copy-start(bf16[27,128,128]{2,1,0:T(8,128)(2,1)} %w_two.1) | copy-start | bytes 2654212
  2.9 43.4 %copy-start.1 = (bf16[27,64,128]{2,1,0:T(8,128)(2,1)S(1)}, bf16[27,64,128]{2,1,0:T(8,128)(2,1)}, u32[]{:S(2)}) copy-start(bf16[27,64,128]{2,1,0:T(8,128)(2,1)} %w_one.1) | copy-start | bytes 1327108
  3.0 37.9 %all-to-all-start = ((bf16[16,32,8,128]{3,2,1,0:T(8,128)(2,1)}), bf16[16,32,8,128]{3,2,1,0:T(8,128)(2,1)S(1)}, u32[]{:S(2)}, u32[]{:S(2)}) async-start(bf16[16,32,8,128]{3,2,1,0:T(8,128)(2,1)} %shard_map.94), calls=%async_computation | async-start | bytes 2097152 | tf_op jit(solution)/shard_map/all_to_all | solution.py:291
  41.0 10.4 %collective-permute-start.1 = (bf16[16,10,8,128]{3,2,1,0:T(8,128)(2,1)S(1)}, bf16[16,10,8,128]{3,2,1,0:T(8,128)(2,1)S(1)}, u32[]{:S(2)}, u32[]{:S(2)}) collective-permute-start(bf16[16,10,8,128]{3,2,1,0:T(8,128)(2,1)S(1)} %get-tuple-element.27), channel_id=1, source_target_pairs={{16,0},{32,16},{48,32},{64,48},{80,64},{96,80},{112,96},{128,112},... | collective-permute-start | bytes 983048 | tf_op jit(solution)/shard_map/ppermute | solution.py:297
  46.3 7.3 %collective-permute-start = (bf16[16,10,8,128]{3,2,1,0:T(8,128)(2,1)S(1)}, bf16[16,10,8,128]{3,2,1,0:T(8,128)(2,1)S(1)}, u32[]{:S(2)}, u32[]{:S(2)}) collective-permute-start(bf16[16,10,8,128]{3,2,1,0:T(8,128)(2,1)S(1)} %get-tuple-element.28), channel_id=1, source_target_pairs={{0,16},{16,32},{32,48},{48,64},{64,80},{80,96},{96,112},{112,128},... | collective-permute-start | bytes 983048 | tf_op jit(solution)/shard_map/ppermute | solution.py:296
  58.7 5.1 %collective-permute-start.2 = (bf16[24,128,128]{2,1,0:T(8,128)(2,1)S(1)}, bf16[24,128,128]{2,1,0:T(8,128)(2,1)S(1)}, u32[]{:S(2)}, u32[]{:S(2)}) collective-permute-start(bf16[24,128,128]{2,1,0:T(8,128)(2,1)S(1)} %get-tuple-element.25), channel_id=1, source_target_pairs={{0,16},{16,0},{1,17},{17,1},{2,18},{18,2},{3,19},{19,3},{4,20},{20... | collective-permute-start | bytes 2359304 | tf_op jit(solution)/shard_map/ppermute | solution.py:340
  100.0 12.1 %all-to-all-start.3 = ((f32[16,3,8,128]{3,2,1,0:T(8,128)}), f32[16,3,8,128]{3,2,1,0:T(8,128)S(1)}, u32[]{:S(2)}, u32[]{:S(2)}) async-start(f32[16,3,8,128]{3,2,1,0:T(8,128)} %broadcast_in_dim.2), calls=%async_computation.3 | async-start | bytes 393216 | tf_op jit(solution)/shard_map/all_to_all | solution.py:354

commit v6 on v5

--- a/solution.py
+++ b/solution.py
@@ -50,17 +50,8 @@
     return ref[:, t].astype(F32).reshape(128, X)
 
 
-def store_slab(core, mine, theirs, s, slab):
-    at = s // 6 * 3 + s % 3
-    owner = s // 3 % 2
-
-    @pl.when(core == owner)
-    def _():
-        mine[at] = slab
-
-    @pl.when(core != owner)
-    def _():
-        theirs[at] = slab.astype(BF16)
+def store_slab(core, slabs, s, slab):
+    slabs[core ^ (s // 3 % 2), s // 6 * 3 + s % 3] = slab
 
 
 def shuffle(back):
@@ -70,8 +61,7 @@
     return jnp.where(at == j, F32(1.0), F32(0.0)).astype(BF16)
 
 
-def scaled(scal, pre, w, r):
-    scale = kept_scale(scal[2], scal[3], scal[0] + w, scal[1] + r)
+def scaled(pre, scale):
     return (jnp.maximum(pre, 0.0) * scale).astype(BF16), jnp.where(pre > 0, scale, 0.0)
 
 
@@ -127,7 +117,7 @@
     return total
 
 
-def kernel_a(scal, got, w_two, w_one, g3, hid, mask, two, wk, feat, wf, fin, one, act, p3):
+def kernel_a(scal, got, w_two, w_one, g3, hid, mask, edge, two, wk, feat, wf, fin, one, act, p3):
     for kd in range(3):
         for kh in range(3):
             for kw in range(3):
@@ -144,10 +134,14 @@
         for kd in range(3):
             hid[z + kd] = hid[z + kd] + total[kd * MID : (kd + 1) * MID]
     act[...] = jnp.zeros_like(act)
-    for w in range(Z):
+    for w in range(-1, Z + 1):
         for r in range(R):
             cols = slice(r * X, (r + 1) * X)
-            hidden, kept = scaled(scal, tile(got, PRE[w] + r), w, r)
+            scale = kept_scale(scal[2], scal[3], scal[0] + w, scal[1] + r)
+            if not 0 <= w < Z:
+                edge[0 if w < 0 else 1, :, cols] = scale.astype(BF16)
+                continue
+            hidden, kept = scaled(tile(got, PRE[w] + r), scale)
             act[(w + 1) * MID : (w + 2) * MID, cols] = hidden
             mask[w, :, cols] = kept.astype(BF16)
     for kh in range(3):
@@ -180,12 +174,11 @@
 
 
 def kernel_c(
-    scal, halo_l, halo_r, g3, part_hid, mask, part_two, wk, feat, wf, part_fin, part_one,
-    fout, mine, theirs, g, hid, act, p3, fin,
+    scal, halo_l, halo_r, g3, part_hid, mask, edge, part_two, wk, feat, wf, part_fin, part_one,
+    fout, slabs, theirs, g, hid, act, p3, fin,
 ):
     core, has_l, has_r = scal[4], scal[5] > 0, scal[6] > 0
-    mine[20:] = jnp.zeros((4, 128, 128), F32)
-    theirs[20:] = jnp.zeros((4, 128, 128), BF16)
+    slabs[:, 20:] = jnp.zeros((2, 4, 128, 128), F32)
     for at in range(4):
         for r in range(4):
             if at < 2:
@@ -206,10 +199,10 @@
         for r in range(R):
             cols = slice(r * X, (r + 1) * X)
             if j == 0:
-                hidden, kept = scaled(scal, jnp.where(has_l, tile(halo_l, 8 + r), 0.0), -1, r)
+                hidden, kept = scaled(jnp.where(has_l, tile(halo_l, 8 + r), 0.0), edge[0, :, cols].astype(F32))
                 act[0, :, cols] = hidden
             elif j == Z + 1:
-                hidden, kept = scaled(scal, jnp.where(has_r, tile(halo_r, r), 0.0), Z, r)
+                hidden, kept = scaled(jnp.where(has_r, tile(halo_r, r), 0.0), edge[1, :, cols].astype(F32))
                 act[1, :, cols] = hidden
             else:
                 kept = mask[j - 1, :, cols].astype(F32)
@@ -223,24 +216,25 @@
                 slab = part_two[kh, kw * 128 : (kw + 1) * 128, kd * MID : (kd + 1) * MID]
                 if kd != 1:
                     slab = slab + (low if kd == 0 else high)[kw * 128 : (kw + 1) * 128]
-                store_slab(core, mine, theirs, 9 * kd + 3 * kh + kw, slab)
+                store_slab(core, slabs, 9 * kd + 3 * kh + kw, slab)
     fin[...] = part_fin[...]
     for at, plane in enumerate(outer):
         add_feature_terms(fin, wf, p3[at], plane)
+    last = []
+    for kh in range(3):
+        total = raw_one_terms(feat, [(plane, p3[at]) for at, plane in enumerate(outer)], part_one[kh], kh)
+        for kw in range(3):
+            store_slab(core, slabs, 27 + 3 * kh + kw, total[kw * 128 : (kw + 1) * 128, : 2 * CIN])
+            last.append(total[kw * 128 : (kw + 1) * 128, 2 * CIN :])
+    last.append(jnp.zeros((128, CIN), F32))
+    for b in range(5):
+        store_slab(core, slabs, 36 + b, jnp.concatenate([last[b], last[b + 5]], axis=1))
     back = shuffle(True)
     for w in range(Z):
         for i in range(2):
             rows = jnp.concatenate([fin[w, :, (2 * i + r) * X : (2 * i + r + 1) * X] for r in range(2)], axis=0)
             fout[:, 2 * w + i] = dot(back, rows.astype(BF16)).reshape(16, 8, X).astype(BF16)
-    last = []
-    for kh in range(3):
-        total = raw_one_terms(feat, [(plane, p3[at]) for at, plane in enumerate(outer)], part_one[kh], kh)
-        for kw in range(3):
-            store_slab(core, mine, theirs, 27 + 3 * kh + kw, total[kw * 128 : (kw + 1) * 128, : 2 * CIN])
-            last.append(total[kw * 128 : (kw + 1) * 128, 2 * CIN :])
-    last.append(jnp.zeros((128, CIN), F32))
-    for b in range(5):
-        store_slab(core, mine, theirs, 36 + b, jnp.concatenate([last[b], last[b + 5]], axis=1))
+    theirs[...] = slabs[1].astype(BF16)
 
 
 def kernel_p(shares, feature, sent):
@@ -252,6 +246,16 @@
         sent[:, i] = high.reshape(16, 8, X).astype(BF16)
         sent[:, 3 + i] = (total - high).reshape(16, 8, X).astype(BF16)
     sent[:, 6:] = feature[...]
+
+
+def kernel_q(got, copies):
+    scale = 1.0 / math.sqrt(NZ * NY * X)
+    total = got[0, :6].astype(F32)
+    for j in range(1, 16):
+        total = total + got[j, :6].astype(F32)
+    total = (total[:3] + total[3:]) * scale
+    for j in range(16):
+        copies[j] = total
 
 
 VMEM, SMEM = pl.BlockSpec(memory_space=pltpu.VMEM), pl.BlockSpec(memory_space=pltpu.SMEM)
@@ -307,6 +311,7 @@
             ((Z, 384, 4 * X), BF16),
             ((Z + 2, MID, R * X), F32),
             ((Z, MID, R * X), BF16),
+            ((2, MID, R * X), BF16),
             ((3, 384, 384), F32),
             ((3, 384, 384), BF16),
             (((Z + 4) * CIN, 4 * X), BF16),
@@ -318,12 +323,12 @@
         6 * 10**9,
         1,
     )
-    feature, mine, theirs = call(
+    feature, slabs, theirs = call(
         kernel_c,
         (scal, halo_l, halo_r) + tuple(own),
         [
             ((16, 8, 8, X), BF16),
-            ((24, 128, 128), F32),
+            ((2, 24, 128, 128), F32),
             ((24, 128, 128), BF16),
         ],
         [
@@ -337,7 +342,7 @@
         1,
     )
 
-    mine = (mine + lax.ppermute(theirs, "core", swap).astype(F32)).astype(BF16)
+    mine = (slabs[0] + lax.ppermute(theirs, "core", swap).astype(F32)).astype(BF16)
     shares = lax.all_to_all(mine.reshape(8, 3, 128, 128), ("x", "zl"), 0, 0, tiled=True)
     (sent,) = call(kernel_p, (shares, feature), [((16, 14, 8, X), BF16)], [], 10**6, 0)
     got = lax.all_to_all(sent, CHAN, 0, 0, tiled=True)
@@ -348,10 +353,8 @@
     second = rows[:, :, 2] + jnp.concatenate([rows[1:, :, 0], none])
     feature = jnp.stack([first, second], axis=2).transpose(3, 1, 0, 2, 4).reshape(4, Z, NY, X)
 
-    scale = 1.0 / math.sqrt(NZ * NY * X)
-    part = got[:, :6].astype(F32).sum(axis=0)
-    part = (part[:3] + part[3:]) * scale
-    total = lax.all_to_all(jnp.broadcast_to(part[None], (16, 3, 8, 128)), SLAB, 0, 0, tiled=True)
+    (copies,) = call(kernel_q, (got,), [((16, 3, 8, 128), F32)], [], 10**6, 0)
+    total = lax.all_to_all(copies, SLAB, 0, 0, tiled=True)
     total = total.reshape(48, 8, 128)
     two, one = total[:27], total[27:41].reshape(14, 8, 2, CIN)
     one = jnp.concatenate([one[:9, :, 0], one[:9, :, 1], one[9:, :, 0], one[9:13, :, 1]])

time: 115 us -> 113 us (0.983)
    pallas_call x3 -> x4, Pallas kernels: 9.52 us -> 8.37 us  [call(): pl.pallas_call(body, out_shape=tuple((jax.ShapeDtypeStruct(shape, kind) f...]
where the time goes in v6:
time: 113 us
  blocking collectives  35.1 us (31%)
  waiting for transfers between devices  34.9 us (31%)
  starting transfers between devices  25.8 us (23%)
  Pallas kernels  10.7 us (9%)
  local copies, waits for them, and re-layouts  3.48 us (3%)
  between operations  2.11 us (2%)
    all_to_all x1, waiting for transfers between devices, shards(): got = lax.all_to_all(sent, CHAN, 0, 0, tiled=True)  24.6 us
    all_to_all x1, blocking collectives, shards(): got = lax.all_to_all(sent, CHAN, 0, 0, tiled=True)  19 us
    all_to_all x1, blocking collectives, shards(): lax.all_to_all(mine.reshape(8, 3, 128, 128), ('x', 'zl'), 0, 0, tiled=True)  16.1 us
    all_to_all x1, starting transfers between devices, shards(): got = lax.all_to_all(sent, CHAN, 0, 0, tiled=True)  11.9 us
    pallas_call x4, Pallas kernels, call(): pl.pallas_call(body, out_shape=tuple((jax.ShapeDtypeStruct(shape, kind) f...  8.37 us
    all_to_all x1, waiting for transfers between devices, shards(): total = lax.all_to_all(copies, SLAB, 0, 0, tiled=True)  5.53 us
    all_to_all x1, starting transfers between devices, shards(): total = lax.all_to_all(copies, SLAB, 0, 0, tiled=True)  5.37 us
    ppermute x1, starting transfers between devices, shards(): halo_r = lax.ppermute(got[:, :10], SLAB, down)  5.34 us
  transfers between devices with their start and end apart: 5, of which 5 were waited for; matrix products, arithmetic and copies ran while one was open for 1% of the time, Pallas kernels for 4%

profile of v6, /device:TPU:1, one launch (start us, length us, event | category | flops | bytes accessed | tf_op | source)
XLA Modules:
  0.0 112.5 jit_solution(5487166843205728966)
XLA Ops:
  0.6 2.3 %shard_map.94 = bf16[16,32,8,128]{3,2,1,0:T(8,128)(2,1)} custom-call(bf16[8,4,32,128]{3,2,1,0:T(8,128)(2,1)} %grad_in.1, bf16[8,4,32,128]{3,2,1,0:T(8,128)(2,1)} %pre_in.1, bf16[4,4,32,128]{3,2,1,0:T(8,128)(2,1)} %feat_in.1), custom_call_target="tpu_custom_call" | custom-call | tf_op jit(solution)/shard_map/pallas_call | solution.py:280
  2.9 0.0 copy-start
  3.0 0.0 copy-start.1
  3.0 11.9 %all-to-all-start = ((bf16[16,32,8,128]{3,2,1,0:T(8,128)(2,1)}), bf16[16,32,8,128]{3,2,1,0:T(8,128)(2,1)S(1)}, u32[]{:S(2)}, u32[]{:S(2)}) async-start(bf16[16,32,8,128]{3,2,1,0:T(8,128)(2,1)} %shard_map.94), calls=%async_computation | async-start | bytes 2097152 | tf_op jit(solution)/shard_map/all_to_all | solution.py:295
  16.2 0.1 stack.40.scal
  16.3 24.6 %all-to-all-done.got = bf16[16,32,8,128]{3,2,1,0:T(8,128)(2,1)S(1)} async-done(((bf16[16,32,8,128]{3,2,1,0:T(8,128)(2,1)}), bf16[16,32,8,128]{3,2,1,0:T(8,128)(2,1)S(1)}, u32[]{:S(2)}, u32[]{:S(2)}) %all-to-all-start) | async-done | bytes 1048608 | tf_op jit(solution)/shard_map/all_to_all | solution.py:295
  41.0 5.3 %collective-permute-start.1 = (bf16[16,10,8,128]{3,2,1,0:T(8,128)(2,1)S(1)}, bf16[16,10,8,128]{3,2,1,0:T(8,128)(2,1)S(1)}, u32[]{:S(2)}, u32[]{:S(2)}) collective-permute-start(bf16[16,10,8,128]{3,2,1,0:T(8,128)(2,1)S(1)} %get-tuple-element.29), channel_id=1, source_target_pairs={{16,0},{32,16},{48,32},{64,48},{80,64},{96,80},{112,96},{128,112},... | collective-permute-start | bytes 983048 | tf_op jit(solution)/shard_map/ppermute | solution.py:301
  46.3 0.0 collective-permute-start
  46.3 0.0 copy-done
  46.3 0.0 copy-done.1
  46.3 4.5 %shard_map.95 = (bf16[4,384,512]{2,1,0:T(8,128)(2,1)S(1)}, f32[6,128,256]{2,1,0:T(8,128)S(1)}, bf16[4,128,256]{2,1,0:T(8,128)(2,1)S(1)}, bf16[2,128,256]{2,1,0:T...) custom-call(s32[7]{0:T(128)S(1)} %stack.40.scal, ...), custom_call_target="tpu_custom_call" | custom-call | flops 6000000000 | bytes 4194304 | tf_op jit(solution)/shard_map/pallas_call | solution.py:265
  50.8 0.6 collective-permute-done.1.halo_r
  51.4 2.3 %collective-permute-done.halo_l = bf16[16,10,8,128]{3,2,1,0:T(8,128)(2,1)S(1)} collective-permute-done((bf16[16,10,8,128]{3,2,1,0:T(8,128)(2,1)S(1)}, bf16[16,10,8,128]{3,2,1,0:T(8,128)(2,1)S(1)}, u32[]{:S(2)}, u32[]{:S(2)}) %collective-permute-start) | collective-permute-done | bytes 327712 | tf_op jit(solution)/shard_map/ppermute | solution.py:300
  53.6 3.0 %shard_map.96 = (bf16[16,8,8,128]{3,2,1,0:T(8,128)(2,1)S(1)}, f32[2,24,128,128]{3,2,1,0:T(8,128)S(1)}, bf16[24,128,128]{2,1,0:T(8,128)(2,1)S(1)}) custom-call(s32[7]{0:T(128)S(1)} %stack.40.scal, bf16[16,10,8,128]{3,2,1,0:T(8,128)(2,1)S(1)} %collective-permute-done.halo_l, bf16[16,10,8,128]{3,2,1,0:T(8,128)(2,1)S(1)} %collective-permute-done.1.halo_r, ...), custom_call_target="tpu_custom_call" | custom-call | flops 3000000000 | bytes 4194304 | tf_op jit(solution)/shard_map/pallas_call | solution.py:265
  56.7 3.2 %collective-permute-start.2 = (bf16[24,128,128]{2,1,0:T(8,128)(2,1)S(1)}, bf16[24,128,128]{2,1,0:T(8,128)(2,1)S(1)}, u32[]{:S(2)}, u32[]{:S(2)}) collective-permute-start(bf16[24,128,128]{2,1,0:T(8,128)(2,1)S(1)} %get-tuple-element.27), channel_id=1, source_target_pairs={{0,16},{16,0},{1,17},{17,1},{2,18},{18,2},{3,19},{19,3},{4,20},{20... | collective-permute-start | bytes 2359304 | tf_op jit(solution)/shard_map/ppermute | solution.py:345
  59.9 1.9 %collective-permute-done.2 = bf16[24,128,128]{2,1,0:T(8,128)(2,1)S(1)} collective-permute-done((bf16[24,128,128]{2,1,0:T(8,128)(2,1)S(1)}, bf16[24,128,128]{2,1,0:T(8,128)(2,1)S(1)}, u32[]{:S(2)}, u32[]{:S(2)}) %collective-permute-start.2) | collective-permute-done | bytes 786464 | tf_op jit(solution)/shard_map/ppermute | solution.py:345
  61.8 0.2 fusion
  62.1 16.1 %all_to_all.20.shares = bf16[8,3,128,128]{3,2,1,0:T(8,128)(2,1)S(1)} all-to-all(bf16[8,3,128,128]{3,2,1,0:T(8,128)(2,1)S(1)} %bitcast.52), channel_id=1, replica_groups=mesh['x'=4,'zl'=2,'core'=2,'y'=4,'zh'=4] {'x','zl'}, dimensions={0} | all-to-all | bytes 1572864 | tf_op jit(solution)/shard_map/all_to_all | solution.py:346
  78.1 0.1 shard_map.97
  78.3 19.0 %all_to_all.21.got = bf16[16,14,8,128]{3,2,1,0:T(8,128)(2,1)S(1)} all-to-all(bf16[16,14,8,128]{3,2,1,0:T(8,128)(2,1)S(1)} %shard_map.97), channel_id=1, replica_groups=mesh['x'=4,'zl'=2,'core'=2,'y'=4,'zh'=4] {'y','zh'}, dimensions={0} | all-to-all | bytes 917504 | tf_op jit(solution)/shard_map/all_to_all | solution.py:348
  97.3 0.7 shard_map.98
  98.0 5.4 %all-to-all-start.3 = ((f32[16,3,8,128]{3,2,1,0:T(8,128)}), f32[16,3,8,128]{3,2,1,0:T(8,128)S(1)}, u32[]{:S(2)}, u32[]{:S(2)}) async-start(f32[16,3,8,128]{3,2,1,0:T(8,128)} %shard_map.98), calls=%async_computation.3 | async-start | bytes 393216 | tf_op jit(solution)/shard_map/all_to_all | solution.py:357
  103.5 0.1 fusion.4
  103.6 0.1 maximum_bitcast_fusion
  103.6 0.9 copy.27
  104.5 5.5 %all-to-all-done.3 = f32[16,3,8,128]{3,2,1,0:T(8,128)S(1)} async-done(((f32[16,3,8,128]{3,2,1,0:T(8,128)}), f32[16,3,8,128]{3,2,1,0:T(8,128)S(1)}, u32[]{:S(2)}, u32[]{:S(2)}) %all-to-all-start.3) | async-done | bytes 196640 | tf_op jit(solution)/shard_map/all_to_all | solution.py:357
  110.1 0.1 reshape.36
  110.2 0.1 fusion.6
  110.3 0.1 copy.29
  110.5 0.8 reshape.37
  111.3 0.2 copy.30
  111.6 0.9 reshape.38
  (9 shorter events, 0.2 us)
Async XLA Ops:
  2.9 43.4 %copy-start = (bf16[27,128,128]{2,1,0:T(8,128)(2,1)S(1)}, bf16[27,128,128]{2,1,0:T(8,128)(2,1)}, u32[]{:S(2)}) copy-start(bf16[27,128,128]{2,1,0:T(8,128)(2,1)} %w_two.1) | copy-start | bytes 2654212
  3.0 43.4 %copy-start.1 = (bf16[27,64,128]{2,1,0:T(8,128)(2,1)S(1)}, bf16[27,64,128]{2,1,0:T(8,128)(2,1)}, u32[]{:S(2)}) copy-start(bf16[27,64,128]{2,1,0:T(8,128)(2,1)} %w_one.1) | copy-start | bytes 1327108
  3.0 37.9 %all-to-all-start = ((bf16[16,32,8,128]{3,2,1,0:T(8,128)(2,1)}), bf16[16,32,8,128]{3,2,1,0:T(8,128)(2,1)S(1)}, u32[]{:S(2)}, u32[]{:S(2)}) async-start(bf16[16,32,8,128]{3,2,1,0:T(8,128)(2,1)} %shard_map.94), calls=%async_computation | async-start | bytes 2097152 | tf_op jit(solution)/shard_map/all_to_all | solution.py:295
  41.0 10.4 %collective-permute-start.1 = (bf16[16,10,8,128]{3,2,1,0:T(8,128)(2,1)S(1)}, bf16[16,10,8,128]{3,2,1,0:T(8,128)(2,1)S(1)}, u32[]{:S(2)}, u32[]{:S(2)}) collective-permute-start(bf16[16,10,8,128]{3,2,1,0:T(8,128)(2,1)S(1)} %get-tuple-element.29), channel_id=1, source_target_pairs={{16,0},{32,16},{48,32},{64,48},{80,64},{96,80},{112,96},{128,112},... | collective-permute-start | bytes 983048 | tf_op jit(solution)/shard_map/ppermute | solution.py:301
  46.3 7.3 %collective-permute-start = (bf16[16,10,8,128]{3,2,1,0:T(8,128)(2,1)S(1)}, bf16[16,10,8,128]{3,2,1,0:T(8,128)(2,1)S(1)}, u32[]{:S(2)}, u32[]{:S(2)}) collective-permute-start(bf16[16,10,8,128]{3,2,1,0:T(8,128)(2,1)S(1)} %get-tuple-element.30), channel_id=1, source_target_pairs={{0,16},{16,32},{32,48},{48,64},{64,80},{80,96},{96,112},{112,128},... | collective-permute-start | bytes 983048 | tf_op jit(solution)/shard_map/ppermute | solution.py:300
  56.7 5.1 %collective-permute-start.2 = (bf16[24,128,128]{2,1,0:T(8,128)(2,1)S(1)}, bf16[24,128,128]{2,1,0:T(8,128)(2,1)S(1)}, u32[]{:S(2)}, u32[]{:S(2)}) collective-permute-start(bf16[24,128,128]{2,1,0:T(8,128)(2,1)S(1)} %get-tuple-element.27), channel_id=1, source_target_pairs={{0,16},{16,0},{1,17},{17,1},{2,18},{18,2},{3,19},{19,3},{4,20},{20... | collective-permute-start | bytes 2359304 | tf_op jit(solution)/shard_map/ppermute | solution.py:345
  98.0 12.1 %all-to-all-start.3 = ((f32[16,3,8,128]{3,2,1,0:T(8,128)}), f32[16,3,8,128]{3,2,1,0:T(8,128)S(1)}, u32[]{:S(2)}, u32[]{:S(2)}) async-start(f32[16,3,8,128]{3,2,1,0:T(8,128)} %shard_map.98), calls=%async_computation.3 | async-start | bytes 393216 | tf_op jit(solution)/shard_map/all_to_all | solution.py:357

commit v7 on v6

--- a/solution.py
+++ b/solution.py
@@ -65,7 +65,7 @@
     return (jnp.maximum(pre, 0.0) * scale).astype(BF16), jnp.where(pre > 0, scale, 0.0)
 
 
-def kernel_s(grad_in, pre_in, feat_in, sent, grad, pre, feat, rows8, rows4, sems):
+def kernel_s(grad_in, pre_in, feat_in, out, sent, grad, pre, feat, rows8, rows4, sems):
     copies = [
         pltpu.make_async_copy(src, dst, sems.at[i])
         for i, (src, dst) in enumerate(((grad_in, grad), (pre_in, pre), (feat_in, feat)))
@@ -86,18 +86,25 @@
         sent[:, at + 2] = rows[:, 1]
         sent[:-1, at + 3] = rows[1:, 0]
     copies[1].wait()
-    copies[2].wait()
     for z in range(Z):
         for c in range(8):
             rows8[Z + z, pl.ds(c, NY, stride=8), :] = pre[c, z].astype(F32)
         rows = rows8[Z + z].reshape(16, 2, 8, X).astype(BF16)
         sent[:, PRE[z]] = rows[:, 0]
         sent[:, PRE[z] + 1] = rows[:, 1]
+    first = pltpu.make_async_copy(sent.at[:, :FEAT], out.at[:, :FEAT], sems.at[3])
+    first.start()
+    copies[2].wait()
+    for z in range(Z):
         for c in range(4):
             rows4[z, pl.ds(4 + c, NY, stride=4), :] = feat[c, z].astype(F32)
         rows = rows4[z].reshape(17, 8, X).astype(BF16)
         sent[:, FEAT + 2 * z] = rows[:-1]
         sent[:, FEAT + 2 * z + 1] = rows[1:]
+    last = pltpu.make_async_copy(sent.at[:, FEAT:], out.at[:, FEAT:], sems.at[4])
+    last.start()
+    first.wait()
+    last.wait()
 
 
 def add_feature_terms(fin, wf, rows, plane):
@@ -281,14 +288,15 @@
         kernel_s,
         out_shape=jax.ShapeDtypeStruct((16, 32, 8, X), BF16),
         in_specs=[anywhere] * 3,
-        out_specs=VMEM,
+        out_specs=anywhere,
         scratch_shapes=[
+            pltpu.VMEM((16, 32, 8, X), BF16),
             pltpu.VMEM(out_grad.shape, BF16),
             pltpu.VMEM(pre_act.shape, BF16),
             pltpu.VMEM(features.shape, BF16),
             pltpu.VMEM((2 * Z, NY * 8, X), F32),
             pltpu.VMEM((Z, (NY + 2) * 4, X), F32),
-            pltpu.SemaphoreType.DMA((3,)),
+            pltpu.SemaphoreType.DMA((5,)),
         ],
         compiler_params=pltpu.CompilerParams(vmem_limit_bytes=56 * 1024 * 1024),
     )(out_grad, pre_act, features)

time: 113 us -> 113 us (level)
  no operation moved by 1% of the time
where the time goes in v7:
time: 113 us; the launch traced here: 112 us
  blocking collectives  35.1 us (31%)
  waiting for transfers between devices  34.9 us (31%)
  starting transfers between devices  25.8 us (23%)
  Pallas kernels  10.6 us (9%)
  local copies, waits for them, and re-layouts  3.48 us (3%)
  between operations  2.11 us (2%)
    all_to_all x1, waiting for transfers between devices, shards(): got = lax.all_to_all(sent, CHAN, 0, 0, tiled=True)  24.6 us
    all_to_all x1, blocking collectives, shards(): got = lax.all_to_all(sent, CHAN, 0, 0, tiled=True)  19 us
    all_to_all x1, blocking collectives, shards(): lax.all_to_all(mine.reshape(8, 3, 128, 128), ('x', 'zl'), 0, 0, tiled=True)  16.1 us
    all_to_all x1, starting transfers between devices, shards(): got = lax.all_to_all(sent, CHAN, 0, 0, tiled=True)  11.9 us
    pallas_call x4, Pallas kernels, call(): pl.pallas_call(body, out_shape=tuple((jax.ShapeDtypeStruct(shape, kind) f...  8.36 us
    all_to_all x1, waiting for transfers between devices, shards(): total = lax.all_to_all(copies, SLAB, 0, 0, tiled=True)  5.53 us
    all_to_all x1, starting transfers between devices, shards(): total = lax.all_to_all(copies, SLAB, 0, 0, tiled=True)  5.37 us
    ppermute x1, starting transfers between devices, shards(): halo_r = lax.ppermute(got[:, :10], SLAB, down)  5.34 us
  transfers between devices with their start and end apart: 5, of which 5 were waited for; matrix products, arithmetic and copies ran while one was open for 1% of the time, Pallas kernels for 4%

profile of v7, /device:TPU:1, one launch (start us, length us, event | category | flops | bytes accessed | tf_op | source)
XLA Modules:
  0.0 112.5 jit_solution(6386338113615750941)
XLA Ops:
  0.6 2.3 %shard_map.94 = bf16[16,32,8,128]{3,2,1,0:T(8,128)(2,1)} custom-call(bf16[8,4,32,128]{3,2,1,0:T(8,128)(2,1)} %grad_in.1, bf16[8,4,32,128]{3,2,1,0:T(8,128)(2,1)} %pre_in.1, bf16[4,4,32,128]{3,2,1,0:T(8,128)(2,1)} %feat_in.1), custom_call_target="tpu_custom_call" | custom-call | tf_op jit(solution)/shard_map/pallas_call | solution.py:287
  2.9 0.0 copy-start
  2.9 0.0 copy-start.1
  2.9 11.9 %all-to-all-start = ((bf16[16,32,8,128]{3,2,1,0:T(8,128)(2,1)}), bf16[16,32,8,128]{3,2,1,0:T(8,128)(2,1)S(1)}, u32[]{:S(2)}, u32[]{:S(2)}) async-start(bf16[16,32,8,128]{3,2,1,0:T(8,128)(2,1)} %shard_map.94), calls=%async_computation | async-start | bytes 2097152 | tf_op jit(solution)/shard_map/all_to_all | solution.py:303
  16.1 0.1 stack.40.scal
  16.2 24.6 %all-to-all-done.got = bf16[16,32,8,128]{3,2,1,0:T(8,128)(2,1)S(1)} async-done(((bf16[16,32,8,128]{3,2,1,0:T(8,128)(2,1)}), bf16[16,32,8,128]{3,2,1,0:T(8,128)(2,1)S(1)}, u32[]{:S(2)}, u32[]{:S(2)}) %all-to-all-start) | async-done | bytes 1048608 | tf_op jit(solution)/shard_map/all_to_all | solution.py:303
  40.9 5.3 %collective-permute-start.1 = (bf16[16,10,8,128]{3,2,1,0:T(8,128)(2,1)S(1)}, bf16[16,10,8,128]{3,2,1,0:T(8,128)(2,1)S(1)}, u32[]{:S(2)}, u32[]{:S(2)}) collective-permute-start(bf16[16,10,8,128]{3,2,1,0:T(8,128)(2,1)S(1)} %get-tuple-element.29), channel_id=1, source_target_pairs={{16,0},{32,16},{48,32},{64,48},{80,64},{96,80},{112,96},{128,112},... | collective-permute-start | bytes 983048 | tf_op jit(solution)/shard_map/ppermute | solution.py:309
  46.2 0.0 collective-permute-start
  46.3 0.0 copy-done
  46.3 0.0 copy-done.1
  46.3 4.5 %shard_map.95 = (bf16[4,384,512]{2,1,0:T(8,128)(2,1)S(1)}, f32[6,128,256]{2,1,0:T(8,128)S(1)}, bf16[4,128,256]{2,1,0:T(8,128)(2,1)S(1)}, bf16[2,128,256]{2,1,0:T...) custom-call(s32[7]{0:T(128)S(1)} %stack.40.scal, ...), custom_call_target="tpu_custom_call" | custom-call | flops 6000000000 | bytes 4194304 | tf_op jit(solution)/shard_map/pallas_call | solution.py:272
  50.7 0.6 collective-permute-done.1.halo_r
  51.3 2.3 %collective-permute-done.halo_l = bf16[16,10,8,128]{3,2,1,0:T(8,128)(2,1)S(1)} collective-permute-done((bf16[16,10,8,128]{3,2,1,0:T(8,128)(2,1)S(1)}, bf16[16,10,8,128]{3,2,1,0:T(8,128)(2,1)S(1)}, u32[]{:S(2)}, u32[]{:S(2)}) %collective-permute-start) | collective-permute-done | bytes 327712 | tf_op jit(solution)/shard_map/ppermute | solution.py:308
  53.6 3.0 %shard_map.96 = (bf16[16,8,8,128]{3,2,1,0:T(8,128)(2,1)S(1)}, f32[2,24,128,128]{3,2,1,0:T(8,128)S(1)}, bf16[24,128,128]{2,1,0:T(8,128)(2,1)S(1)}) custom-call(s32[7]{0:T(128)S(1)} %stack.40.scal, bf16[16,10,8,128]{3,2,1,0:T(8,128)(2,1)S(1)} %collective-permute-done.halo_l, bf16[16,10,8,128]{3,2,1,0:T(8,128)(2,1)S(1)} %collective-permute-done.1.halo_r, ...), custom_call_target="tpu_custom_call" | custom-call | flops 3000000000 | bytes 4194304 | tf_op jit(solution)/shard_map/pallas_call | solution.py:272
  56.6 3.2 %collective-permute-start.2 = (bf16[24,128,128]{2,1,0:T(8,128)(2,1)S(1)}, bf16[24,128,128]{2,1,0:T(8,128)(2,1)S(1)}, u32[]{:S(2)}, u32[]{:S(2)}) collective-permute-start(bf16[24,128,128]{2,1,0:T(8,128)(2,1)S(1)} %get-tuple-element.27), channel_id=1, source_target_pairs={{0,16},{16,0},{1,17},{17,1},{2,18},{18,2},{3,19},{19,3},{4,20},{20... | collective-permute-start | bytes 2359304 | tf_op jit(solution)/shard_map/ppermute | solution.py:353
  59.8 1.9 %collective-permute-done.2 = bf16[24,128,128]{2,1,0:T(8,128)(2,1)S(1)} collective-permute-done((bf16[24,128,128]{2,1,0:T(8,128)(2,1)S(1)}, bf16[24,128,128]{2,1,0:T(8,128)(2,1)S(1)}, u32[]{:S(2)}, u32[]{:S(2)}) %collective-permute-start.2) | collective-permute-done | bytes 786464 | tf_op jit(solution)/shard_map/ppermute | solution.py:353
  61.8 0.2 fusion
  62.0 16.1 %all_to_all.20.shares = bf16[8,3,128,128]{3,2,1,0:T(8,128)(2,1)S(1)} all-to-all(bf16[8,3,128,128]{3,2,1,0:T(8,128)(2,1)S(1)} %bitcast.52), channel_id=1, replica_groups=mesh['x'=4,'zl'=2,'core'=2,'y'=4,'zh'=4] {'x','zl'}, dimensions={0} | all-to-all | bytes 1572864 | tf_op jit(solution)/shard_map/all_to_all | solution.py:354
  78.1 0.1 shard_map.97
  78.2 19.0 %all_to_all.21.got = bf16[16,14,8,128]{3,2,1,0:T(8,128)(2,1)S(1)} all-to-all(bf16[16,14,8,128]{3,2,1,0:T(8,128)(2,1)S(1)} %shard_map.97), channel_id=1, replica_groups=mesh['x'=4,'zl'=2,'core'=2,'y'=4,'zh'=4] {'y','zh'}, dimensions={0} | all-to-all | bytes 917504 | tf_op jit(solution)/shard_map/all_to_all | solution.py:356
  97.2 0.7 shard_map.98
  97.9 5.4 %all-to-all-start.3 = ((f32[16,3,8,128]{3,2,1,0:T(8,128)}), f32[16,3,8,128]{3,2,1,0:T(8,128)S(1)}, u32[]{:S(2)}, u32[]{:S(2)}) async-start(f32[16,3,8,128]{3,2,1,0:T(8,128)} %shard_map.98), calls=%async_computation.3 | async-start | bytes 393216 | tf_op jit(solution)/shard_map/all_to_all | solution.py:365
  103.4 0.1 fusion.4
  103.5 0.1 maximum_bitcast_fusion
  103.6 0.9 copy.27
  104.5 5.5 %all-to-all-done.3 = f32[16,3,8,128]{3,2,1,0:T(8,128)S(1)} async-done(((f32[16,3,8,128]{3,2,1,0:T(8,128)}), f32[16,3,8,128]{3,2,1,0:T(8,128)S(1)}, u32[]{:S(2)}, u32[]{:S(2)}) %all-to-all-start.3) | async-done | bytes 196640 | tf_op jit(solution)/shard_map/all_to_all | solution.py:365
  110.0 0.1 reshape.36
  110.2 0.1 fusion.6
  110.3 0.1 copy.29
  110.4 0.8 reshape.37
  111.3 0.2 copy.30
  111.5 0.9 reshape.38
  (9 shorter events, 0.2 us)
Async XLA Ops:
  2.9 43.4 %copy-start = (bf16[27,128,128]{2,1,0:T(8,128)(2,1)S(1)}, bf16[27,128,128]{2,1,0:T(8,128)(2,1)}, u32[]{:S(2)}) copy-start(bf16[27,128,128]{2,1,0:T(8,128)(2,1)} %w_two.1) | copy-start | bytes 2654212
  2.9 43.4 %copy-start.1 = (bf16[27,64,128]{2,1,0:T(8,128)(2,1)S(1)}, bf16[27,64,128]{2,1,0:T(8,128)(2,1)}, u32[]{:S(2)}) copy-start(bf16[27,64,128]{2,1,0:T(8,128)(2,1)} %w_one.1) | copy-start | bytes 1327108
  2.9 37.9 %all-to-all-start = ((bf16[16,32,8,128]{3,2,1,0:T(8,128)(2,1)}), bf16[16,32,8,128]{3,2,1,0:T(8,128)(2,1)S(1)}, u32[]{:S(2)}, u32[]{:S(2)}) async-start(bf16[16,32,8,128]{3,2,1,0:T(8,128)(2,1)} %shard_map.94), calls=%async_computation | async-start | bytes 2097152 | tf_op jit(solution)/shard_map/all_to_all | solution.py:303
  40.9 10.4 %collective-permute-start.1 = (bf16[16,10,8,128]{3,2,1,0:T(8,128)(2,1)S(1)}, bf16[16,10,8,128]{3,2,1,0:T(8,128)(2,1)S(1)}, u32[]{:S(2)}, u32[]{:S(2)}) collective-permute-start(bf16[16,10,8,128]{3,2,1,0:T(8,128)(2,1)S(1)} %get-tuple-element.29), channel_id=1, source_target_pairs={{16,0},{32,16},{48,32},{64,48},{80,64},{96,80},{112,96},{128,112},... | collective-permute-start | bytes 983048 | tf_op jit(solution)/shard_map/ppermute | solution.py:309
  46.2 7.3 %collective-permute-start = (bf16[16,10,8,128]{3,2,1,0:T(8,128)(2,1)S(1)}, bf16[16,10,8,128]{3,2,1,0:T(8,128)(2,1)S(1)}, u32[]{:S(2)}, u32[]{:S(2)}) collective-permute-start(bf16[16,10,8,128]{3,2,1,0:T(8,128)(2,1)S(1)} %get-tuple-element.30), channel_id=1, source_target_pairs={{0,16},{16,32},{32,48},{48,64},{64,80},{80,96},{96,112},{112,128},... | collective-permute-start | bytes 983048 | tf_op jit(solution)/shard_map/ppermute | solution.py:308
  56.6 5.1 %collective-permute-start.2 = (bf16[24,128,128]{2,1,0:T(8,128)(2,1)S(1)}, bf16[24,128,128]{2,1,0:T(8,128)(2,1)S(1)}, u32[]{:S(2)}, u32[]{:S(2)}) collective-permute-start(bf16[24,128,128]{2,1,0:T(8,128)(2,1)S(1)} %get-tuple-element.27), channel_id=1, source_target_pairs={{0,16},{16,0},{1,17},{17,1},{2,18},{18,2},{3,19},{19,3},{4,20},{20... | collective-permute-start | bytes 2359304 | tf_op jit(solution)/shard_map/ppermute | solution.py:353
  97.9 12.1 %all-to-all-start.3 = ((f32[16,3,8,128]{3,2,1,0:T(8,128)}), f32[16,3,8,128]{3,2,1,0:T(8,128)S(1)}, u32[]{:S(2)}, u32[]{:S(2)}) async-start(f32[16,3,8,128]{3,2,1,0:T(8,128)} %shard_map.98), calls=%async_computation.3 | async-start | bytes 393216 | tf_op jit(solution)/shard_map/all_to_all | solution.py:365

commit v8 on v6

--- a/solution.py
+++ b/solution.py
@@ -178,14 +178,15 @@
     fout, slabs, theirs, g, hid, act, p3, fin,
 ):
     core, has_l, has_r = scal[4], scal[5] > 0, scal[6] > 0
-    slabs[:, 20:] = jnp.zeros((2, 4, 128, 128), F32)
+    slabs[:, 20:] = jnp.zeros((2, 1, 128, 128), F32)
     for at in range(4):
         for r in range(4):
             if at < 2:
                 store_shifts(g, at, r, jnp.where(has_l, tile(halo_l, 4 * at + r), 0.0))
             else:
                 store_shifts(g, at, r, jnp.where(has_r, tile(halo_r, 4 * at - 6 + r), 0.0))
-    hid[...] = part_hid[...]
+    hid[0:2] = part_hid[0:2]
+    hid[Z:] = part_hid[Z:]
     for at, plane, first, end in ((0, -2, 2, 3), (1, -1, 1, 3), (2, 4, 0, 2), (3, 5, 0, 1)):
         total = None
         for kh in range(3):
@@ -328,8 +329,8 @@
         (scal, halo_l, halo_r) + tuple(own),
         [
             ((16, 8, 8, X), BF16),
-            ((2, 24, 128, 128), F32),
-            ((24, 128, 128), BF16),
+            ((2, 21, 128, 128), F32),
+            ((21, 128, 128), BF16),
         ],
         [
             ((4, 384, 4 * X), BF16),
@@ -343,6 +344,7 @@
     )
 
     mine = (slabs[0] + lax.ppermute(theirs, "core", swap).astype(F32)).astype(BF16)
+    mine = jnp.concatenate([mine, jnp.zeros((3, 128, 128), BF16)])
     shares = lax.all_to_all(mine.reshape(8, 3, 128, 128), ("x", "zl"), 0, 0, tiled=True)
     (sent,) = call(kernel_p, (shares, feature), [((16, 14, 8, X), BF16)], [], 10**6, 0)
     got = lax.all_to_all(sent, CHAN, 0, 0, tiled=True)

time: 113 us -> 113 us (level)
  no operation moved by 1% of the time
where the time goes in v8:
time: 113 us; the launch traced here: 112 us
  blocking collectives  35.1 us (31%)
  waiting for transfers between devices  34.8 us (31%)
  starting transfers between devices  25.8 us (23%)
  Pallas kernels  10.6 us (9%)
  local copies, waits for them, and re-layouts  3.56 us (3%)
  between operations  2.12 us (2%)
    all_to_all x1, waiting for transfers between devices, shards(): got = lax.all_to_all(sent, CHAN, 0, 0, tiled=True)  24.6 us
    all_to_all x1, blocking collectives, shards(): got = lax.all_to_all(sent, CHAN, 0, 0, tiled=True)  19 us
    all_to_all x1, blocking collectives, shards(): lax.all_to_all(mine.reshape(8, 3, 128, 128), ('x', 'zl'), 0, 0, tiled=True)  16.1 us
    all_to_all x1, starting transfers between devices, shards(): got = lax.all_to_all(sent, CHAN, 0, 0, tiled=True)  11.9 us
    pallas_call x4, Pallas kernels, call(): pl.pallas_call(body, out_shape=tuple((jax.ShapeDtypeStruct(shape, kind) f...  8.32 us
    all_to_all x1, waiting for transfers between devices, shards(): total = lax.all_to_all(copies, SLAB, 0, 0, tiled=True)  5.53 us
    all_to_all x1, starting transfers between devices, shards(): total = lax.all_to_all(copies, SLAB, 0, 0, tiled=True)  5.37 us
    ppermute x1, starting transfers between devices, shards(): halo_r = lax.ppermute(got[:, :10], SLAB, down)  5.34 us
  transfers between devices with their start and end apart: 5, of which 5 were waited for; matrix products, arithmetic and copies ran while one was open for 1% of the time, Pallas kernels for 4%

profile of v8, /device:TPU:1, one launch (start us, length us, event | category | flops | bytes accessed | tf_op | source)
XLA Modules:
  0.0 112.4 jit_solution(2829441034175459909)
XLA Ops:
  0.6 2.3 %shard_map.94 = bf16[16,32,8,128]{3,2,1,0:T(8,128)(2,1)} custom-call(bf16[8,4,32,128]{3,2,1,0:T(8,128)(2,1)} %grad_in.1, bf16[8,4,32,128]{3,2,1,0:T(8,128)(2,1)} %pre_in.1, bf16[4,4,32,128]{3,2,1,0:T(8,128)(2,1)} %feat_in.1), custom_call_target="tpu_custom_call" | custom-call | tf_op jit(solution)/shard_map/pallas_call | solution.py:281
  2.9 0.0 copy-start
  3.0 0.0 copy-start.1
  3.0 11.9 %all-to-all-start = ((bf16[16,32,8,128]{3,2,1,0:T(8,128)(2,1)}), bf16[16,32,8,128]{3,2,1,0:T(8,128)(2,1)S(1)}, u32[]{:S(2)}, u32[]{:S(2)}) async-start(bf16[16,32,8,128]{3,2,1,0:T(8,128)(2,1)} %shard_map.94), calls=%async_computation | async-start | bytes 2097152 | tf_op jit(solution)/shard_map/all_to_all | solution.py:296
  16.2 0.1 stack.40.scal
  16.3 24.6 %all-to-all-done.got = bf16[16,32,8,128]{3,2,1,0:T(8,128)(2,1)S(1)} async-done(((bf16[16,32,8,128]{3,2,1,0:T(8,128)(2,1)}), bf16[16,32,8,128]{3,2,1,0:T(8,128)(2,1)S(1)}, u32[]{:S(2)}, u32[]{:S(2)}) %all-to-all-start) | async-done | bytes 1048608 | tf_op jit(solution)/shard_map/all_to_all | solution.py:296
  41.0 5.3 %collective-permute-start.1 = (bf16[16,10,8,128]{3,2,1,0:T(8,128)(2,1)S(1)}, bf16[16,10,8,128]{3,2,1,0:T(8,128)(2,1)S(1)}, u32[]{:S(2)}, u32[]{:S(2)}) collective-permute-start(bf16[16,10,8,128]{3,2,1,0:T(8,128)(2,1)S(1)} %get-tuple-element.29), channel_id=1, source_target_pairs={{16,0},{32,16},{48,32},{64,48},{80,64},{96,80},{112,96},{128,112},... | collective-permute-start | bytes 983048 | tf_op jit(solution)/shard_map/ppermute | solution.py:302
  46.3 0.0 collective-permute-start
  46.3 0.0 copy-done
  46.3 0.0 copy-done.1
  46.3 4.5 %shard_map.95 = (bf16[4,384,512]{2,1,0:T(8,128)(2,1)S(1)}, f32[6,128,256]{2,1,0:T(8,128)S(1)}, bf16[4,128,256]{2,1,0:T(8,128)(2,1)S(1)}, bf16[2,128,256]{2,1,0:T...) custom-call(s32[7]{0:T(128)S(1)} %stack.40.scal, ...), custom_call_target="tpu_custom_call" | custom-call | flops 6000000000 | bytes 4194304 | tf_op jit(solution)/shard_map/pallas_call | solution.py:266
  50.8 0.6 collective-permute-done.1.halo_r
  51.4 2.3 %collective-permute-done.halo_l = bf16[16,10,8,128]{3,2,1,0:T(8,128)(2,1)S(1)} collective-permute-done((bf16[16,10,8,128]{3,2,1,0:T(8,128)(2,1)S(1)}, bf16[16,10,8,128]{3,2,1,0:T(8,128)(2,1)S(1)}, u32[]{:S(2)}, u32[]{:S(2)}) %collective-permute-start) | collective-permute-done | bytes 327712 | tf_op jit(solution)/shard_map/ppermute | solution.py:301
  53.6 3.0 %shard_map.96 = (bf16[16,8,8,128]{3,2,1,0:T(8,128)(2,1)S(1)}, f32[2,21,128,128]{3,2,1,0:T(8,128)S(1)}, bf16[21,128,128]{2,1,0:T(8,128)(2,1)S(1)}) custom-call(s32[7]{0:T(128)S(1)} %stack.40.scal, bf16[16,10,8,128]{3,2,1,0:T(8,128)(2,1)S(1)} %collective-permute-done.halo_l, bf16[16,10,8,128]{3,2,1,0:T(8,128)(2,1)S(1)} %collective-permute-done.1.halo_r, ...), custom_call_target="tpu_custom_call" | custom-call | flops 3000000000 | bytes 4194304 | tf_op jit(solution)/shard_map/pallas_call | solution.py:266
  56.6 3.2 %collective-permute-start.2 = (bf16[21,128,128]{2,1,0:T(8,128)(2,1)S(1)}, bf16[21,128,128]{2,1,0:T(8,128)(2,1)S(1)}, u32[]{:S(2)}, u32[]{:S(2)}) collective-permute-start(bf16[21,128,128]{2,1,0:T(8,128)(2,1)S(1)} %get-tuple-element.27), channel_id=1, source_target_pairs={{0,16},{16,0},{1,17},{17,1},{2,18},{18,2},{3,19},{19,3},{4,20},{20... | collective-permute-start | bytes 2064392 | tf_op jit(solution)/shard_map/ppermute | solution.py:346
  59.8 1.8 %collective-permute-done.2 = bf16[21,128,128]{2,1,0:T(8,128)(2,1)S(1)} collective-permute-done((bf16[21,128,128]{2,1,0:T(8,128)(2,1)S(1)}, bf16[21,128,128]{2,1,0:T(8,128)(2,1)S(1)}, u32[]{:S(2)}, u32[]{:S(2)}) %collective-permute-start.2) | collective-permute-done | bytes 688160 | tf_op jit(solution)/shard_map/ppermute | solution.py:346
  61.6 0.2 fusion
  61.8 0.1 concatenate.12
  61.9 16.1 %all_to_all.20.shares = bf16[8,3,128,128]{3,2,1,0:T(8,128)(2,1)S(1)} all-to-all(bf16[8,3,128,128]{3,2,1,0:T(8,128)(2,1)S(1)} %bitcast.52), channel_id=1, replica_groups=mesh['x'=4,'zl'=2,'core'=2,'y'=4,'zh'=4] {'x','zl'}, dimensions={0} | all-to-all | bytes 1572864 | tf_op jit(solution)/shard_map/all_to_all | solution.py:348
  78.0 0.1 shard_map.97
  78.1 19.0 %all_to_all.21.got = bf16[16,14,8,128]{3,2,1,0:T(8,128)(2,1)S(1)} all-to-all(bf16[16,14,8,128]{3,2,1,0:T(8,128)(2,1)S(1)} %shard_map.97), channel_id=1, replica_groups=mesh['x'=4,'zl'=2,'core'=2,'y'=4,'zh'=4] {'y','zh'}, dimensions={0} | all-to-all | bytes 917504 | tf_op jit(solution)/shard_map/all_to_all | solution.py:350
  97.1 0.7 shard_map.98
  97.8 5.4 %all-to-all-start.3 = ((f32[16,3,8,128]{3,2,1,0:T(8,128)}), f32[16,3,8,128]{3,2,1,0:T(8,128)S(1)}, u32[]{:S(2)}, u32[]{:S(2)}) async-start(f32[16,3,8,128]{3,2,1,0:T(8,128)} %shard_map.98), calls=%async_computation.3 | async-start | bytes 393216 | tf_op jit(solution)/shard_map/all_to_all | solution.py:359
  103.3 0.1 fusion.4
  103.4 0.1 maximum_bitcast_fusion
  103.5 0.9 copy.27
  104.4 5.5 %all-to-all-done.3 = f32[16,3,8,128]{3,2,1,0:T(8,128)S(1)} async-done(((f32[16,3,8,128]{3,2,1,0:T(8,128)}), f32[16,3,8,128]{3,2,1,0:T(8,128)S(1)}, u32[]{:S(2)}, u32[]{:S(2)}) %all-to-all-start.3) | async-done | bytes 196640 | tf_op jit(solution)/shard_map/all_to_all | solution.py:359
  109.9 0.1 reshape.36
  110.1 0.1 fusion.6
  110.2 0.1 copy.29
  110.4 0.8 reshape.37
  111.2 0.2 copy.30
  111.4 0.9 reshape.38
  (9 shorter events, 0.2 us)
Async XLA Ops:
  2.9 43.4 %copy-start = (bf16[27,128,128]{2,1,0:T(8,128)(2,1)S(1)}, bf16[27,128,128]{2,1,0:T(8,128)(2,1)}, u32[]{:S(2)}) copy-start(bf16[27,128,128]{2,1,0:T(8,128)(2,1)} %w_two.1) | copy-start | bytes 2654212
  3.0 43.4 %copy-start.1 = (bf16[27,64,128]{2,1,0:T(8,128)(2,1)S(1)}, bf16[27,64,128]{2,1,0:T(8,128)(2,1)}, u32[]{:S(2)}) copy-start(bf16[27,64,128]{2,1,0:T(8,128)(2,1)} %w_one.1) | copy-start | bytes 1327108
  3.0 37.9 %all-to-all-start = ((bf16[16,32,8,128]{3,2,1,0:T(8,128)(2,1)}), bf16[16,32,8,128]{3,2,1,0:T(8,128)(2,1)S(1)}, u32[]{:S(2)}, u32[]{:S(2)}) async-start(bf16[16,32,8,128]{3,2,1,0:T(8,128)(2,1)} %shard_map.94), calls=%async_computation | async-start | bytes 2097152 | tf_op jit(solution)/shard_map/all_to_all | solution.py:296
  41.0 10.4 %collective-permute-start.1 = (bf16[16,10,8,128]{3,2,1,0:T(8,128)(2,1)S(1)}, bf16[16,10,8,128]{3,2,1,0:T(8,128)(2,1)S(1)}, u32[]{:S(2)}, u32[]{:S(2)}) collective-permute-start(bf16[16,10,8,128]{3,2,1,0:T(8,128)(2,1)S(1)} %get-tuple-element.29), channel_id=1, source_target_pairs={{16,0},{32,16},{48,32},{64,48},{80,64},{96,80},{112,96},{128,112},... | collective-permute-start | bytes 983048 | tf_op jit(solution)/shard_map/ppermute | solution.py:302
  46.3 7.3 %collective-permute-start = (bf16[16,10,8,128]{3,2,1,0:T(8,128)(2,1)S(1)}, bf16[16,10,8,128]{3,2,1,0:T(8,128)(2,1)S(1)}, u32[]{:S(2)}, u32[]{:S(2)}) collective-permute-start(bf16[16,10,8,128]{3,2,1,0:T(8,128)(2,1)S(1)} %get-tuple-element.30), channel_id=1, source_target_pairs={{0,16},{16,32},{32,48},{48,64},{64,80},{80,96},{96,112},{112,128},... | collective-permute-start | bytes 983048 | tf_op jit(solution)/shard_map/ppermute | solution.py:301
  56.6 5.0 %collective-permute-start.2 = (bf16[21,128,128]{2,1,0:T(8,128)(2,1)S(1)}, bf16[21,128,128]{2,1,0:T(8,128)(2,1)S(1)}, u32[]{:S(2)}, u32[]{:S(2)}) collective-permute-start(bf16[21,128,128]{2,1,0:T(8,128)(2,1)S(1)} %get-tuple-element.27), channel_id=1, source_target_pairs={{0,16},{16,0},{1,17},{17,1},{2,18},{18,2},{3,19},{19,3},{4,20},{20... | collective-permute-start | bytes 2064392 | tf_op jit(solution)/shard_map/ppermute | solution.py:346
  97.8 12.1 %all-to-all-start.3 = ((f32[16,3,8,128]{3,2,1,0:T(8,128)}), f32[16,3,8,128]{3,2,1,0:T(8,128)S(1)}, u32[]{:S(2)}, u32[]{:S(2)}) async-start(f32[16,3,8,128]{3,2,1,0:T(8,128)} %shard_map.98), calls=%async_computation.3 | async-start | bytes 393216 | tf_op jit(solution)/shard_map/all_to_all | solution.py:359
